TPU v7x, 32 devices: a whole 2x2x4 slice. The times are simulated.
32 devices in a mesh: groups: 2 (over y), feat: 4 (over z), layer: 2 (over x), row: 2 (over core).
Axes of the slice: x: 2, y: 2, z: 4, core: 2. Of those that a mesh axis runs over, the one named last changes fastest.
Arguments:
- resid_buf: bfloat16 [512, 2, 4608], P(('groups', 'feat', 'row')), parts along dimension 0, may hold values from -6 to 6
- shuffle: int32 [512], P('groups'), parts along dimension 0, may hold values from 0 to 255, each once
- mlp_out: bfloat16 [512, 2, 4608], P(('groups', 'feat', 'row')), parts along dimension 0, may hold values from -5 to 5
- enc_weight: bfloat16 [2, 8192, 4608], P('layer', 'feat', 'row'), may hold values from -0.09375 to 0.09375
- dec_weight: bfloat16 [2, 8192, 2, 4608], P('layer', 'feat', None, 'row'), may hold values from -0.0625 to 0.0625
- enc_bias: float32 [2, 8192], P('layer', 'feat'), may hold values from -0.5 to 0.5
- dec_bias: float32 [2, 4608], replicated, may hold values from -3 to 3
Outputs:
- rebuilt: bfloat16 [512, 2, 4608], P(('groups', 'feat', 'row')), parts along dimension 0
- enc_grad: bfloat16 [4, 8192, 4608], P(('groups', 'layer'), 'feat', 'row'), parts along dimension 0
- dec_grad: bfloat16 [4, 8192, 2, 4608], P(('groups', 'layer'), 'feat', None, 'row'), parts along dimension 0
- bias_grad: float32 [4, 8192], P(('groups', 'layer'), 'feat'), parts along dimension 0
There are 2 independent parts, one for each index of `groups`. A program takes and returns all parts, laid end to end along the dimension named above; an argument that names none is the same for every part. Nothing has to cross between parts.
Inputs may be any that keep to these rules, and one draw needn't show every extreme that they name: `shuffle`: a permutation of the 256 buffer rows.
All inputs are finite; a program needn't handle non-finite values.
Results may differ from a plain program's by a relative error of at most 0.04.
Values may be sent and summed in bfloat16 or wider, within the bound.
No kernel may reach another device: no remote copies, remote signals or barrier semaphores. Data moves between devices by JAX's collectives and lax.ppermute only.
A program may use at most 128 MiB of HBM per device.

v0:
```python
import jax
import jax.numpy as jnp
from jax import lax
from jax.sharding import PartitionSpec as P

LAYERS = 2


def from_behind(block, axis, distance):
    devices = range(lax.axis_size(axis))
    route = [(i - distance, i) for i in devices if i - distance in devices]
    return lax.ppermute(block, axis, route)


def dot_last(left, right):
    return lax.dot_general(
        left, right, (((1,), (1,)), ((), ())), preferred_element_type=jnp.float32
    )


def dot_first(left, right):
    return lax.dot_general(
        left, right, (((0,), (0,)), ((), ())), preferred_element_type=jnp.float32
    )


def on_device(resid_buf, shuffle, mlp_out, enc_weight, dec_weight, enc_bias, dec_bias):
    feat_count = lax.axis_size("feat")
    row_count = lax.axis_size("row")
    sub_blocks = lax.axis_size("layer") // LAYERS
    layer_pos = lax.axis_index("layer")
    row_pos = lax.axis_index("row")
    source = layer_pos // sub_blocks
    rows_each = resid_buf.shape[0]
    width = dec_bias.shape[1]
    half_width = enc_weight.shape[2]
    local_rows = rows_each * feat_count
    total_rows = local_rows * row_count
    loss_scale = float(total_rows) ** (-0.5)
    own_layer = lax.dynamic_index_in_dim(resid_buf, source, axis=1, keepdims=False)
    buffer_all = lax.all_gather(own_layer, ("feat", "row"), axis=0, tiled=True)
    batch_rows = jnp.take(buffer_all, shuffle, axis=0)
    blocks = batch_rows.reshape(feat_count, row_count, rows_each, width)
    inputs_half = lax.dynamic_slice_in_dim(
        jnp.swapaxes(blocks, 0, 1), row_pos * half_width, half_width, axis=3
    )
    inputs_half = inputs_half.reshape(total_rows, half_width)
    own_half_dec = dec_weight[0][:, 0]
    next_half_dec = dec_weight[0][:, 1]
    pre_all = lax.psum(dot_last(inputs_half, enc_weight[0]), "row") + enc_bias[0]
    features_all = jnp.maximum(pre_all, 0.0).astype(jnp.bfloat16)
    own_part = jnp.dot(features_all, own_half_dec, preferred_element_type=jnp.float32)
    next_part = jnp.dot(features_all, next_half_dec, preferred_element_type=jnp.float32)
    carried = from_behind(next_part, "layer", sub_blocks)
    spread = (own_part + carried).reshape(row_count, local_rows, half_width)
    halves = lax.psum_scatter(spread, "feat", scatter_dimension=1, tiled=True)
    joined = lax.all_to_all(halves, "row", split_axis=0, concat_axis=2, tiled=True)
    section_sum = joined.reshape(rows_each, width)
    target_ids = jnp.arange(LAYERS, dtype=jnp.int32)
    target_slots = jnp.where((target_ids == source)[:, None, None], section_sum[None], 0.0)
    totals = lax.psum(target_slots, "layer")
    recon_sum = jnp.swapaxes(totals, 0, 1) + dec_bias[None]
    errors = (recon_sum - mlp_out.astype(jnp.float32)).astype(jnp.bfloat16)
    gathered = lax.all_gather(errors, ("feat", "row"), axis=0, tiled=True)
    error_grid = gathered.reshape(feat_count, row_count, rows_each, LAYERS, width)
    errors_mine = lax.dynamic_index_in_dim(error_grid, row_pos, axis=1, keepdims=False)
    errors_mine = errors_mine.reshape(local_rows, LAYERS, width)
    errors_half = lax.dynamic_slice_in_dim(
        jnp.swapaxes(error_grid, 0, 1), row_pos * half_width, half_width, axis=4
    )
    errors_half = errors_half.reshape(total_rows, LAYERS, half_width)
    live_next = source + 1 < LAYERS
    next_index = jnp.minimum(source + 1, LAYERS - 1)
    half_own = lax.dynamic_index_in_dim(errors_half, source, axis=1, keepdims=False)
    half_next = lax.dynamic_index_in_dim(errors_half, next_index, axis=1, keepdims=False)
    half_next = jnp.where(live_next, half_next, jnp.zeros_like(half_next))
    half_terms = dot_last(half_own, own_half_dec) + dot_last(half_next, next_half_dec)
    grad_feats = lax.psum(half_terms, "row") * loss_scale
    grad_all = jnp.where(pre_all > 0, grad_feats, 0.0).astype(jnp.bfloat16)
    grad_own = loss_scale * dot_first(features_all, half_own)
    grad_next = loss_scale * dot_first(features_all, half_next)
    enc_grad = dot_first(grad_all, inputs_half).astype(jnp.bfloat16)
    dec_grad = jnp.stack([grad_own, grad_next], axis=1).astype(jnp.bfloat16)
    bias_grad = jnp.sum(grad_all.astype(jnp.float32), axis=0)
    return (recon_sum.astype(jnp.bfloat16), enc_grad[None], dec_grad[None], bias_grad[None])


def solution(mesh):
    return jax.shard_map(
        on_device,
        mesh=mesh,
        in_specs=(
            P(("groups", "feat", "row"), None, None),
            P("groups"),
            P(("groups", "feat", "row"), None, None),
            P("layer", "feat", "row"),
            P("layer", "feat", None, "row"),
            P("layer", "feat"),
            P(),
        ),
        out_specs=(
            P(("groups", "feat", "row"), None, None),
            P(("groups", "layer"), "feat", "row"),
            P(("groups", "layer"), "feat", None, "row"),
            P(("groups", "layer"), "feat"),
        ),
        check_vma=False,
    )
```

profile of v0, /device:TPU:0, one launch (start us, length us, event | category | flops | bytes accessed | tf_op | source)
XLA Modules:
  0.0 531.1 jit_solution(15762774988231695739)
XLA Ops:
  7.2 1.0 copy-done
  8.2 0.6 constant_dynamic-slice_fusion.1
  8.9 0.7 copy.39
  9.8 34.8 %all-gather.6.cloned.1.call-done = bf16[256,1,4608]{2,0,1:T(8,128)(2,1)} async-done(((bf16[32,1,4608]{2,0,1:T(8,128)(2,1)}), bf16[256,1,4608]{2,0,1:T(8,128)(2,1)}) %all-gather.6.cloned.1.call-update) | async-done | bytes 2359312 | tf_op jit(solution)/shard_map/all_gather | solution.py:41
  44.6 6.3 %gather_fusion = bf16[256,4608]{1,0:T(8,128)(2,1)S(1)} fusion(bf16[256,4608]{1,0:T(8,128)(2,1)} %bitcast.65, s32[1024]{0:T(1024)S(1)} %pad_clamp_fusion), kind=kCustom, calls=%fused_computation | custom fusion | bytes 4719616 | tf_op jit(solution)/shard_map/jit(_take)/gather | solution.py:42
  51.2 1.0 copy-done.4
  52.2 7.6 %fusion.3 = f32[256,2048]{1,0:T(8,128)} fusion(bf16[256,2304]{1,0:T(8,128)(2,1)S(1)} %bitcast.71, bf16[1,2048,2304]{2,1,0:T(8,128)(2,1)} %param.10), kind=kOutput, calls=%fused_computation.11 | convolution fusion | flops 2415919104 | bytes 12713984 | tf_op jit(solution)/shard_map/dot_general | solution.py:16
  59.9 18.4 %copy.45 = bf16[1,2048,2,2304]{3,1,2,0:T(8,128)(2,1)} copy(bf16[1,2048,2,2304]{3,2,1,0:T(2,128)(2,1)} %param.11) | data formatting | bytes 37748736 | tf_op args[4]
  78.4 2.0 all-reduce.6.cloned.1.call-done
  80.3 2.0 maximum_convert_fusion
  82.3 6.6 %fusion.8 = f32[256,2304]{1,0:T(8,128)S(1)} fusion(bf16[256,2048]{1,0:T(8,128)(2,1)S(1)} %maximum_convert_fusion, bf16[2048,2,2304]{2,0,1:T(8,128)(2,1)} %bitcast.66), kind=kOutput, calls=%fused_computation.16 | convolution fusion | flops 2415919104 | bytes 12845056 | tf_op jit(solution)/shard_map/dot_general | solution.py:53
  88.9 4.1 collective-permute-start
  93.0 50.6 %collective-permute-done = f32[256,2304]{1,0:T(8,128)S(1)} collective-permute-done((f32[256,2304]{1,0:T(8,128)S(1)}, f32[256,2304]{1,0:T(8,128)S(1)}, u32[]{:S(2)}, u32[]{:S(2)}) %collective-permute-start) | collective-permute-done | bytes 2359328 | tf_op jit(solution)/shard_map/ppermute | solution.py:12
  143.7 2.7 fusion.9
  146.4 3.2 copy.32
  151.5 95.8 %all-reduce.12.cloned.1.call-done = f32[2,128,2304]{2,0,1:T(2,128)} async-done(((f32[2,128,2304]{2,0,1:T(2,128)}), f32[2,128,2304]{2,0,1:T(2,128)}) %all-reduce.12.cloned.1.call-update) | async-done | bytes 2359312
  247.3 1.1 constant_dynamic-slice_fusion.2
  248.5 4.2 all_to_all.15
  253.2 1.2 broadcast_select_fusion
  254.4 42.1 %all-reduce.8.cloned.1.call-done = f32[2,32,4608]{2,1,0:T(8,128)} async-done(((f32[2,32,4608]{2,1,0:T(8,128)}), f32[2,32,4608]{2,1,0:T(8,128)}) %all-reduce.8.cloned.1.call-update) | async-done | bytes 1179664 | tf_op jit(solution)/shard_map/psum | solution.py:61
  296.5 2.5 fusion.15
  299.1 1.4 copy.37
  300.6 50.3 %all-gather.4.cloned.1.call-done = bf16[256,2,4608]{2,0,1:T(8,128)(2,1)} async-done(((bf16[32,2,4608]{2,0,1:T(8,128)(2,1)}), bf16[256,2,4608]{2,0,1:T(8,128)(2,1)}) %all-gather.4.cloned.1.call-update) | async-done | bytes 4718608 | tf_op jit(solution)/shard_map/all_gather | solution.py:64
  350.8 1.9 dynamic-slice_bitcast_fusion
  352.9 6.1 %fusion.5 = f32[256,2048]{1,0:T(8,128)S(1)} fusion(bf16[2048,2,2304]{2,0,1:T(8,128)(2,1)} %bitcast.67, bf16[256,2,2304]{2,0,1:T(8,128)(2,1)S(1)} %bitcast.73, s32[]{:T(128)S(6)} %select_n.47), kind=kOutput, calls=%fused_computation.13 | convolution fusion | flops 2415919104 | bytes 12713988 | tf_op jit(solution)/shard_map/dot_general | solution.py:16
  359.0 7.7 %fusion.10 = f32[256,2048]{1,0:T(8,128)} fusion(f32[256,2048]{1,0:T(8,128)S(1)} %fusion.5, bf16[2048,2,2304]{2,0,1:T(8,128)(2,1)} %bitcast.68, bf16[256,2,2304]{2,0,1:T(8,128)(2,1)S(1)} %bitcast.74, s32[]{:T(128)S(6)} %select_n.52, pred[]{:T(512)S(6)} %lt.28), kind=kOutput, calls=%fused_computation.18 | convolution fusion | flops 2417033216 | bytes 14811141 | tf_op jit(solution)/shard_map/dot_general | solution.py:16
  366.7 4.4 fusion.1
  371.0 5.2 fusion.2
  376.3 7.4 %pad_maximum_fusion = bf16[1,2048,2,2304]{3,1,2,0:T(8,128)(2,1)S(1)} fusion(bf16[1,2048,1,2304]{3,1,2,0:T(8,128)(2,1)} %fusion.2, bf16[1,2048,1,2304]{3,1,2,0:T(8,128)(2,1)S(1)} %fusion.1), kind=kLoop, calls=%fused_computation.1 | loop fusion | flops 9437184 | bytes 37748736 | tf_op jit(solution)/shard_map/stack | solution.py:83
  383.7 132.7 %copy.38 = bf16[1,2048,2,2304]{3,2,1,0:T(2,128)(2,1)} copy(bf16[1,2048,2,2304]{3,1,2,0:T(8,128)(2,1)S(1)} %pad_maximum_fusion) | data formatting | bytes 37748736
  516.4 2.7 convert_reduce_fusion
  519.1 5.2 fusion
  (50 shorter events, 2.7 us)
Async XLA Ops:
  7.2 1.1 copy-start
  7.2 2.5 copy-start.11
  7.2 37.4 %all-gather.6.cloned.1.call-start = ((), (), s32[]{:S(2)}) async-start(), calls=%async_computation.5 | async-start | bytes 2654208 | tf_op jit(solution)/shard_map/all_gather | solution.py:41
  9.6 70.7 %all-reduce.6.cloned.1.call-start = ((), (), s32[]{:S(2)}) async-start(), calls=%async_computation.1 | async-start | bytes 4194304 | tf_op jit(solution)/shard_map/psum | solution.py:50
  51.2 1.0 copy-start.4
  59.9 20.5 %copy-start.10 = (f32[1,2048]{1,0:T(1,128)S(1)}, f32[1,2048]{1,0:T(1,128)}, u32[]{:S(2)}) copy-start(f32[1,2048]{1,0:T(1,128)} %param.12) | copy-start | bytes 24580
  59.9 187.5 %all-reduce.12.cloned.1.call-start = ((), (), s32[]{:S(2)}) async-start(), calls=%async_computation.6 | async-start | bytes 4718592
  80.3 63.3 %copy-start.2 = (bf16[1,2048,2,2304]{3,1,2,0:T(8,128)(2,1)S(1)}, bf16[1,2048,2,2304]{3,1,2,0:T(8,128)(2,1)}, u32[]{:S(2)}) copy-start(bf16[1,2048,2,2304]{3,1,2,0:T(8,128)(2,1)} %copy.45) | copy-start | bytes 56623108
  88.9 54.7 %collective-permute-start = (f32[256,2304]{1,0:T(8,128)S(1)}, f32[256,2304]{1,0:T(8,128)S(1)}, u32[]{:S(2)}, u32[]{:S(2)}) collective-permute-start(f32[256,2304]{1,0:T(8,128)S(1)} %fusion.8), channel_id=1, source_target_pairs={{0,2},{1,3},{4,6},{5,7},{8,10},{9,11},{12,14},{13,15},{16,18},{17,... | collective-permute-start | bytes 7077896 | tf_op jit(solution)/shard_map/ppermute | solution.py:12
  149.6 0.7 copy-start.12
  149.6 146.9 %all-reduce.8.cloned.1.call-start = ((), (), s32[]{:S(2)}) async-start(), calls=%async_computation.2 | async-start | bytes 2359296 | tf_op jit(solution)/shard_map/psum | solution.py:61
  253.2 43.3 %copy-start.9 = (f32[2,4608]{1,0:T(2,128)S(1)}, f32[2,4608]{1,0:T(2,128)}, u32[]{:S(2)}) copy-start(f32[2,4608]{1,0:T(2,128)} %param.13) | copy-start | bytes 110596
  254.4 96.4 %all-gather.4.cloned.1.call-start = ((), (), s32[]{:S(2)}) async-start(), calls=%async_computation.3 | async-start | bytes 5308416 | tf_op jit(solution)/shard_map/all_gather | solution.py:64
  296.5 2.6 copy-start.6
  299.0 217.4 %all-reduce.10.cloned.1.call-start = ((), (), s32[]{:S(2)}) async-start(), calls=%async_computation.4 | async-start | bytes 4194304 | tf_op jit(solution)/shard_map/psum | solution.py:78
  352.9 6.1 %copy-start.7 = (bf16[2,4,32,2,2304]{4,2,1,0,3:T(8,128)(2,1)}, bf16[2,4,32,2,2304]{4,2,1,0,3:T(8,128)(2,1)S(1)}, u32[]{:S(2)}) copy-start(bf16[2,4,32,2,2304]{4,2,1,0,3:T(8,128)(2,1)S(1)} %copy.36) | copy-start | bytes 7077892
  366.6 4.4 copy-start.8
  383.7 132.7 %copy-start.3 = (f32[256,2048]{1,0:T(8,128)S(1)}, f32[256,2048]{1,0:T(8,128)}, u32[]{:S(2)}) copy-start(f32[256,2048]{1,0:T(8,128)} %all-reduce.6.cloned.1.call-done) | copy-start | bytes 6291460
  516.4 2.7 copy-start.5
  519.1 5.2 copy-start.1
Sparse Core Ops, SparseCore 0:
  10.2 34.3 all-gather.5
  60.0 20.3 all-reduce.5
  149.7 97.5 all-reduce.11
  254.5 41.9 all-reduce.7
  299.1 51.6 all-gather.3
  366.8 20.0 all-reduce.9
where the time goes:
time: 532 us; the launch traced here: 531 us
  waiting for transfers between devices  276 us (52%)
  local copies, waits for them, and re-layouts  170 us (32%)
  matrix products  45.5 us (9%)
  other arithmetic  16.1 us (3%)
  between operations  15 us (3%)
    unnamed x33, local copies, waits for them, and re-layouts  158 us
    unnamed x7, waiting for transfers between devices  95.9 us
    ppermute x1, waiting for transfers between devices, from_behind(): return lax.ppermute(block, axis, route)  50.6 us
    all_gather x1, waiting for transfers between devices, on_device(): gathered = lax.all_gather(errors, ('feat', 'row'), axis=0, tiled=True)  50.3 us
    psum x1, waiting for transfers between devices, on_device(): totals = lax.psum(target_slots, 'layer')  42.1 us
    all_gather x1, waiting for transfers between devices, on_device(): buffer_all = lax.all_gather(own_layer, ('feat', 'row'), axis=0, tiled=True)  34.8 us
    dot_general x3, matrix products, dot_last(): lax.dot_general(left, right, (((1,), (1,)), ((), ())), preferred_element_...  21.3 us
    dot_general x3, matrix products, dot_first(): lax.dot_general(left, right, (((0,), (0,)), ((), ())), preferred_element_...  14.8 us
  transfers between devices with their start and end apart: 7, of which 6 were waited for; matrix products, arithmetic and copies ran while one was open for 32% of the time, Pallas kernels for 0%

commit v1 on v0

v1 whole, which is shorter than its diff:
```python
import functools

import jax
import jax.numpy as jnp
from jax import lax
from jax.experimental import pallas as pl
from jax.experimental.pallas import tpu as pltpu
from jax.sharding import PartitionSpec as P

CHUNKS = 2


def shifted(block, axis, distance):
    count = lax.axis_size(axis)
    return lax.ppermute(block, axis, [(i, (i + distance) % count) for i in range(count)])


def dot_last(left, right):
    return lax.dot_general(
        left, right, (((1,), (1,)), ((), ())), preferred_element_type=jnp.float32
    )


def dot_first(left, right):
    return lax.dot_general(
        left, right, (((0,), (0,)), ((), ())), preferred_element_type=jnp.float32
    )


def shift_order(count):
    return sorted(range(1, count), key=lambda k: -min(k, count - k))


def dec_grad_kernel(scale, features_ref, own_ref, next_ref, out_ref):
    features = features_ref[...]
    own = dot_first(features, own_ref[...])
    out_ref[:, 0, :] = (scale * own).astype(out_ref.dtype)
    following = dot_first(features, next_ref[...])
    out_ref[:, 1, :] = (scale * following).astype(out_ref.dtype)


def dec_grad_call(features, own, following, scale):
    rows, count = features.shape
    width = own.shape[1]
    block = min(128, count)
    return pl.pallas_call(
        functools.partial(dec_grad_kernel, scale),
        grid=(count // block,),
        in_specs=[
            pl.BlockSpec((rows, block), lambda i: (0, i)),
            pl.BlockSpec((rows, width), lambda i: (0, 0)),
            pl.BlockSpec((rows, width), lambda i: (0, 0)),
        ],
        out_specs=pl.BlockSpec((block, 2, width), lambda i: (i, 0, 0)),
        out_shape=jax.ShapeDtypeStruct((count, 2, width), jnp.bfloat16),
        cost_estimate=pl.CostEstimate(
            flops=4 * rows * count * width,
            bytes_accessed=4 * count * width + 4 * rows * width + 2 * rows * count,
            transcendentals=0,
        ),
        compiler_params=pltpu.CompilerParams(vmem_limit_bytes=32 * 1024 * 1024),
    )(features, own, following)


def on_device(resid_buf, shuffle, mlp_out, enc_weight, dec_weight, enc_bias, dec_bias):
    f32, bf16 = jnp.float32, jnp.bfloat16
    feat_count = lax.axis_size("feat")
    layer_count = lax.axis_size("layer")
    layers = resid_buf.shape[1]
    sub_blocks = layer_count // layers
    feat_pos = lax.axis_index("feat")
    source = lax.axis_index("layer") // sub_blocks
    row_pos = lax.axis_index("row")
    first_core = row_pos == 0
    leading = source + 1 < layers
    rows_each, _, width = resid_buf.shape
    half = enc_weight.shape[2]
    piece = half // CHUNKS
    block_rows = rows_each * lax.axis_size("row")
    total_rows = block_rows * feat_count
    loss_scale = float(total_rows) ** (-0.5)
    order = shift_order(feat_count)

    def to_half(block):
        left, right = block[:, :half], block[:, half:]
        mine = jnp.where(first_core, left, right)
        got = shifted(jnp.where(first_core, right, left), "row", 1)
        return jnp.concatenate(
            [jnp.where(first_core, mine, got), jnp.where(first_core, got, mine)], axis=0
        )

    def from_half(block):
        upper, lower = block[:rows_each], block[rows_each:]
        mine = jnp.where(first_core, upper, lower)
        got = shifted(jnp.where(first_core, lower, upper), "row", 1)
        return jnp.concatenate(
            [jnp.where(first_core, mine, got), jnp.where(first_core, got, mine)], axis=1
        )

    def section_total(block):
        total = block
        for step in range(1, sub_blocks):
            pairs = [
                (i, (i // sub_blocks) * sub_blocks + (i + step) % sub_blocks)
                for i in range(layer_count)
            ]
            total = total + lax.ppermute(block, "layer", pairs)
        return total

    own_layer = jnp.where(leading, resid_buf[:, 0], resid_buf[:, layers - 1])
    own_block = to_half(own_layer)
    arrived = {0: own_block}
    for k in order:
        arrived[k] = shifted(own_block, "feat", k)
    buffered = jnp.concatenate([arrived[k] for k in range(feat_count)], axis=0)
    blocks = shuffle.reshape(feat_count, block_rows)
    relative = (feat_pos - jnp.arange(feat_count)) % feat_count
    wanted = jnp.take(blocks, relative, axis=0).reshape(total_rows)
    place = ((feat_pos - wanted // block_rows) % feat_count) * block_rows + wanted % block_rows
    picks = (place[:, None] == jnp.arange(total_rows)[None]).astype(bf16)
    inputs = jnp.dot(picks, buffered, preferred_element_type=f32).astype(bf16)

    mlp_half = [to_half(mlp_out[:, t]) for t in range(layers)]
    bias_half = lax.dynamic_slice_in_dim(dec_bias, row_pos * half, half, axis=1)
    own_dec = dec_weight[0][:, 0]
    next_dec = dec_weight[0][:, 1]

    partial_pre = dot_last(inputs, enc_weight[0])
    pre = partial_pre + shifted(partial_pre, "row", 1) + enc_bias
    features = jnp.maximum(pre, 0.0).astype(bf16)

    next_part = jnp.dot(features, next_dec, preferred_element_type=f32).astype(bf16)
    own_part = jnp.dot(features, own_dec, preferred_element_type=f32)
    sent_part = own_part.astype(bf16)
    forward = [(i, i + sub_blocks) for i in range(layer_count - sub_blocks)]
    backward = [(j, i) for i, j in forward]

    def rows_of(array, k):
        j = (feat_count - k) % feat_count
        return array[j * block_rows : (j + 1) * block_rows]

    columns = [slice(c * piece, (c + 1) * piece) for c in range(CHUNKS)]
    carried = [lax.ppermute(next_part[:, cols], "layer", forward) for cols in columns]
    own_sum = []
    for cols in columns:
        total = rows_of(own_part, 0)[:, cols]
        for k in order:
            total = total + shifted(rows_of(sent_part, k)[:, cols], "feat", k).astype(f32)
        own_sum.append(total)
    first_errors, last_errors, rebuilt = [], [], []
    for c, cols in enumerate(columns):
        recon_first = section_total(own_sum[c]) + bias_half[0, cols]
        error_first = (recon_first - mlp_half[0][:, cols].astype(f32)).astype(bf16)
        gathered = {0: error_first}
        total = own_sum[c] + rows_of(carried[c], 0).astype(f32)
        for k in order:
            got = shifted(jnp.where(leading, error_first, rows_of(carried[c], k)), "feat", k)
            gathered[k] = got
            total = total + got.astype(f32)
        recon_last = section_total(total) + bias_half[layers - 1, cols]
        error_last = (recon_last - mlp_half[layers - 1][:, cols].astype(f32)).astype(bf16)
        error_last = jnp.where(leading, lax.ppermute(error_last, "layer", backward), error_last)
        own_rebuilt = jnp.where(leading, recon_first, recon_last).astype(bf16)
        other = shifted(own_rebuilt, "layer", sub_blocks)
        rebuilt.append(
            (jnp.where(leading, own_rebuilt, other), jnp.where(leading, other, own_rebuilt))
        )
        first_errors.append(jnp.concatenate([gathered[k] for k in range(feat_count)], axis=0))
        last = {0: error_last}
        for k in order:
            last[k] = shifted(error_last, "feat", k)
        last_errors.append(jnp.concatenate([last[k] for k in range(feat_count)], axis=0))
    first_error = jnp.concatenate(first_errors, axis=1)
    last_error = jnp.concatenate(last_errors, axis=1)
    own_error = jnp.where(leading, first_error, last_error)
    next_error = jnp.where(leading, last_error, jnp.zeros_like(last_error))

    terms = dot_last(own_error, own_dec) + dot_last(next_error, next_dec)
    grad_feats = (terms + shifted(terms, "row", 1)) * loss_scale
    grad_pre = jnp.where(pre > 0, grad_feats, 0.0).astype(bf16)
    dec_grad = dec_grad_call(features, own_error, next_error, loss_scale)
    enc_grad = dot_first(grad_pre, inputs).astype(bf16)
    bias_grad = jnp.sum(grad_pre.astype(f32), axis=0)
    halves = [jnp.concatenate([piece_[t] for piece_ in rebuilt], axis=1) for t in range(layers)]
    output = jnp.stack([from_half(block) for block in halves], axis=1)
    return output, enc_grad[None], dec_grad[None], bias_grad[None]


def solution(mesh):
    return jax.shard_map(
        on_device,
        mesh=mesh,
        in_specs=(
            P(("groups", "feat", "row"), None, None),
            P("groups"),
            P(("groups", "feat", "row"), None, None),
            P("layer", "feat", "row"),
            P("layer", "feat", None, "row"),
            P("layer", "feat"),
            P(),
        ),
        out_specs=(
            P(("groups", "feat", "row"), None, None),
            P(("groups", "layer"), "feat", "row"),
            P(("groups", "layer"), "feat", None, "row"),
            P(("groups", "layer"), "feat"),
        ),
        check_vma=False,
    )
```

time: 532 us -> 215 us (0.40)
  waiting for transfers between devices: 276 us -> 65.7 us
  local copies, waits for them, and re-layouts: 170 us -> 24.7 us
  starting transfers between devices: 4.35 us -> 56.4 us
  Pallas kernels: 0 us -> 15.8 us
  matrix products: 45.5 us -> 29.8 us
  between operations: 15 us -> 1.17 us
    unnamed x33 -> x42, local copies, waits for them, and re-layouts: 158 us -> 20.5 us
    unnamed x7 -> x0, waiting for transfers between devices: 95.9 us -> none
    all_gather x2 -> x0, waiting for transfers between devices: 85 us -> none  [the longest x1 50.3 us: on_device(): gathered = lax.all_gather(errors, ('feat', 'row'), axis=0, tiled=True)]
    ppermute x1 -> x34, starting transfers between devices: 4.1 us -> 56.4 us  [the longest x30 49.1 us: shifted(): lax.ppermute(block, axis, [(i, (i + distance) % count) for i in range(cou...]
    psum x3 -> x0, waiting for transfers between devices: 44 us -> none  [the longest x1 42.1 us: on_device(): totals = lax.psum(target_slots, 'layer')]
    pallas_call x0 -> x1, Pallas kernels: none -> 15.8 us  [dec_grad_call(): pl.pallas_call(functools.partial(dec_grad_kernel, scale), grid=(count //...]
    ppermute x1 -> x34, waiting for transfers between devices: 50.6 us -> 65.7 us  [the longest x30 61.1 us: shifted(): lax.ppermute(block, axis, [(i, (i + distance) % count) for i in range(cou...]
    select_n x3 -> x21, other arithmetic: 1.43 us -> 14.4 us  [the longest x1 8.24 us: on_device(): own_error = jnp.where(leading, first_error, last_error)]
  transfers between devices with their start and end apart: 7 -> 34, of which waited for: 6 -> 13; matrix products, arithmetic and copies ran while one was open for 32% -> 27% of each run, Pallas kernels for 0% -> 7%
where the time goes in v1:
time: 215 us; the launch traced here: 214 us
  waiting for transfers between devices  65.7 us (31%)
  starting transfers between devices  56.4 us (26%)
  matrix products  29.8 us (14%)
  local copies, waits for them, and re-layouts  24.7 us (11%)
  other arithmetic  20.8 us (10%)
  Pallas kernels  15.8 us (7%)
    ppermute x30, waiting for transfers between devices, shifted(): lax.ppermute(block, axis, [(i, (i + distance) % count) for i in range(cou...  61.1 us
    ppermute x30, starting transfers between devices, shifted(): lax.ppermute(block, axis, [(i, (i + distance) % count) for i in range(cou...  49.1 us
    unnamed x42, local copies, waits for them, and re-layouts  20.5 us
    pallas_call x1, Pallas kernels, dec_grad_call(): pl.pallas_call(functools.partial(dec_grad_kernel, scale), grid=(count //...  15.8 us
    dot_general x3, matrix products, dot_last(): lax.dot_general(left, right, (((1,), (1,)), ((), ())), preferred_element_...  14.7 us
    select_n x1, other arithmetic, on_device(): own_error = jnp.where(leading, first_error, last_error)  8.24 us
    dot_general x1, matrix products, on_device(): jnp.dot(features, next_dec, preferred_element_type=f32).astype(bf16)  6.71 us
    dot_general x1, matrix products, dot_first(): lax.dot_general(left, right, (((0,), (0,)), ((), ())), preferred_element_...  5.19 us
  transfers between devices with their start and end apart: 34, of which 13 were waited for; matrix products, arithmetic and copies ran while one was open for 27% of the time, Pallas kernels for 7%

profile of v1, /device:TPU:0, one launch (start us, length us, event | category | flops | bytes accessed | tf_op | source)
XLA Modules:
  0.0 214.4 jit_solution(16601745632046433446)
XLA Ops:
  0.6 2.3 %fusion.30 = (bf16[32,1,4608]{2,1,0:T(2,128)(2,1)S(1)}, bf16[32,1,4608]{2,1,0:T(2,128)(2,1)S(1)}) fusion(bf16[32,2,4608]{2,1,0:T(2,128)(2,1)} %param.7), kind=kLoop, calls=%fused_computation.131 | loop fusion | bytes 1179648 | tf_op jit(solution)/shard_map/slice | solution.py:110
  4.8 3.0 %collective-permute-start.1 = (bf16[64,2304]{1,0:T(8,128)(2,1)S(1)}, bf16[64,2304]{1,0:T(8,128)(2,1)S(1)}, u32[]{:S(2)}, u32[]{:S(2)}) collective-permute-start(bf16[64,2304]{1,0:T(8,128)(2,1)S(1)} %pad_maximum_fusion.1), channel_id=1, source_target_pairs={{0,4},{4,8},{8,12},{12,0},{1,5},{5,9},{9,13},{13,1},{2,6},{6,10},{... | collective-permute-start | bytes 884744 | tf_op jit(solution)/shard_map/ppermute | solution.py:15
  11.0 6.6 %collective-permute-done.1 = bf16[64,2304]{1,0:T(8,128)(2,1)S(1)} collective-permute-done((bf16[64,2304]{1,0:T(8,128)(2,1)S(1)}, bf16[64,2304]{1,0:T(8,128)(2,1)S(1)}, u32[]{:S(2)}, u32[]{:S(2)}) %collective-permute-start.1) | collective-permute-done | bytes 294944 | tf_op jit(solution)/shard_map/ppermute | solution.py:15
  17.7 18.4 %collective-permute-done.2 = bf16[64,2304]{1,0:T(8,128)(2,1)S(1)} collective-permute-done((bf16[64,2304]{1,0:T(8,128)(2,1)S(1)}, bf16[64,2304]{1,0:T(8,128)(2,1)S(1)}, u32[]{:S(2)}, u32[]{:S(2)}) %collective-permute-start.2) | collective-permute-done | bytes 294944 | tf_op jit(solution)/shard_map/ppermute | solution.py:15
  36.7 5.6 %fusion.1 = f32[256,2048]{1,0:T(8,128)S(1)} fusion(bf16[256,2304]{1,0:T(8,128)(2,1)S(1)} %convolution_convert_fusion.1, bf16[1,2048,2304]{2,1,0:T(8,128)(2,1)} %param.10), kind=kOutput, calls=%fused_computation.6 | convolution fusion | flops 2415919104 | bytes 12713984 | tf_op jit(solution)/shard_map/dot_general | solution.py:19
  44.6 18.2 %copy.33 = bf16[1,2048,2,2304]{3,1,2,0:T(8,128)(2,1)} copy(bf16[1,2048,2,2304]{3,2,1,0:T(2,128)(2,1)} %param.11) | data formatting | bytes 37748736 | tf_op args[4]
  63.0 2.8 %maximum_convert_fusion.features_ref = bf16[256,2048]{1,0:T(8,128)(2,1)S(1)} fusion(f32[2048]{0:T(1024)S(1)} %bitcast.56, f32[256,2048]{1,0:T(8,128)} %copy-done.1, f32[256,2048]{1,0:T(8,128)} %collective-permute-done.4), kind=kLoop, calls=%fused_computation.17 | loop fusion | flops 2097152 | bytes 5251072 | tf_op jit(solution)/shard_map/convert_element_type | solution.py:130
  65.8 6.7 %fusion.7 = bf16[256,2304]{1,0:T(8,128)(2,1)S(1)} fusion(bf16[256,2048]{1,0:T(8,128)(2,1)S(1)} %maximum_convert_fusion.features_ref, bf16[2048,2,2304]{2,0,1:T(8,128)(2,1)} %bitcast.47), kind=kOutput, calls=%fused_computation.12 | convolution fusion | flops 2416508928 | bytes 11665408 | tf_op jit(solution)/shard_map/dot_general | solution.py:132
  73.3 2.6 %fusion.31 = (bf16[256,2304]{1,0:T(8,128)(2,1)S(1)}, f32[256,2304]{1,0:T(8,128)S(1)}) fusion(bf16[256,2048]{1,0:T(8,128)(2,1)S(1)} %maximum_convert_fusion.features_ref, bf16[2048,2,2304]{2,0,1:T(8,128)(2,1)S(1)} %bitcast.48), kind=kOutput, calls=%fused_computation.132 | convolution fusion | flops 2416508928 | bytes 14024704 | tf_op jit(solution)/shard_map/dot_general | solution.py:133
  78.4 3.4 %collective-permute-start.8 = (bf16[256,1152]{1,0:T(8,128)(2,1)S(1)}, bf16[256,1152]{1,0:T(8,128)(2,1)S(1)}, u32[]{:S(2)}, u32[]{:S(2)}) collective-permute-start(bf16[256,1152]{1,0:T(8,128)(2,1)S(1)} %get-tuple-element.41), channel_id=1, source_target_pairs={{0,2},{1,3},{4,6},{5,7},{8,10},{9,11},{12,14},{13,15},{16,18},{17,... | collective-permute-start | bytes 1769480 | tf_op jit(solution)/shard_map/ppermute | solution.py:143
  83.2 2.5 %collective-permute-done.5 = bf16[64,1152]{1,0:T(8,128)(2,1)S(1)} collective-permute-done((bf16[64,1152]{1,0:T(8,128)(2,1)S(1)}, bf16[64,1152]{1,0:T(8,128)(2,1)S(1)}, u32[]{:S(2)}, u32[]{:S(2)}) %collective-permute-start.5) | collective-permute-done | bytes 147488 | tf_op jit(solution)/shard_map/ppermute | solution.py:15
  86.0 2.8 %collective-permute-done.16 = bf16[64,1152]{1,0:T(8,128)(2,1)S(1)} collective-permute-done((bf16[64,1152]{1,0:T(8,128)(2,1)S(1)}, bf16[64,1152]{1,0:T(8,128)(2,1)S(1)}, u32[]{:S(2)}, u32[]{:S(2)}) %collective-permute-start.16) | collective-permute-done | bytes 147488 | tf_op jit(solution)/shard_map/ppermute | solution.py:15
  91.1 6.4 %collective-permute-start.6 = (bf16[64,1152]{1,0:T(8,128)(2,1)S(1)}, bf16[64,1152]{1,0:T(8,128)(2,1)S(1)}, u32[]{:S(2)}, u32[]{:S(2)}) collective-permute-start(bf16[64,1152]{1,0:T(8,128)(2,1)S(1)} %get-tuple-element.40), channel_id=1, source_target_pairs={{0,4},{4,8},{8,12},{12,0},{1,5},{5,9},{9,13},{13,1},{2,6},{6,10},{... | collective-permute-start | bytes 442376 | tf_op jit(solution)/shard_map/ppermute | solution.py:15
  98.8 3.7 %collective-permute-done.7 = bf16[64,1152]{1,0:T(8,128)(2,1)S(1)} collective-permute-done((bf16[64,1152]{1,0:T(8,128)(2,1)S(1)}, bf16[64,1152]{1,0:T(8,128)(2,1)S(1)}, u32[]{:S(2)}, u32[]{:S(2)}) %collective-permute-start.7) | collective-permute-done | bytes 147488 | tf_op jit(solution)/shard_map/ppermute | solution.py:15
  102.5 4.6 %collective-permute-done.17 = bf16[256,1152]{1,0:T(8,128)(2,1)S(1)} collective-permute-done((bf16[256,1152]{1,0:T(8,128)(2,1)S(1)}, bf16[256,1152]{1,0:T(8,128)(2,1)S(1)}, u32[]{:S(2)}, u32[]{:S(2)}) %collective-permute-start.17) | collective-permute-done | bytes 589856 | tf_op jit(solution)/shard_map/ppermute | solution.py:143
  107.4 2.5 %collective-permute-start.10 = (bf16[64,1152]{1,0:T(8,128)(2,1)S(1)}, bf16[64,1152]{1,0:T(8,128)(2,1)S(1)}, u32[]{:S(2)}, u32[]{:S(2)}) collective-permute-start(bf16[64,1152]{1,0:T(8,128)(2,1)S(1)} %get-tuple-element.18), channel_id=1, source_target_pairs={{0,8},{4,12},{8,0},{12,4},{1,9},{5,13},{9,1},{13,5},{2,10},{6,14},... | collective-permute-start | bytes 442376 | tf_op jit(solution)/shard_map/ppermute | solution.py:15
  114.6 10.3 %collective-permute-done.10 = bf16[64,1152]{1,0:T(8,128)(2,1)S(1)} collective-permute-done((bf16[64,1152]{1,0:T(8,128)(2,1)S(1)}, bf16[64,1152]{1,0:T(8,128)(2,1)S(1)}, u32[]{:S(2)}, u32[]{:S(2)}) %collective-permute-start.10) | collective-permute-done | bytes 147488 | tf_op jit(solution)/shard_map/ppermute | solution.py:15
  126.4 2.7 %collective-permute-start.13 = (bf16[64,1152]{1,0:T(8,128)(2,1)S(1)}, bf16[64,1152]{1,0:T(8,128)(2,1)S(1)}, u32[]{:S(2)}, u32[]{:S(2)}) collective-permute-start(bf16[64,1152]{1,0:T(8,128)(2,1)S(1)} %get-tuple-element.32), channel_id=1, source_target_pairs={{0,2},{2,0},{1,3},{3,1},{4,6},{6,4},{5,7},{7,5},{8,10},{10,8},{9,1... | collective-permute-start | bytes 442376 | tf_op jit(solution)/shard_map/ppermute | solution.py:15
  133.5 2.7 %collective-permute-start.21 = (bf16[64,1152]{1,0:T(8,128)(2,1)S(1)}, bf16[64,1152]{1,0:T(8,128)(2,1)S(1)}, u32[]{:S(2)}, u32[]{:S(2)}) collective-permute-start(bf16[64,1152]{1,0:T(8,128)(2,1)S(1)} %get-tuple-element.34), channel_id=1, source_target_pairs={{0,2},{2,0},{1,3},{3,1},{4,6},{6,4},{5,7},{7,5},{8,10},{10,8},{9,1... | collective-permute-start | bytes 442376 | tf_op jit(solution)/shard_map/ppermute | solution.py:15
  136.3 4.5 %collective-permute-start.28 = (bf16[64,1152]{1,0:T(8,128)(2,1)S(1)}, bf16[64,1152]{1,0:T(8,128)(2,1)S(1)}, u32[]{:S(2)}, u32[]{:S(2)}) collective-permute-start(bf16[64,1152]{1,0:T(8,128)(2,1)S(1)} %broadcast_select_fusion.2), channel_id=1, source_target_pairs={{0,12},{4,0},{8,4},{12,8},{1,13},{5,1},{9,5},{13,9},{2,14},{6,2},{... | collective-permute-start | bytes 442376 | tf_op jit(solution)/shard_map/ppermute | solution.py:15
  140.8 3.3 %collective-permute-start.27 = (bf16[64,1152]{1,0:T(8,128)(2,1)S(1)}, bf16[64,1152]{1,0:T(8,128)(2,1)S(1)}, u32[]{:S(2)}, u32[]{:S(2)}) collective-permute-start(bf16[64,1152]{1,0:T(8,128)(2,1)S(1)} %broadcast_select_fusion.2), channel_id=1, source_target_pairs={{0,8},{4,12},{8,0},{12,4},{1,9},{5,13},{9,1},{13,5},{2,10},{6,14},... | collective-permute-start | bytes 442376 | tf_op jit(solution)/shard_map/ppermute | solution.py:15
  144.1 4.1 %collective-permute-start.26 = (bf16[64,1152]{1,0:T(8,128)(2,1)S(1)}, bf16[64,1152]{1,0:T(8,128)(2,1)S(1)}, u32[]{:S(2)}, u32[]{:S(2)}) collective-permute-start(bf16[64,1152]{1,0:T(8,128)(2,1)S(1)} %broadcast_select_fusion.2), channel_id=1, source_target_pairs={{0,4},{4,8},{8,12},{12,0},{1,5},{5,9},{9,13},{13,1},{2,6},{6,10},{... | collective-permute-start | bytes 442376 | tf_op jit(solution)/shard_map/ppermute | solution.py:15
  148.4 3.3 %collective-permute-start.31 = (bf16[64,1152]{1,0:T(8,128)(2,1)S(1)}, bf16[64,1152]{1,0:T(8,128)(2,1)S(1)}, u32[]{:S(2)}, u32[]{:S(2)}) collective-permute-start(bf16[64,1152]{1,0:T(8,128)(2,1)S(1)} %broadcast_select_fusion.1), channel_id=1, source_target_pairs={{0,8},{4,12},{8,0},{12,4},{1,9},{5,13},{9,1},{13,5},{2,10},{6,14},... | collective-permute-start | bytes 442376 | tf_op jit(solution)/shard_map/ppermute | solution.py:15
  152.5 2.3 %collective-permute-start.30 = (bf16[64,1152]{1,0:T(8,128)(2,1)S(1)}, bf16[64,1152]{1,0:T(8,128)(2,1)S(1)}, u32[]{:S(2)}, u32[]{:S(2)}) collective-permute-start(bf16[64,1152]{1,0:T(8,128)(2,1)S(1)} %broadcast_select_fusion.1), channel_id=1, source_target_pairs={{0,4},{4,8},{8,12},{12,0},{1,5},{5,9},{9,13},{13,1},{2,6},{6,10},{... | collective-permute-start | bytes 442376 | tf_op jit(solution)/shard_map/ppermute | solution.py:15
  155.5 9.0 %collective-permute-done.27 = bf16[64,1152]{1,0:T(8,128)(2,1)S(1)} collective-permute-done((bf16[64,1152]{1,0:T(8,128)(2,1)S(1)}, bf16[64,1152]{1,0:T(8,128)(2,1)S(1)}, u32[]{:S(2)}, u32[]{:S(2)}) %collective-permute-start.27) | collective-permute-done | bytes 147488 | tf_op jit(solution)/shard_map/ppermute | solution.py:15
  165.0 4.0 %collective-permute-done.31 = bf16[64,1152]{1,0:T(8,128)(2,1)S(1)} collective-permute-done((bf16[64,1152]{1,0:T(8,128)(2,1)S(1)}, bf16[64,1152]{1,0:T(8,128)(2,1)S(1)}, u32[]{:S(2)}, u32[]{:S(2)}) %collective-permute-start.31) | collective-permute-done | bytes 147488 | tf_op jit(solution)/shard_map/ppermute | solution.py:15
  169.2 3.9 %fusion.5 = f32[256,2048]{1,0:T(8,128)} fusion(bf16[256,2304]{1,0:T(8,128)(2,1)S(1)} %broadcast_select_fusion.next_ref, bf16[2048,2,2304]{2,0,1:T(8,128)(2,1)S(1)} %bitcast.49), kind=kOutput, calls=%fused_computation.10 | convolution fusion | flops 2415919104 | bytes 12713984 | tf_op jit(solution)/shard_map/dot_general | solution.py:19
  173.2 8.2 %maximum_select_fusion.own_ref = bf16[256,2304]{1,0:T(8,128)(2,1)S(1)} fusion(bf16[64,1152]{1,0:T(8,128)(2,1)} %copy-done.14, bf16[64,1152]{1,0:T(8,128)(2,1)} %copy-done.10, bf16[64,1152]{1,0:T(8,128)(2,1)} %copy-done.13, bf16[64,1152]{1,0:T(8,128)(2,1)S(1)} %get-tuple-element.29, bf16[64,1152]{1,0:T(8,128)(2,1)} %copy-done.12, ...), kind=kLoop, calls=%fused_computation.19 | loop fusion | flops 19464192 | bytes 3538945 | tf_op jit(solution)/shard_map/jit(_where)/select_n | solution.py:175
  181.4 5.1 %fusion.8 = f32[256,2048]{1,0:T(8,128)} fusion(f32[256,2048]{1,0:T(8,128)} %fusion.5, bf16[256,2304]{1,0:T(8,128)(2,1)S(1)} %maximum_select_fusion.own_ref, bf16[2048,2,2304]{2,0,1:T(8,128)(2,1)S(1)} %bitcast.50), kind=kOutput, calls=%fused_computation.14 | convolution fusion | flops 2416443392 | bytes 14811136 | tf_op jit(solution)/shard_map/dot_general | solution.py:19
  190.3 15.8 %shard_map.102 = bf16[2048,2,2304]{2,1,0:T(2,128)(2,1)} custom-call(bf16[256,2048]{1,0:T(8,128)(2,1)S(1)} %maximum_convert_fusion.features_ref, bf16[256,2304]{1,0:T(8,128)(2,1)S(1)} %maximum_select_fusion.own_ref, bf16[256,2304]{1,0:T(8,128)(2,1)S(1)} %broadcast_select_fusion.next_ref), custom_call_target="tpu_custom_call" | custom-call | flops 4831838208 | bytes 22282240 | tf_op jit(solution)/shard_map/pallas_call | solution.py:46
  206.1 3.0 %convert_reduce_fusion = (f32[2048]{0:T(1024)}, bf16[256,2048]{1,0:T(8,128)(2,1)S(1)}) fusion(f32[256,2048]{1,0:T(8,128)S(1)} %copy-done.6, f32[256,2048]{1,0:T(8,128)S(1)} %collective-permute-done.33, f32[2048]{0:T(1024)S(1)} %bitcast.57, f32[256,2048]{1,0:T(8,128)S(1)} %copy-done.2, f32[256,2048]{1,0:T(8,128)} %collective-permute-done.4), kind=kLoop, calls=%fused_computation.15 | loop fusion | flops 4716544 | bytes 9453568 | tf_op jit(solution)/shard_map/reduce_sum | solution.py:183
  209.2 5.2 %fusion = bf16[1,2048,2304]{2,1,0:T(8,128)(2,1)} fusion(bf16[256,2048]{1,0:T(8,128)(2,1)S(1)} %get-tuple-element.17, bf16[256,2304]{1,0:T(8,128)(2,1)S(1)} %copy-done.4), kind=kOutput, calls=%fused_computation.3 | convolution fusion | flops 2420637696 | bytes 11665408 | tf_op jit(solution)/shard_map/dot_general | solution.py:25
  (128 shorter events, 33.3 us)
Async XLA Ops:
  4.8 12.9 %collective-permute-start.1 = (bf16[64,2304]{1,0:T(8,128)(2,1)S(1)}, bf16[64,2304]{1,0:T(8,128)(2,1)S(1)}, u32[]{:S(2)}, u32[]{:S(2)}) collective-permute-start(bf16[64,2304]{1,0:T(8,128)(2,1)S(1)} %pad_maximum_fusion.1), channel_id=1, source_target_pairs={{0,4},{4,8},{8,12},{12,0},{1,5},{5,9},{9,13},{13,1},{2,6},{6,10},{... | collective-permute-start | bytes 884744 | tf_op jit(solution)/shard_map/ppermute | solution.py:15
  7.9 28.2 %collective-permute-start.3 = (bf16[64,2304]{1,0:T(8,128)(2,1)S(1)}, bf16[64,2304]{1,0:T(8,128)(2,1)S(1)}, u32[]{:S(2)}, u32[]{:S(2)}) collective-permute-start(bf16[64,2304]{1,0:T(8,128)(2,1)S(1)} %pad_maximum_fusion.1), channel_id=1, source_target_pairs={{0,12},{4,0},{8,4},{12,8},{1,13},{5,1},{9,5},{13,9},{2,14},{6,2},{... | collective-permute-start | bytes 884744 | tf_op jit(solution)/shard_map/ppermute | solution.py:15
  10.0 26.0 %collective-permute-start.2 = (bf16[64,2304]{1,0:T(8,128)(2,1)S(1)}, bf16[64,2304]{1,0:T(8,128)(2,1)S(1)}, u32[]{:S(2)}, u32[]{:S(2)}) collective-permute-start(bf16[64,2304]{1,0:T(8,128)(2,1)S(1)} %pad_maximum_fusion.1), channel_id=1, source_target_pairs={{0,8},{4,12},{8,0},{12,4},{1,9},{5,13},{9,1},{13,5},{2,10},{6,14},... | collective-permute-start | bytes 884744 | tf_op jit(solution)/shard_map/ppermute | solution.py:15
  42.3 20.6 %collective-permute-start.4 = (f32[256,2048]{1,0:T(8,128)S(1)}, f32[256,2048]{1,0:T(8,128)}, u32[]{:S(2)}, u32[]{:S(2)}) collective-permute-start(f32[256,2048]{1,0:T(8,128)S(1)} %fusion.1), channel_id=1, source_target_pairs={{0,1},{1,0},{2,3},{3,2},{4,5},{5,4},{6,7},{7,6},{8,9},{9,8},{10,11... | collective-permute-start | bytes 6291464 | tf_op jit(solution)/shard_map/ppermute | solution.py:15
  43.3 19.6 %collective-permute-start.24 = (bf16[32,2304]{1,0:T(8,128)(2,1)S(1)}, bf16[32,2304]{1,0:T(8,128)(2,1)S(1)}, u32[]{:S(2)}, u32[]{:S(2)}) collective-permute-start(bf16[32,2304]{1,0:T(8,128)(2,1)S(1)} %broadcast_select_fusion.9), channel_id=1, source_target_pairs={{0,1},{1,0},{2,3},{3,2},{4,5},{5,4},{6,7},{7,6},{8,9},{9,8},{10,11... | collective-permute-start | bytes 442376 | tf_op jit(solution)/shard_map/ppermute | solution.py:15
  44.6 37.2 %collective-permute-start.9 = (bf16[32,2304]{1,0:T(8,128)(2,1)}, bf16[32,2304]{1,0:T(8,128)(2,1)}, u32[]{:S(2)}, u32[]{:S(2)}) collective-permute-start(bf16[32,2304]{1,0:T(8,128)(2,1)} %broadcast_select_fusion.21), channel_id=1, source_target_pairs={{0,1},{1,0},{2,3},{3,2},{4,5},{5,4},{6,7},{7,6},{8,9},{9,8},{10,11... | collective-permute-start | bytes 442376 | tf_op jit(solution)/shard_map/ppermute | solution.py:15
  76.1 9.7 %collective-permute-start.5 = (bf16[64,1152]{1,0:T(8,128)(2,1)S(1)}, bf16[64,1152]{1,0:T(8,128)(2,1)S(1)}, u32[]{:S(2)}, u32[]{:S(2)}) collective-permute-start(bf16[64,1152]{1,0:T(8,128)(2,1)S(1)} %get-tuple-element.35), channel_id=1, source_target_pairs={{0,8},{4,12},{8,0},{12,4},{1,9},{5,13},{9,1},{13,5},{2,10},{6,14},... | collective-permute-start | bytes 442376 | tf_op jit(solution)/shard_map/ppermute | solution.py:15
  76.1 12.7 %collective-permute-start.16 = (bf16[64,1152]{1,0:T(8,128)(2,1)S(1)}, bf16[64,1152]{1,0:T(8,128)(2,1)S(1)}, u32[]{:S(2)}, u32[]{:S(2)}) collective-permute-start(bf16[64,1152]{1,0:T(8,128)(2,1)S(1)} %get-tuple-element.36), channel_id=1, source_target_pairs={{0,12},{4,0},{8,4},{12,8},{1,13},{5,1},{9,5},{13,9},{2,14},{6,2},{... | collective-permute-start | bytes 442376 | tf_op jit(solution)/shard_map/ppermute | solution.py:15
  77.8 13.3 %collective-permute-start.15 = (bf16[64,1152]{1,0:T(8,128)(2,1)S(1)}, bf16[64,1152]{1,0:T(8,128)(2,1)S(1)}, u32[]{:S(2)}, u32[]{:S(2)}) collective-permute-start(bf16[64,1152]{1,0:T(8,128)(2,1)S(1)} %get-tuple-element.37), channel_id=1, source_target_pairs={{0,4},{4,8},{8,12},{12,0},{1,5},{5,9},{9,13},{13,1},{2,6},{6,10},{... | collective-permute-start | bytes 442376 | tf_op jit(solution)/shard_map/ppermute | solution.py:15
  78.4 24.1 %collective-permute-start.8 = (bf16[256,1152]{1,0:T(8,128)(2,1)S(1)}, bf16[256,1152]{1,0:T(8,128)(2,1)S(1)}, u32[]{:S(2)}, u32[]{:S(2)}) collective-permute-start(bf16[256,1152]{1,0:T(8,128)(2,1)S(1)} %get-tuple-element.41), channel_id=1, source_target_pairs={{0,2},{1,3},{4,6},{5,7},{8,10},{9,11},{12,14},{13,15},{16,18},{17,... | collective-permute-start | bytes 1769480 | tf_op jit(solution)/shard_map/ppermute | solution.py:143
  81.9 25.2 %collective-permute-start.17 = (bf16[256,1152]{1,0:T(8,128)(2,1)S(1)}, bf16[256,1152]{1,0:T(8,128)(2,1)S(1)}, u32[]{:S(2)}, u32[]{:S(2)}) collective-permute-start(bf16[256,1152]{1,0:T(8,128)(2,1)S(1)} %get-tuple-element.42), channel_id=1, source_target_pairs={{0,2},{1,3},{4,6},{5,7},{8,10},{9,11},{12,14},{13,15},{16,18},{17,... | collective-permute-start | bytes 1769480 | tf_op jit(solution)/shard_map/ppermute | solution.py:143
  85.7 13.1 %collective-permute-start.14 = (bf16[64,1152]{1,0:T(8,128)(2,1)S(1)}, bf16[64,1152]{1,0:T(8,128)(2,1)S(1)}, u32[]{:S(2)}, u32[]{:S(2)}) collective-permute-start(bf16[64,1152]{1,0:T(8,128)(2,1)S(1)} %get-tuple-element.38), channel_id=1, source_target_pairs={{0,8},{4,12},{8,0},{12,4},{1,9},{5,13},{9,1},{13,5},{2,10},{6,14},... | collective-permute-start | bytes 442376 | tf_op jit(solution)/shard_map/ppermute | solution.py:15
  88.8 13.7 %collective-permute-start.7 = (bf16[64,1152]{1,0:T(8,128)(2,1)S(1)}, bf16[64,1152]{1,0:T(8,128)(2,1)S(1)}, u32[]{:S(2)}, u32[]{:S(2)}) collective-permute-start(bf16[64,1152]{1,0:T(8,128)(2,1)S(1)} %get-tuple-element.39), channel_id=1, source_target_pairs={{0,12},{4,0},{8,4},{12,8},{1,13},{5,1},{9,5},{13,9},{2,14},{6,2},{... | collective-permute-start | bytes 442376 | tf_op jit(solution)/shard_map/ppermute | solution.py:15
  91.1 11.5 %collective-permute-start.6 = (bf16[64,1152]{1,0:T(8,128)(2,1)S(1)}, bf16[64,1152]{1,0:T(8,128)(2,1)S(1)}, u32[]{:S(2)}, u32[]{:S(2)}) collective-permute-start(bf16[64,1152]{1,0:T(8,128)(2,1)S(1)} %get-tuple-element.40), channel_id=1, source_target_pairs={{0,4},{4,8},{8,12},{12,0},{1,5},{5,9},{9,13},{13,1},{2,6},{6,10},{... | collective-permute-start | bytes 442376 | tf_op jit(solution)/shard_map/ppermute | solution.py:15
  107.4 17.5 %collective-permute-start.10 = (bf16[64,1152]{1,0:T(8,128)(2,1)S(1)}, bf16[64,1152]{1,0:T(8,128)(2,1)S(1)}, u32[]{:S(2)}, u32[]{:S(2)}) collective-permute-start(bf16[64,1152]{1,0:T(8,128)(2,1)S(1)} %get-tuple-element.18), channel_id=1, source_target_pairs={{0,8},{4,12},{8,0},{12,4},{1,9},{5,13},{9,1},{13,5},{2,10},{6,14},... | collective-permute-start | bytes 442376 | tf_op jit(solution)/shard_map/ppermute | solution.py:15
  109.9 20.1 %collective-permute-start.18 = (bf16[64,1152]{1,0:T(8,128)(2,1)S(1)}, bf16[64,1152]{1,0:T(8,128)(2,1)S(1)}, u32[]{:S(2)}, u32[]{:S(2)}) collective-permute-start(bf16[64,1152]{1,0:T(8,128)(2,1)S(1)} %get-tuple-element.28), channel_id=1, source_target_pairs={{0,8},{4,12},{8,0},{12,4},{1,9},{5,13},{9,1},{13,5},{2,10},{6,14},... | collective-permute-start | bytes 442376 | tf_op jit(solution)/shard_map/ppermute | solution.py:15
  110.4 14.5 %collective-permute-start.11 = (bf16[64,1152]{1,0:T(8,128)(2,1)S(1)}, bf16[64,1152]{1,0:T(8,128)(2,1)S(1)}, u32[]{:S(2)}, u32[]{:S(2)}) collective-permute-start(bf16[64,1152]{1,0:T(8,128)(2,1)S(1)} %get-tuple-element.43), channel_id=1, source_target_pairs={{0,4},{4,8},{8,12},{12,0},{1,5},{5,9},{9,13},{13,1},{2,6},{6,10},{... | collective-permute-start | bytes 442376 | tf_op jit(solution)/shard_map/ppermute | solution.py:15
  112.4 12.5 %collective-permute-start.12 = (bf16[64,1152]{1,0:T(8,128)(2,1)S(1)}, bf16[64,1152]{1,0:T(8,128)(2,1)S(1)}, u32[]{:S(2)}, u32[]{:S(2)}) collective-permute-start(bf16[64,1152]{1,0:T(8,128)(2,1)S(1)} %get-tuple-element.44), channel_id=1, source_target_pairs={{0,12},{4,0},{8,4},{12,8},{1,13},{5,1},{9,5},{13,9},{2,14},{6,2},{... | collective-permute-start | bytes 442376 | tf_op jit(solution)/shard_map/ppermute | solution.py:15
  114.5 15.5 %collective-permute-start.19 = (bf16[64,1152]{1,0:T(8,128)(2,1)S(1)}, bf16[64,1152]{1,0:T(8,128)(2,1)S(1)}, u32[]{:S(2)}, u32[]{:S(2)}) collective-permute-start(bf16[64,1152]{1,0:T(8,128)(2,1)S(1)} %get-tuple-element.45), channel_id=1, source_target_pairs={{0,4},{4,8},{8,12},{12,0},{1,5},{5,9},{9,13},{13,1},{2,6},{6,10},{... | collective-permute-start | bytes 442376 | tf_op jit(solution)/shard_map/ppermute | solution.py:15
  125.1 11.2 %collective-permute-start.25 = (bf16[64,1152]{1,0:T(8,128)(2,1)S(1)}, bf16[64,1152]{1,0:T(8,128)(2,1)S(1)}, u32[]{:S(2)}, u32[]{:S(2)}) collective-permute-start(bf16[64,1152]{1,0:T(8,128)(2,1)S(1)} %get-tuple-element.31), channel_id=1, source_target_pairs={{2,0},{3,1},{6,4},{7,5},{10,8},{11,9},{14,12},{15,13},{18,16},{19,... | collective-permute-start | bytes 442376 | tf_op jit(solution)/shard_map/ppermute | solution.py:162
  126.4 21.9 %collective-permute-start.13 = (bf16[64,1152]{1,0:T(8,128)(2,1)S(1)}, bf16[64,1152]{1,0:T(8,128)(2,1)S(1)}, u32[]{:S(2)}, u32[]{:S(2)}) collective-permute-start(bf16[64,1152]{1,0:T(8,128)(2,1)S(1)} %get-tuple-element.32), channel_id=1, source_target_pairs={{0,2},{2,0},{1,3},{3,1},{4,6},{6,4},{5,7},{7,5},{8,10},{10,8},{9,1... | collective-permute-start | bytes 442376 | tf_op jit(solution)/shard_map/ppermute | solution.py:15
  132.2 11.9 %collective-permute-start.29 = (bf16[64,1152]{1,0:T(8,128)(2,1)S(1)}, bf16[64,1152]{1,0:T(8,128)(2,1)S(1)}, u32[]{:S(2)}, u32[]{:S(2)}) collective-permute-start(bf16[64,1152]{1,0:T(8,128)(2,1)S(1)} %get-tuple-element.33), channel_id=1, source_target_pairs={{2,0},{3,1},{6,4},{7,5},{10,8},{11,9},{14,12},{15,13},{18,16},{19,... | collective-permute-start | bytes 442376 | tf_op jit(solution)/shard_map/ppermute | solution.py:162
  133.5 14.8 %collective-permute-start.21 = (bf16[64,1152]{1,0:T(8,128)(2,1)S(1)}, bf16[64,1152]{1,0:T(8,128)(2,1)S(1)}, u32[]{:S(2)}, u32[]{:S(2)}) collective-permute-start(bf16[64,1152]{1,0:T(8,128)(2,1)S(1)} %get-tuple-element.34), channel_id=1, source_target_pairs={{0,2},{2,0},{1,3},{3,1},{4,6},{6,4},{5,7},{7,5},{8,10},{10,8},{9,1... | collective-permute-start | bytes 442376 | tf_op jit(solution)/shard_map/ppermute | solution.py:15
  136.3 16.2 %collective-permute-start.28 = (bf16[64,1152]{1,0:T(8,128)(2,1)S(1)}, bf16[64,1152]{1,0:T(8,128)(2,1)S(1)}, u32[]{:S(2)}, u32[]{:S(2)}) collective-permute-start(bf16[64,1152]{1,0:T(8,128)(2,1)S(1)} %broadcast_select_fusion.2), channel_id=1, source_target_pairs={{0,12},{4,0},{8,4},{12,8},{1,13},{5,1},{9,5},{13,9},{2,14},{6,2},{... | collective-permute-start | bytes 442376 | tf_op jit(solution)/shard_map/ppermute | solution.py:15
  140.8 23.7 %collective-permute-start.27 = (bf16[64,1152]{1,0:T(8,128)(2,1)S(1)}, bf16[64,1152]{1,0:T(8,128)(2,1)S(1)}, u32[]{:S(2)}, u32[]{:S(2)}) collective-permute-start(bf16[64,1152]{1,0:T(8,128)(2,1)S(1)} %broadcast_select_fusion.2), channel_id=1, source_target_pairs={{0,8},{4,12},{8,0},{12,4},{1,9},{5,13},{9,1},{13,5},{2,10},{6,14},... | collective-permute-start | bytes 442376 | tf_op jit(solution)/shard_map/ppermute | solution.py:15
  144.1 20.4 %collective-permute-start.26 = (bf16[64,1152]{1,0:T(8,128)(2,1)S(1)}, bf16[64,1152]{1,0:T(8,128)(2,1)S(1)}, u32[]{:S(2)}, u32[]{:S(2)}) collective-permute-start(bf16[64,1152]{1,0:T(8,128)(2,1)S(1)} %broadcast_select_fusion.2), channel_id=1, source_target_pairs={{0,4},{4,8},{8,12},{12,0},{1,5},{5,9},{9,13},{13,1},{2,6},{6,10},{... | collective-permute-start | bytes 442376 | tf_op jit(solution)/shard_map/ppermute | solution.py:15
  148.3 16.8 %collective-permute-start.32 = (bf16[64,1152]{1,0:T(8,128)(2,1)S(1)}, bf16[64,1152]{1,0:T(8,128)(2,1)S(1)}, u32[]{:S(2)}, u32[]{:S(2)}) collective-permute-start(bf16[64,1152]{1,0:T(8,128)(2,1)S(1)} %broadcast_select_fusion.1), channel_id=1, source_target_pairs={{0,12},{4,0},{8,4},{12,8},{1,13},{5,1},{9,5},{13,9},{2,14},{6,2},{... | collective-permute-start | bytes 442376 | tf_op jit(solution)/shard_map/ppermute | solution.py:15
  148.4 20.6 %collective-permute-start.31 = (bf16[64,1152]{1,0:T(8,128)(2,1)S(1)}, bf16[64,1152]{1,0:T(8,128)(2,1)S(1)}, u32[]{:S(2)}, u32[]{:S(2)}) collective-permute-start(bf16[64,1152]{1,0:T(8,128)(2,1)S(1)} %broadcast_select_fusion.1), channel_id=1, source_target_pairs={{0,8},{4,12},{8,0},{12,4},{1,9},{5,13},{9,1},{13,5},{2,10},{6,14},... | collective-permute-start | bytes 442376 | tf_op jit(solution)/shard_map/ppermute | solution.py:15
  152.5 16.5 %collective-permute-start.30 = (bf16[64,1152]{1,0:T(8,128)(2,1)S(1)}, bf16[64,1152]{1,0:T(8,128)(2,1)S(1)}, u32[]{:S(2)}, u32[]{:S(2)}) collective-permute-start(bf16[64,1152]{1,0:T(8,128)(2,1)S(1)} %broadcast_select_fusion.1), channel_id=1, source_target_pairs={{0,4},{4,8},{8,12},{12,0},{1,5},{5,9},{9,13},{13,1},{2,6},{6,10},{... | collective-permute-start | bytes 442376 | tf_op jit(solution)/shard_map/ppermute | solution.py:15
  164.5 22.0 %collective-permute-start.23 = (bf16[32,2304]{1,0:T(8,128)(2,1)}, bf16[32,2304]{1,0:T(8,128)(2,1)}, u32[]{:S(2)}, u32[]{:S(2)}) collective-permute-start(bf16[32,2304]{1,0:T(8,128)(2,1)} %broadcast_select_fusion.13), channel_id=1, source_target_pairs={{0,1},{1,0},{2,3},{3,2},{4,5},{5,4},{6,7},{7,6},{8,9},{9,8},{10,11... | collective-permute-start | bytes 442376 | tf_op jit(solution)/shard_map/ppermute | solution.py:15
  164.5 23.1 %collective-permute-start.22 = (bf16[32,2304]{1,0:T(8,128)(2,1)}, bf16[32,2304]{1,0:T(8,128)(2,1)}, u32[]{:S(2)}, u32[]{:S(2)}) collective-permute-start(bf16[32,2304]{1,0:T(8,128)(2,1)} %broadcast_select_fusion.17), channel_id=1, source_target_pairs={{0,1},{1,0},{2,3},{3,2},{4,5},{5,4},{6,7},{7,6},{8,9},{9,8},{10,11... | collective-permute-start | bytes 442376 | tf_op jit(solution)/shard_map/ppermute | solution.py:15
  186.5 19.6 %collective-permute-start.33 = (f32[256,2048]{1,0:T(8,128)}, f32[256,2048]{1,0:T(8,128)S(1)}, u32[]{:S(2)}, u32[]{:S(2)}) collective-permute-start(f32[256,2048]{1,0:T(8,128)} %fusion.8), channel_id=1, source_target_pairs={{0,1},{1,0},{2,3},{3,2},{4,5},{5,4},{6,7},{7,6},{8,9},{9,8},{10,11... | collective-permute-start | bytes 6291464 | tf_op jit(solution)/shard_map/ppermute | solution.py:15
  (20 other events, 300.3 us)

commit v2 on v1

v2 whole, which is shorter than its diff:
```python
import functools

import jax
import jax.numpy as jnp
from jax import lax
from jax.experimental import pallas as pl
from jax.experimental.pallas import tpu as pltpu
from jax.sharding import PartitionSpec as P

CHUNKS = 2


def shifted(block, axis, distance):
    count = lax.axis_size(axis)
    return lax.ppermute(block, axis, [(i, (i + distance) % count) for i in range(count)])


def dot_last(left, right):
    return lax.dot_general(
        left, right, (((1,), (1,)), ((), ())), preferred_element_type=jnp.float32
    )


def dot_first(left, right):
    return lax.dot_general(
        left, right, (((0,), (0,)), ((), ())), preferred_element_type=jnp.float32
    )


def shift_order(count):
    return sorted(range(1, count), key=lambda k: -min(k, count - k))


def vmem_params():
    return pltpu.CompilerParams(vmem_limit_bytes=24 * 1024 * 1024)


def encoder_kernel(inputs_ref, weight_ref, out_ref):
    count, half = weight_ref.shape
    rows = inputs_ref.shape[0]
    block = min(256, count)

    def product(weight_block, out_block):
        out_block[...] = dot_last(inputs_ref[...], weight_block[...])

    pltpu.emit_pipeline(
        product,
        grid=(count // block,),
        in_specs=[pl.BlockSpec((block, half), lambda i: (i, 0))],
        out_specs=[pl.BlockSpec((rows, block), lambda i: (0, i))],
    )(weight_ref, out_ref)


def encoder_call(inputs, weight):
    rows, count = inputs.shape[0], weight.shape[0]
    return pl.pallas_call(
        encoder_kernel,
        in_specs=[
            pl.BlockSpec(memory_space=pltpu.VMEM),
            pl.BlockSpec(memory_space=pltpu.HBM),
        ],
        out_specs=pl.BlockSpec(memory_space=pl.ANY),
        out_shape=jax.ShapeDtypeStruct((rows, count), jnp.float32),
        compiler_params=vmem_params(),
    )(inputs, weight)


def pair_kernel(first_ref, second_ref, out_ref):
    out_ref[:, 0, :] = first_ref[...]
    out_ref[:, 1, :] = second_ref[...]


def pair_call(first, second):
    rows, width = first.shape
    return pl.pallas_call(
        pair_kernel,
        out_shape=jax.ShapeDtypeStruct((rows, 2, width), first.dtype),
        compiler_params=vmem_params(),
    )(first, second)


def dec_grad_kernel(scale, features_ref, own_ref, next_ref, *rest):
    out_ref = rest[-1]
    features = features_ref[...]
    own = dot_first(features, own_ref[...])
    out_ref[:, 0, :] = (scale * own).astype(out_ref.dtype)
    following = dot_first(features, next_ref[...])
    out_ref[:, 1, :] = (scale * following).astype(out_ref.dtype)


def dec_grad_call(features, own, following, scale, chunk, chunks, before=None):
    rows, count = features.shape
    piece = own.shape[1]
    block = min(512, count)
    specs = [
        pl.BlockSpec((rows, block), lambda i: (0, i)),
        pl.BlockSpec((rows, piece), lambda i: (0, 0)),
        pl.BlockSpec((rows, piece), lambda i: (0, 0)),
    ]
    operands = [features, own, following]
    aliases = {}
    if before is not None:
        specs.append(pl.BlockSpec(memory_space=pl.ANY))
        operands.append(before)
        aliases = {3: 0}
    return pl.pallas_call(
        functools.partial(dec_grad_kernel, scale),
        grid=(count // block,),
        in_specs=specs,
        out_specs=pl.BlockSpec((block, 2, piece), lambda i: (i, 0, chunk)),
        out_shape=jax.ShapeDtypeStruct((count, 2, piece * chunks), jnp.bfloat16),
        input_output_aliases=aliases,
        cost_estimate=pl.CostEstimate(
            flops=4 * rows * count * piece,
            bytes_accessed=4 * count * piece + 4 * rows * piece + 2 * rows * count,
            transcendentals=0,
        ),
        compiler_params=vmem_params(),
    )(*operands)


def enc_grad_kernel(scale, mine_ref, other_ref, live_ref, inputs_ref, enc_ref, bias_ref):
    grad = (mine_ref[...].astype(jnp.float32) + other_ref[...].astype(jnp.float32)) * scale
    grad = jnp.where(live_ref[...].astype(jnp.float32) > 0, grad, 0.0).astype(jnp.bfloat16)
    bias_ref[...] = jnp.sum(grad.astype(jnp.float32), axis=0, keepdims=True)
    enc_ref[...] = dot_first(grad, inputs_ref[...]).astype(enc_ref.dtype)


def enc_grad_call(mine, other, live, inputs, scale):
    rows, count = mine.shape
    half = inputs.shape[1]
    block = min(512, count)
    columns = pl.BlockSpec((rows, block), lambda i: (0, i))
    return pl.pallas_call(
        functools.partial(enc_grad_kernel, scale),
        grid=(count // block,),
        in_specs=[columns, columns, columns, pl.BlockSpec((rows, half), lambda i: (0, 0))],
        out_specs=[
            pl.BlockSpec((block, half), lambda i: (i, 0)),
            pl.BlockSpec((1, block), lambda i: (0, i)),
        ],
        out_shape=[
            jax.ShapeDtypeStruct((count, half), jnp.bfloat16),
            jax.ShapeDtypeStruct((1, count), jnp.float32),
        ],
        cost_estimate=pl.CostEstimate(
            flops=2 * rows * count * half,
            bytes_accessed=2 * count * half + 6 * rows * count + 2 * rows * half,
            transcendentals=0,
        ),
        compiler_params=vmem_params(),
    )(mine, other, live, inputs)


def on_device(resid_buf, shuffle, mlp_out, enc_weight, dec_weight, enc_bias, dec_bias):
    f32, bf16 = jnp.float32, jnp.bfloat16
    feat_count = lax.axis_size("feat")
    layer_count = lax.axis_size("layer")
    layers = resid_buf.shape[1]
    sub_blocks = layer_count // layers
    feat_pos = lax.axis_index("feat")
    source = lax.axis_index("layer") // sub_blocks
    row_pos = lax.axis_index("row")
    first_core = row_pos == 0
    leading = source + 1 < layers
    rows_each, _, width = resid_buf.shape
    half = enc_weight.shape[2]
    piece = half // CHUNKS
    block_rows = rows_each * lax.axis_size("row")
    total_rows = block_rows * feat_count
    loss_scale = float(total_rows) ** (-0.5)
    order = shift_order(feat_count)

    def to_half(block):
        left, right = block[:, :half], block[:, half:]
        mine = jnp.where(first_core, left, right)
        got = shifted(jnp.where(first_core, right, left), "row", 1)
        return jnp.concatenate(
            [jnp.where(first_core, mine, got), jnp.where(first_core, got, mine)], axis=0
        )

    def from_half(block):
        upper, lower = block[:rows_each], block[rows_each:]
        mine = jnp.where(first_core, upper, lower)
        got = shifted(jnp.where(first_core, lower, upper), "row", 1)
        return jnp.concatenate(
            [jnp.where(first_core, mine, got), jnp.where(first_core, got, mine)], axis=1
        )

    def section_total(block):
        total = block
        for step in range(1, sub_blocks):
            pairs = [
                (i, (i // sub_blocks) * sub_blocks + (i + step) % sub_blocks)
                for i in range(layer_count)
            ]
            total = total + lax.ppermute(block, "layer", pairs)
        return total

    own_layer = jnp.where(leading, resid_buf[:, 0], resid_buf[:, layers - 1])
    own_block = to_half(own_layer)
    arrived = {0: own_block}
    for k in order:
        arrived[k] = shifted(own_block, "feat", k)
    own_mlp, sent_block = lax.optimization_barrier((mlp_out, own_block))
    mlp_half = [to_half(own_mlp[:, t]) for t in range(layers)]
    mlp_half, dec_weight = lax.optimization_barrier((mlp_half, dec_weight))
    slots = jnp.swapaxes(dec_weight[0], 0, 1)
    buffered = jnp.concatenate([arrived[k] for k in range(feat_count)], axis=0)
    buffered, slots, enc_weight = lax.optimization_barrier((buffered, slots, enc_weight))
    blocks = shuffle.reshape(feat_count, block_rows)
    relative = (feat_pos - jnp.arange(feat_count)) % feat_count
    wanted = jnp.take(blocks, relative, axis=0).reshape(total_rows)
    place = ((feat_pos - wanted // block_rows) % feat_count) * block_rows + wanted % block_rows
    picks = (place[:, None] == jnp.arange(total_rows)[None]).astype(bf16)
    inputs = jnp.dot(picks, buffered, preferred_element_type=f32).astype(bf16)

    bias_half = lax.dynamic_slice_in_dim(dec_bias, row_pos * half, half, axis=1)

    partial_pre = encoder_call(inputs, enc_weight[0])
    pre = partial_pre + shifted(partial_pre, "row", 1) + enc_bias
    features, live = lax.optimization_barrier(
        (jnp.maximum(pre, 0.0).astype(bf16), (pre > 0).astype(bf16))
    )

    next_part = jnp.dot(features, slots[1], preferred_element_type=f32).astype(bf16)
    own_part = jnp.dot(features, slots[0], preferred_element_type=f32)
    forward = [(i, i + sub_blocks) for i in range(layer_count - sub_blocks)]
    backward = [(j, i) for i, j in forward]
    low, high = slice(0, piece), slice(piece, half)

    def rows_of(array, k):
        j = (feat_count - k) % feat_count
        return array[j * block_rows : (j + 1) * block_rows]

    def move(pick):
        arriving = [None] * feat_count
        for k in order:
            arriving[k] = shifted(pick(k), "feat", k)
        return arriving

    def reduced(partial, arriving):
        total = rows_of(partial, 0).astype(f32)
        for k in order:
            total = total + arriving[k].astype(f32)
        return section_total(total)

    def joined(block, arriving):
        return jnp.concatenate([block] + arriving[1:], axis=0)

    def error_of(recon, t, cols):
        return (recon - mlp_half[t][:, cols].astype(f32)).astype(bf16)

    last = layers - 1
    carried = lax.ppermute(next_part[:, high], "layer", forward)
    low_part = jnp.where(leading, next_part[:, low].astype(f32), own_part[:, low])
    low_sent = low_part.astype(bf16)
    low_moved = move(lambda k: rows_of(low_sent, k))
    near = order[-1]
    low_moved[near], carried = lax.optimization_barrier((low_moved[near], carried))
    second_part = jnp.where(leading, own_part[:, low], own_part[:, high] + carried.astype(f32))
    second_sent = second_part.astype(bf16)
    second_moved = move(lambda k: rows_of(second_sent, k))
    low_sum = reduced(low_part, low_moved)
    low_total = low_sum + shifted(low_sum, "layer", sub_blocks)
    recon_last_low = low_total + bias_half[last, low]
    last_low = error_of(recon_last_low, last, low)
    second_sum = reduced(second_part, second_moved)
    recon_second = second_sum + jnp.where(leading, bias_half[0, low], bias_half[last, high])
    second_mlp = jnp.where(leading, mlp_half[0][:, low], mlp_half[last][:, high])
    second_error = (recon_second - second_mlp.astype(f32)).astype(bf16)
    high_sent = own_part[:, high].astype(bf16)
    third_moved = move(lambda k: jnp.where(leading, rows_of(high_sent, k), second_error))
    third_moved[near], fourth = lax.optimization_barrier((third_moved[near], last_low))
    fourth_moved = move(lambda k: fourth)
    last_high_all = lax.ppermute(joined(second_error, third_moved), "layer", backward)
    third_high_all = joined(second_error, third_moved)
    third_sum = reduced(own_part[:, high], third_moved)
    recon_third = third_sum + bias_half[0, high]
    third_error = error_of(recon_third, 0, high)
    recon_low, recon_high = recon_second.astype(bf16), recon_third.astype(bf16)
    other_half = shifted(recon_low, "layer", sub_blocks)
    lead_high = lax.ppermute(recon_high, "layer", forward)
    fourth_moved[near], other_half, fifth = lax.optimization_barrier(
        (fourth_moved[near], other_half, second_error)
    )
    fifth_moved = move(lambda k: fifth)
    fourth_all = joined(fourth, fourth_moved)
    first_rows = jnp.concatenate(
        [jnp.where(leading, recon_low, other_half), jnp.where(leading, recon_high, lead_high)], axis=1
    )
    last_rows = jnp.concatenate(
        [recon_last_low.astype(bf16), jnp.where(leading, other_half, recon_low)], axis=1
    )
    output = pair_call(from_half(first_rows), from_half(last_rows))
    empty = jnp.zeros((total_rows, piece), bf16)
    next_low = jnp.where(leading, fourth_all, empty)
    next_high = jnp.where(leading, last_high_all, empty)
    next_terms = dot_last(jnp.concatenate([next_low, next_high], axis=1), slots[1])
    fifth_moved[near], next_terms, output, live, sixth = lax.optimization_barrier(
        (fifth_moved[near], next_terms, output, live, third_error)
    )
    sixth_moved = move(lambda k: sixth)

    own_low = jnp.where(leading, joined(second_error, fifth_moved), fourth_all)
    sixth_moved[near], own_low = lax.optimization_barrier((sixth_moved[near], own_low))
    dec_low = dec_grad_call(features, own_low, next_low, loss_scale, 0, CHUNKS)
    early = next_terms
    sixth_moved, dec_low, early = lax.optimization_barrier((sixth_moved[1:], dec_low, early))
    own_high = jnp.where(leading, joined(third_error, [None] + sixth_moved), third_high_all)
    terms = (early + dot_last(jnp.concatenate([own_low, own_high], axis=1), slots[0])).astype(bf16)
    other_terms = shifted(terms, "row", 1)
    dec_grad = dec_grad_call(features, own_high, next_high, loss_scale, 1, CHUNKS, dec_low)
    enc_grad, bias_grad = enc_grad_call(terms, other_terms, live, inputs, loss_scale)
    return output, enc_grad[None], dec_grad[None], bias_grad


def solution(mesh):
    return jax.shard_map(
        on_device,
        mesh=mesh,
        in_specs=(
            P(("groups", "feat", "row"), None, None),
            P("groups"),
            P(("groups", "feat", "row"), None, None),
            P("layer", "feat", "row"),
            P("layer", "feat", None, "row"),
            P("layer", "feat"),
            P(),
        ),
        out_specs=(
            P(("groups", "feat", "row"), None, None),
            P(("groups", "layer"), "feat", "row"),
            P(("groups", "layer"), "feat", None, "row"),
            P(("groups", "layer"), "feat"),
        ),
        check_vma=False,
    )
```

time: 215 us -> 171 us (0.80); the launches traced: 214 us -> 168 us
  waiting for transfers between devices: 65.7 us -> 38.2 us
  Pallas kernels: 15.8 us -> 29.7 us
  matrix products: 29.8 us -> 16.4 us
  other arithmetic: 20.8 us -> 8.91 us
  local copies, waits for them, and re-layouts: 24.7 us -> 18.7 us
    ppermute x30, waiting for transfers between devices: 61.1 us -> 32 us  [shifted(): lax.ppermute(block, axis, [(i, (i + distance) % count) for i in range(cou...]
    unnamed x42 -> x29, local copies, waits for them, and re-layouts: 20.5 us -> 0.15 us
    pallas_call x0 -> x3, Pallas kernels: none -> 12.8 us  [the longest x1 5.91 us: encoder_call(): pl.pallas_call(encoder_kernel, in_specs=[pl.BlockSpec(memory_space=pltpu....]
    optimization_barrier x0 -> x2, local copies, waits for them, and re-layouts: none -> 12.3 us  [the longest x1 12.3 us: on_device(): mlp_half, dec_weight = lax.optimization_barrier((mlp_half, dec_weight))]
    dot_general x3 -> x2, matrix products: 14.5 us -> 5.41 us  [the longest x1 2.71 us: on_device(): own_part = jnp.dot(features, slots[0], preferred_element_type=f32)]
    select_n x9 -> x8, other arithmetic: 8.86 us -> 0.64 us  [the longest x2 0.18 us: on_device(): jnp.where(leading, rows_of(high_sent, k), second_error)]
    ppermute x30, starting transfers between devices: 49.1 us -> 42.4 us  [shifted(): lax.ppermute(block, axis, [(i, (i + distance) % count) for i in range(cou...]
    ppermute x4 -> x3, starting transfers between devices: 7.35 us -> 12.3 us  [the longest x1 6.67 us: on_device(): lead_high = lax.ppermute(recon_high, 'layer', forward)]
  transfers between devices with their start and end apart: 34 -> 33, of which waited for: 13 -> 16; matrix products, arithmetic and copies ran while one was open for 27% -> 17% of each run, Pallas kernels for 7% -> 11%
where the time goes in v2:
time: 171 us; the launch traced here: 168 us
  starting transfers between devices  54.7 us (32%)
  waiting for transfers between devices  38.2 us (22%)
  Pallas kernels  29.7 us (17%)
  local copies, waits for them, and re-layouts  18.7 us (11%)
  matrix products  16.4 us (10%)
  other arithmetic  8.91 us (5%)
    ppermute x30, starting transfers between devices, shifted(): lax.ppermute(block, axis, [(i, (i + distance) % count) for i in range(cou...  42.4 us
    ppermute x30, waiting for transfers between devices, shifted(): lax.ppermute(block, axis, [(i, (i + distance) % count) for i in range(cou...  32 us
    pallas_call x2, Pallas kernels, dec_grad_call(): pl.pallas_call(functools.partial(dec_grad_kernel, scale), grid=(count //...  16.9 us
    optimization_barrier x1, local copies, waits for them, and re-layouts, on_device(): mlp_half, dec_weight = lax.optimization_barrier((mlp_half, dec_weight))  12.3 us
    dot_general x2, matrix products, dot_last(): lax.dot_general(left, right, (((1,), (1,)), ((), ())), preferred_element_...  10.4 us
    ppermute x1, starting transfers between devices, on_device(): lead_high = lax.ppermute(recon_high, 'layer', forward)  6.67 us
    pallas_call x1, Pallas kernels, encoder_call(): pl.pallas_call(encoder_kernel, in_specs=[pl.BlockSpec(memory_space=pltpu....  5.91 us
    pallas_call x1, Pallas kernels, enc_grad_call(): pl.pallas_call(functools.partial(enc_grad_kernel, scale), grid=(count //...  5.81 us
  transfers between devices with their start and end apart: 33, of which 16 were waited for; matrix products, arithmetic and copies ran while one was open for 17% of the time, Pallas kernels for 11%

profile of v2, /device:TPU:0, one launch (start us, length us, event | category | flops | bytes accessed | tf_op | source)
XLA Modules:
  0.0 167.9 jit_solution(6311734198017690979)
XLA Ops:
  0.6 2.4 %fusion.54 = (bf16[32,1,4608]{2,1,0:T(2,128)(2,1)S(1)}, bf16[32,1,4608]{2,1,0:T(2,128)(2,1)S(1)}) fusion(bf16[32,2,4608]{2,1,0:T(2,128)(2,1)} %param.7), kind=kLoop, calls=%fused_computation.146 | loop fusion | bytes 1179648 | tf_op jit(solution)/shard_map/slice | solution.py:200
  4.8 5.0 %collective-permute-start.3 = (bf16[64,2304]{1,0:T(8,128)(2,1)S(1)}, bf16[64,2304]{1,0:T(8,128)(2,1)S(1)}, u32[]{:S(2)}, u32[]{:S(2)}) collective-permute-start(bf16[64,2304]{1,0:T(8,128)(2,1)S(1)} %pad_maximum_fusion.2), channel_id=1, source_target_pairs={{0,12},{4,0},{8,4},{12,8},{1,13},{5,1},{9,5},{13,9},{2,14},{6,2},{... | collective-permute-start | bytes 884744 | tf_op jit(solution)/shard_map/ppermute | solution.py:15
  13.6 12.3 %copy.28 = bf16[1,2048,2,2304]{3,1,2,0:T(8,128)(2,1)S(1)} copy(bf16[1,2048,2,2304]{3,2,1,0:T(2,128)(2,1)} %param.11) | data formatting | bytes 37748736 | tf_op jit(solution)/shard_map/optimization_barrier | solution.py:207
  25.9 4.2 %collective-permute-done.1 = bf16[64,2304]{1,0:T(8,128)(2,1)S(1)} collective-permute-done((bf16[64,2304]{1,0:T(8,128)(2,1)S(1)}, bf16[64,2304]{1,0:T(8,128)(2,1)S(1)}, u32[]{:S(2)}, u32[]{:S(2)}) %collective-permute-start.1) | collective-permute-done | bytes 294944 | tf_op jit(solution)/shard_map/ppermute | solution.py:15
  30.1 5.2 %collective-permute-done.2 = bf16[64,2304]{1,0:T(8,128)(2,1)S(1)} collective-permute-done((bf16[64,2304]{1,0:T(8,128)(2,1)S(1)}, bf16[64,2304]{1,0:T(8,128)(2,1)S(1)}, u32[]{:S(2)}, u32[]{:S(2)}) %collective-permute-start.2) | collective-permute-done | bytes 294944 | tf_op jit(solution)/shard_map/ppermute | solution.py:15
  35.9 5.9 %shard_map.102 = f32[256,2048]{1,0:T(8,128)S(1)} custom-call(bf16[256,2304]{1,0:T(8,128)(2,1)S(1)} %convolution_convert_fusion.inputs_ref, bf16[2048,2304]{1,0:T(8,128)(2,1)S(1)} %bitcast.34), custom_call_target="tpu_custom_call" | custom-call | tf_op jit(solution)/shard_map/pallas_call | solution.py:56
  41.9 4.1 %collective-permute-done.6 = f32[256,2048]{1,0:T(8,128)S(1)} collective-permute-done((f32[256,2048]{1,0:T(8,128)S(1)}, f32[256,2048]{1,0:T(8,128)S(1)}, u32[]{:S(2)}, u32[]{:S(2)}) %collective-permute-start.6) | collective-permute-done | bytes 2097184 | tf_op jit(solution)/shard_map/ppermute | solution.py:15
  46.9 2.7 %fusion.12 = bf16[256,2304]{1,0:T(8,128)(2,1)S(1)} fusion(bf16[256,2048]{1,0:T(8,128)(2,1)S(1)} %maximum_convert_fusion.features_ref, bf16[2,2048,2304]{2,1,0:T(8,128)(2,1)S(1)} %bitcast.36), kind=kOutput, calls=%fused_computation.14 | convolution fusion | flops 2416508928 | bytes 11665408 | tf_op jit(solution)/shard_map/dot_general | solution.py:226
  49.6 2.7 %fusion.6 = f32[256,2304]{1,0:T(8,128)S(1)} fusion(bf16[256,2048]{1,0:T(8,128)(2,1)S(1)} %maximum_convert_fusion.features_ref, bf16[2,2048,2304]{2,1,0:T(8,128)(2,1)S(1)} %bitcast.37), kind=kOutput, calls=%fused_computation.8 | convolution fusion | flops 2415919104 | bytes 12845056 | tf_op jit(solution)/shard_map/dot_general | solution.py:227
  53.3 4.3 %collective-permute-start.8 = (bf16[256,1152]{1,0:T(8,128)(2,1)}, bf16[256,1152]{1,0:T(8,128)(2,1)}, u32[]{:S(2)}, u32[]{:S(2)}) collective-permute-start(bf16[256,1152]{1,0:T(8,128)(2,1)} %slice.181), channel_id=1, source_target_pairs={{0,2},{1,3},{4,6},{5,7},{8,10},{9,11},{12,14},{13,15},{16,18},{17,... | collective-permute-start | bytes 1769480 | tf_op jit(solution)/shard_map/ppermute | solution.py:255
  61.0 2.9 %collective-permute-start.13 = (bf16[64,1152]{1,0:T(8,128)(2,1)S(1)}, bf16[64,1152]{1,0:T(8,128)(2,1)S(1)}, u32[]{:S(2)}, u32[]{:S(2)}) collective-permute-start(bf16[64,1152]{1,0:T(8,128)(2,1)S(1)} %copy-done.5), channel_id=1, source_target_pairs={{0,8},{4,12},{8,0},{12,4},{1,9},{5,13},{9,1},{13,5},{2,10},{6,14},... | collective-permute-start | bytes 442376 | tf_op jit(solution)/shard_map/ppermute | solution.py:15
  63.9 2.0 %collective-permute-start.14 = (bf16[64,1152]{1,0:T(8,128)(2,1)S(1)}, bf16[64,1152]{1,0:T(8,128)(2,1)S(1)}, u32[]{:S(2)}, u32[]{:S(2)}) collective-permute-start(bf16[64,1152]{1,0:T(8,128)(2,1)S(1)} %get-tuple-element.84), channel_id=1, source_target_pairs={{0,4},{4,8},{8,12},{12,0},{1,5},{5,9},{9,13},{13,1},{2,6},{6,10},{... | collective-permute-start | bytes 442376 | tf_op jit(solution)/shard_map/ppermute | solution.py:15
  66.0 4.0 %collective-permute-done.8 = bf16[256,1152]{1,0:T(8,128)(2,1)} collective-permute-done((bf16[256,1152]{1,0:T(8,128)(2,1)}, bf16[256,1152]{1,0:T(8,128)(2,1)}, u32[]{:S(2)}, u32[]{:S(2)}) %collective-permute-start.8) | collective-permute-done | bytes 589856 | tf_op jit(solution)/shard_map/ppermute | solution.py:255
  70.0 2.0 %fusion.50 = (bf16[256,1152]{1,0:T(8,128)(2,1)S(1)}, f32[256,1152]{1,0:T(8,128)S(1)}) fusion(bf16[256,1152]{1,0:T(8,128)(2,1)} %collective-permute-done.8, f32[256,2304]{1,0:T(8,128)} %copy-done.1, pred[]{:T(512)S(6)} %lt.39), kind=kLoop, calls=%fused_computation.142 | loop fusion | flops 1179648 | bytes 4718593 | tf_op jit(solution)/shard_map/convert_element_type | solution.py:262
  72.0 2.9 %collective-permute-start.9 = (bf16[64,1152]{1,0:T(8,128)(2,1)S(1)}, bf16[64,1152]{1,0:T(8,128)(2,1)S(1)}, u32[]{:S(2)}, u32[]{:S(2)}) collective-permute-start(bf16[64,1152]{1,0:T(8,128)(2,1)S(1)} %get-tuple-element.86), channel_id=1, source_target_pairs={{0,8},{4,12},{8,0},{12,4},{1,9},{5,13},{9,1},{13,5},{2,10},{6,14},... | collective-permute-start | bytes 442376 | tf_op jit(solution)/shard_map/ppermute | solution.py:15
  77.0 2.7 %collective-permute-done.13 = bf16[64,1152]{1,0:T(8,128)(2,1)S(1)} collective-permute-done((bf16[64,1152]{1,0:T(8,128)(2,1)S(1)}, bf16[64,1152]{1,0:T(8,128)(2,1)S(1)}, u32[]{:S(2)}, u32[]{:S(2)}) %collective-permute-start.13) | collective-permute-done | bytes 147488 | tf_op jit(solution)/shard_map/ppermute | solution.py:15
  80.8 5.4 %collective-permute-done.9 = bf16[64,1152]{1,0:T(8,128)(2,1)S(1)} collective-permute-done((bf16[64,1152]{1,0:T(8,128)(2,1)S(1)}, bf16[64,1152]{1,0:T(8,128)(2,1)S(1)}, u32[]{:S(2)}, u32[]{:S(2)}) %collective-permute-start.9) | collective-permute-done | bytes 147488 | tf_op jit(solution)/shard_map/ppermute | solution.py:15
  86.9 2.8 %collective-permute-start.22 = (bf16[64,1152]{1,0:T(8,128)(2,1)S(1)}, bf16[64,1152]{1,0:T(8,128)(2,1)S(1)}, u32[]{:S(2)}, u32[]{:S(2)}) collective-permute-start(bf16[64,1152]{1,0:T(8,128)(2,1)S(1)} %get-tuple-element.79), channel_id=1, source_target_pairs={{0,8},{4,12},{8,0},{12,4},{1,9},{5,13},{9,1},{13,5},{2,10},{6,14},... | collective-permute-start | bytes 442376 | tf_op jit(solution)/shard_map/ppermute | solution.py:15
  89.7 2.1 %collective-permute-start.12 = (bf16[64,1152]{1,0:T(8,128)(2,1)S(1)}, bf16[64,1152]{1,0:T(8,128)(2,1)S(1)}, u32[]{:S(2)}, u32[]{:S(2)}) collective-permute-start(bf16[64,1152]{1,0:T(8,128)(2,1)S(1)} %get-tuple-element.80), channel_id=1, source_target_pairs={{0,12},{4,0},{8,4},{12,8},{1,13},{5,1},{9,5},{13,9},{2,14},{6,2},{... | collective-permute-start | bytes 442376 | tf_op jit(solution)/shard_map/ppermute | solution.py:15
  91.9 1.7 %collective-permute-start.17 = (bf16[64,1152]{1,0:T(8,128)(2,1)S(1)}, bf16[64,1152]{1,0:T(8,128)(2,1)S(1)}, u32[]{:S(2)}, u32[]{:S(2)}) collective-permute-start(bf16[64,1152]{1,0:T(8,128)(2,1)S(1)} %fusion.48), channel_id=1, source_target_pairs={{0,2},{2,0},{1,3},{3,1},{4,6},{6,4},{5,7},{7,5},{8,10},{10,8},{9,1... | collective-permute-start | bytes 442376 | tf_op jit(solution)/shard_map/ppermute | solution.py:15
  93.7 3.4 %collective-permute-done.12 = bf16[64,1152]{1,0:T(8,128)(2,1)S(1)} collective-permute-done((bf16[64,1152]{1,0:T(8,128)(2,1)S(1)}, bf16[64,1152]{1,0:T(8,128)(2,1)S(1)}, u32[]{:S(2)}, u32[]{:S(2)}) %collective-permute-start.12) | collective-permute-done | bytes 147488 | tf_op jit(solution)/shard_map/ppermute | solution.py:15
  97.1 5.9 %collective-permute-start.20 = (bf16[64,1152]{1,0:T(8,128)(2,1)S(1)}, bf16[64,1152]{1,0:T(8,128)(2,1)S(1)}, u32[]{:S(2)}, u32[]{:S(2)}) collective-permute-start(bf16[64,1152]{1,0:T(8,128)(2,1)S(1)} %get-tuple-element.44), channel_id=1, source_target_pairs={{0,8},{4,12},{8,0},{12,4},{1,9},{5,13},{9,1},{13,5},{2,10},{6,14},... | collective-permute-start | bytes 442376 | tf_op jit(solution)/shard_map/ppermute | solution.py:15
  104.0 2.8 %collective-permute-start.16 = (bf16[64,1152]{1,0:T(8,128)(2,1)S(1)}, bf16[64,1152]{1,0:T(8,128)(2,1)S(1)}, u32[]{:S(2)}, u32[]{:S(2)}) collective-permute-start(bf16[64,1152]{1,0:T(8,128)(2,1)S(1)} %get-tuple-element.44), channel_id=1, source_target_pairs={{0,12},{4,0},{8,4},{12,8},{1,13},{5,1},{9,5},{13,9},{2,14},{6,2},{... | collective-permute-start | bytes 442376 | tf_op jit(solution)/shard_map/ppermute | solution.py:15
  107.9 6.7 %collective-permute-start.24 = (bf16[64,1152]{1,0:T(8,128)(2,1)S(1)}, bf16[64,1152]{1,0:T(8,128)(2,1)S(1)}, u32[]{:S(2)}, u32[]{:S(2)}) collective-permute-start(bf16[64,1152]{1,0:T(8,128)(2,1)S(1)} %get-tuple-element.78), channel_id=1, source_target_pairs={{0,2},{1,3},{4,6},{5,7},{8,10},{9,11},{12,14},{13,15},{16,18},{17,... | collective-permute-start | bytes 442376 | tf_op jit(solution)/shard_map/ppermute | solution.py:283
  118.3 2.9 %collective-permute-start.18 = (bf16[64,1152]{1,0:T(8,128)(2,1)S(1)}, bf16[64,1152]{1,0:T(8,128)(2,1)S(1)}, u32[]{:S(2)}, u32[]{:S(2)}) collective-permute-start(bf16[64,1152]{1,0:T(8,128)(2,1)S(1)} %get-tuple-element.45), channel_id=1, source_target_pairs={{0,12},{4,0},{8,4},{12,8},{1,13},{5,1},{9,5},{13,9},{2,14},{6,2},{... | collective-permute-start | bytes 442376 | tf_op jit(solution)/shard_map/ppermute | solution.py:15
  126.5 5.2 %fusion = f32[256,2048]{1,0:T(8,128)S(1)} fusion(bf16[2,2048,2304]{2,1,0:T(8,128)(2,1)} %bitcast.38, bf16[256,1152]{1,0:T(8,128)(2,1)S(1)} %broadcast_select_fusion.next_ref, bf16[256,1152]{1,0:T(8,128)(2,1)S(1)} %broadcast_select_fusion.1.next_ref), kind=kOutput, calls=%fused_computation.2 | convolution fusion | flops 2418278400 | bytes 12713984 | tf_op jit(solution)/shard_map/dot_general | solution.py:19
  134.3 1.9 %collective-permute-start.27 = (bf16[64,1152]{1,0:T(8,128)(2,1)S(1)}, bf16[64,1152]{1,0:T(8,128)(2,1)S(1)}, u32[]{:S(2)}, u32[]{:S(2)}) collective-permute-start(bf16[64,1152]{1,0:T(8,128)(2,1)S(1)} %get-tuple-element.51), channel_id=1, source_target_pairs={{0,4},{4,8},{8,12},{12,0},{1,5},{5,9},{9,13},{13,1},{2,6},{6,10},{... | collective-permute-start | bytes 442376 | tf_op jit(solution)/shard_map/ppermute | solution.py:15
  136.4 2.9 %collective-permute-done.29 = bf16[64,1152]{1,0:T(8,128)(2,1)S(1)} collective-permute-done((bf16[64,1152]{1,0:T(8,128)(2,1)S(1)}, bf16[64,1152]{1,0:T(8,128)(2,1)S(1)}, u32[]{:S(2)}, u32[]{:S(2)}) %collective-permute-start.29) | collective-permute-done | bytes 147488 | tf_op jit(solution)/shard_map/ppermute | solution.py:15
  139.3 8.5 %shard_map.104.rest_0_ = bf16[2048,2,2304]{2,1,0:T(2,128)(2,1)} custom-call(bf16[256,2048]{1,0:T(8,128)(2,1)S(1)} %maximum_convert_fusion.features_ref, bf16[256,1152]{1,0:T(8,128)(2,1)S(1)} %fusion.25.own_ref, bf16[256,1152]{1,0:T(8,128)(2,1)S(1)} %broadcast_select_fusion.1.next_ref), custom_call_target="tpu_custom_call" | custom-call | flops 2415919104 | bytes 11665408 | tf_op jit(solution)/shard_map/pallas_call | solution.py:106
  147.9 5.2 %fusion.4 = f32[256,2048]{1,0:T(8,128)S(1)} fusion(bf16[2,2048,2304]{2,1,0:T(8,128)(2,1)} %bitcast.39, bf16[256,1152]{1,0:T(8,128)(2,1)S(1)} %maximum_select_fusion.own_ref, bf16[256,1152]{1,0:T(8,128)(2,1)S(1)} %fusion.25.own_ref), kind=kOutput, calls=%fused_computation.6 | convolution fusion | flops 2418278400 | bytes 12713984 | tf_op jit(solution)/shard_map/dot_general | solution.py:19
  153.6 8.5 %shard_map.106 = bf16[2048,2,2304]{2,1,0:T(2,128)(2,1)} custom-call(bf16[256,2048]{1,0:T(8,128)(2,1)S(1)} %maximum_convert_fusion.features_ref, bf16[256,1152]{1,0:T(8,128)(2,1)S(1)} %maximum_select_fusion.own_ref, bf16[256,1152]{1,0:T(8,128)(2,1)S(1)} %broadcast_select_fusion.next_ref, ...), custom_call_target="tpu_custom_call", output_to_operand_aliasing={{}: (3, {})} | custom-call | flops 2415919104 | bytes 11665408 | tf_op jit(solution)/shard_map/pallas_call | solution.py:106
  162.0 5.8 %shard_map.105 = (bf16[2048,2304]{1,0:T(8,128)(2,1)}, f32[1,2048]{1,0:T(1,128)}) custom-call(bf16[256,2048]{1,0:T(8,128)(2,1)S(1)} %add_convert_fusion.mine_ref, bf16[256,2048]{1,0:T(8,128)(2,1)S(1)} %collective-permute-done.32.other_ref, bf16[256,2048]{1,0:T(8,128)(2,1)S(1)} %compare_convert_fusion.live_ref, ...), custom_call_target="tpu_custom_call" | custom-call | flops 2415919104 | bytes 13762560 | tf_op jit(solution)/shard_map/pallas_call | solution.py:134
  (127 shorter events, 29.4 us)
Async XLA Ops:
  3.2 1.5 collective-permute-start
  4.8 30.5 %collective-permute-start.3 = (bf16[64,2304]{1,0:T(8,128)(2,1)S(1)}, bf16[64,2304]{1,0:T(8,128)(2,1)S(1)}, u32[]{:S(2)}, u32[]{:S(2)}) collective-permute-start(bf16[64,2304]{1,0:T(8,128)(2,1)S(1)} %pad_maximum_fusion.2), channel_id=1, source_target_pairs={{0,12},{4,0},{8,4},{12,8},{1,13},{5,1},{9,5},{13,9},{2,14},{6,2},{... | collective-permute-start | bytes 884744 | tf_op jit(solution)/shard_map/ppermute | solution.py:15
  9.9 25.4 %collective-permute-start.2 = (bf16[64,2304]{1,0:T(8,128)(2,1)S(1)}, bf16[64,2304]{1,0:T(8,128)(2,1)S(1)}, u32[]{:S(2)}, u32[]{:S(2)}) collective-permute-start(bf16[64,2304]{1,0:T(8,128)(2,1)S(1)} %pad_maximum_fusion.2), channel_id=1, source_target_pairs={{0,8},{4,12},{8,0},{12,4},{1,9},{5,13},{9,1},{13,5},{2,10},{6,14},... | collective-permute-start | bytes 884744 | tf_op jit(solution)/shard_map/ppermute | solution.py:15
  9.9 20.2 %collective-permute-start.1 = (bf16[64,2304]{1,0:T(8,128)(2,1)S(1)}, bf16[64,2304]{1,0:T(8,128)(2,1)S(1)}, u32[]{:S(2)}, u32[]{:S(2)}) collective-permute-start(bf16[64,2304]{1,0:T(8,128)(2,1)S(1)} %pad_maximum_fusion.2), channel_id=1, source_target_pairs={{0,4},{4,8},{8,12},{12,0},{1,5},{5,9},{9,13},{13,1},{2,6},{6,10},{... | collective-permute-start | bytes 884744 | tf_op jit(solution)/shard_map/ppermute | solution.py:15
  11.0 1.4 collective-permute-start.4
  11.1 1.6 collective-permute-start.5
  41.8 4.2 %collective-permute-start.6 = (f32[256,2048]{1,0:T(8,128)S(1)}, f32[256,2048]{1,0:T(8,128)S(1)}, u32[]{:S(2)}, u32[]{:S(2)}) collective-permute-start(f32[256,2048]{1,0:T(8,128)S(1)} %shard_map.102), channel_id=1, source_target_pairs={{0,1},{1,0},{2,3},{3,2},{4,5},{5,4},{6,7},{7,6},{8,9},{9,8},{10,11... | collective-permute-start | bytes 6291464 | tf_op jit(solution)/shard_map/ppermute | solution.py:15
  53.3 16.7 %collective-permute-start.8 = (bf16[256,1152]{1,0:T(8,128)(2,1)}, bf16[256,1152]{1,0:T(8,128)(2,1)}, u32[]{:S(2)}, u32[]{:S(2)}) collective-permute-start(bf16[256,1152]{1,0:T(8,128)(2,1)} %slice.181), channel_id=1, source_target_pairs={{0,2},{1,3},{4,6},{5,7},{8,10},{9,11},{12,14},{13,15},{16,18},{17,... | collective-permute-start | bytes 1769480 | tf_op jit(solution)/shard_map/ppermute | solution.py:255
  59.5 6.4 %collective-permute-start.7 = (bf16[64,1152]{1,0:T(8,128)(2,1)}, bf16[64,1152]{1,0:T(8,128)(2,1)}, u32[]{:S(2)}, u32[]{:S(2)}) collective-permute-start(bf16[64,1152]{1,0:T(8,128)(2,1)} %get-tuple-element.85), channel_id=1, source_target_pairs={{0,12},{4,0},{8,4},{12,8},{1,13},{5,1},{9,5},{13,9},{2,14},{6,2},{... | collective-permute-start | bytes 442376 | tf_op jit(solution)/shard_map/ppermute | solution.py:15
  61.0 18.7 %collective-permute-start.13 = (bf16[64,1152]{1,0:T(8,128)(2,1)S(1)}, bf16[64,1152]{1,0:T(8,128)(2,1)S(1)}, u32[]{:S(2)}, u32[]{:S(2)}) collective-permute-start(bf16[64,1152]{1,0:T(8,128)(2,1)S(1)} %copy-done.5), channel_id=1, source_target_pairs={{0,8},{4,12},{8,0},{12,4},{1,9},{5,13},{9,1},{13,5},{2,10},{6,14},... | collective-permute-start | bytes 442376 | tf_op jit(solution)/shard_map/ppermute | solution.py:15
  63.9 15.7 %collective-permute-start.14 = (bf16[64,1152]{1,0:T(8,128)(2,1)S(1)}, bf16[64,1152]{1,0:T(8,128)(2,1)S(1)}, u32[]{:S(2)}, u32[]{:S(2)}) collective-permute-start(bf16[64,1152]{1,0:T(8,128)(2,1)S(1)} %get-tuple-element.84), channel_id=1, source_target_pairs={{0,4},{4,8},{8,12},{12,0},{1,5},{5,9},{9,13},{13,1},{2,6},{6,10},{... | collective-permute-start | bytes 442376 | tf_op jit(solution)/shard_map/ppermute | solution.py:15
  72.0 14.2 %collective-permute-start.9 = (bf16[64,1152]{1,0:T(8,128)(2,1)S(1)}, bf16[64,1152]{1,0:T(8,128)(2,1)S(1)}, u32[]{:S(2)}, u32[]{:S(2)}) collective-permute-start(bf16[64,1152]{1,0:T(8,128)(2,1)S(1)} %get-tuple-element.86), channel_id=1, source_target_pairs={{0,8},{4,12},{8,0},{12,4},{1,9},{5,13},{9,1},{13,5},{2,10},{6,14},... | collective-permute-start | bytes 442376 | tf_op jit(solution)/shard_map/ppermute | solution.py:15
  75.0 11.7 %collective-permute-start.11 = (bf16[64,1152]{1,0:T(8,128)(2,1)S(1)}, bf16[64,1152]{1,0:T(8,128)(2,1)S(1)}, u32[]{:S(2)}, u32[]{:S(2)}) collective-permute-start(bf16[64,1152]{1,0:T(8,128)(2,1)S(1)} %get-tuple-element.87), channel_id=1, source_target_pairs={{0,12},{4,0},{8,4},{12,8},{1,13},{5,1},{9,5},{13,9},{2,14},{6,2},{... | collective-permute-start | bytes 442376 | tf_op jit(solution)/shard_map/ppermute | solution.py:15
  75.4 11.3 %collective-permute-start.10 = (bf16[64,1152]{1,0:T(8,128)(2,1)S(1)}, bf16[64,1152]{1,0:T(8,128)(2,1)S(1)}, u32[]{:S(2)}, u32[]{:S(2)}) collective-permute-start(bf16[64,1152]{1,0:T(8,128)(2,1)S(1)} %get-tuple-element.88), channel_id=1, source_target_pairs={{0,4},{4,8},{8,12},{12,0},{1,5},{5,9},{9,13},{13,1},{2,6},{6,10},{... | collective-permute-start | bytes 442376 | tf_op jit(solution)/shard_map/ppermute | solution.py:15
  80.8 12.9 %collective-permute-start.15 = (f32[64,1152]{1,0:T(8,128)S(1)}, f32[64,1152]{1,0:T(8,128)S(1)}, u32[]{:S(2)}, u32[]{:S(2)}) collective-permute-start(f32[64,1152]{1,0:T(8,128)S(1)} %fusion.30), channel_id=1, source_target_pairs={{0,2},{2,0},{1,3},{3,1},{4,6},{6,4},{5,7},{7,5},{8,10},{10,8},{9,1... | collective-permute-start | bytes 884744 | tf_op jit(solution)/shard_map/ppermute | solution.py:15
  86.9 17.1 %collective-permute-start.22 = (bf16[64,1152]{1,0:T(8,128)(2,1)S(1)}, bf16[64,1152]{1,0:T(8,128)(2,1)S(1)}, u32[]{:S(2)}, u32[]{:S(2)}) collective-permute-start(bf16[64,1152]{1,0:T(8,128)(2,1)S(1)} %get-tuple-element.79), channel_id=1, source_target_pairs={{0,8},{4,12},{8,0},{12,4},{1,9},{5,13},{9,1},{13,5},{2,10},{6,14},... | collective-permute-start | bytes 442376 | tf_op jit(solution)/shard_map/ppermute | solution.py:15
  89.7 7.4 %collective-permute-start.12 = (bf16[64,1152]{1,0:T(8,128)(2,1)S(1)}, bf16[64,1152]{1,0:T(8,128)(2,1)S(1)}, u32[]{:S(2)}, u32[]{:S(2)}) collective-permute-start(bf16[64,1152]{1,0:T(8,128)(2,1)S(1)} %get-tuple-element.80), channel_id=1, source_target_pairs={{0,12},{4,0},{8,4},{12,8},{1,13},{5,1},{9,5},{13,9},{2,14},{6,2},{... | collective-permute-start | bytes 442376 | tf_op jit(solution)/shard_map/ppermute | solution.py:15
  91.8 15.0 %collective-permute-start.21 = (bf16[64,1152]{1,0:T(8,128)(2,1)S(1)}, bf16[64,1152]{1,0:T(8,128)(2,1)S(1)}, u32[]{:S(2)}, u32[]{:S(2)}) collective-permute-start(bf16[64,1152]{1,0:T(8,128)(2,1)S(1)} %get-tuple-element.67), channel_id=1, source_target_pairs={{0,4},{4,8},{8,12},{12,0},{1,5},{5,9},{9,13},{13,1},{2,6},{6,10},{... | collective-permute-start | bytes 442376 | tf_op jit(solution)/shard_map/ppermute | solution.py:15
  91.9 22.8 %collective-permute-start.17 = (bf16[64,1152]{1,0:T(8,128)(2,1)S(1)}, bf16[64,1152]{1,0:T(8,128)(2,1)S(1)}, u32[]{:S(2)}, u32[]{:S(2)}) collective-permute-start(bf16[64,1152]{1,0:T(8,128)(2,1)S(1)} %fusion.48), channel_id=1, source_target_pairs={{0,2},{2,0},{1,3},{3,1},{4,6},{6,4},{5,7},{7,5},{8,10},{10,8},{9,1... | collective-permute-start | bytes 442376 | tf_op jit(solution)/shard_map/ppermute | solution.py:15
  97.1 24.1 %collective-permute-start.20 = (bf16[64,1152]{1,0:T(8,128)(2,1)S(1)}, bf16[64,1152]{1,0:T(8,128)(2,1)S(1)}, u32[]{:S(2)}, u32[]{:S(2)}) collective-permute-start(bf16[64,1152]{1,0:T(8,128)(2,1)S(1)} %get-tuple-element.44), channel_id=1, source_target_pairs={{0,8},{4,12},{8,0},{12,4},{1,9},{5,13},{9,1},{13,5},{2,10},{6,14},... | collective-permute-start | bytes 442376 | tf_op jit(solution)/shard_map/ppermute | solution.py:15
  103.0 15.3 %collective-permute-start.19 = (bf16[64,1152]{1,0:T(8,128)(2,1)S(1)}, bf16[64,1152]{1,0:T(8,128)(2,1)S(1)}, u32[]{:S(2)}, u32[]{:S(2)}) collective-permute-start(bf16[64,1152]{1,0:T(8,128)(2,1)S(1)} %get-tuple-element.44), channel_id=1, source_target_pairs={{0,4},{4,8},{8,12},{12,0},{1,5},{5,9},{9,13},{13,1},{2,6},{6,10},{... | collective-permute-start | bytes 442376 | tf_op jit(solution)/shard_map/ppermute | solution.py:15
  104.0 12.0 %collective-permute-start.16 = (bf16[64,1152]{1,0:T(8,128)(2,1)S(1)}, bf16[64,1152]{1,0:T(8,128)(2,1)S(1)}, u32[]{:S(2)}, u32[]{:S(2)}) collective-permute-start(bf16[64,1152]{1,0:T(8,128)(2,1)S(1)} %get-tuple-element.44), channel_id=1, source_target_pairs={{0,12},{4,0},{8,4},{12,8},{1,13},{5,1},{9,5},{13,9},{2,14},{6,2},{... | collective-permute-start | bytes 442376 | tf_op jit(solution)/shard_map/ppermute | solution.py:15
  107.9 9.3 %collective-permute-start.24 = (bf16[64,1152]{1,0:T(8,128)(2,1)S(1)}, bf16[64,1152]{1,0:T(8,128)(2,1)S(1)}, u32[]{:S(2)}, u32[]{:S(2)}) collective-permute-start(bf16[64,1152]{1,0:T(8,128)(2,1)S(1)} %get-tuple-element.78), channel_id=1, source_target_pairs={{0,2},{1,3},{4,6},{5,7},{8,10},{9,11},{12,14},{13,15},{16,18},{17,... | collective-permute-start | bytes 442376 | tf_op jit(solution)/shard_map/ppermute | solution.py:283
  114.7 11.8 %collective-permute-start.23 = (bf16[256,1152]{1,0:T(8,128)(2,1)S(1)}, bf16[256,1152]{1,0:T(8,128)(2,1)S(1)}, u32[]{:S(2)}, u32[]{:S(2)}) collective-permute-start(bf16[256,1152]{1,0:T(8,128)(2,1)S(1)} %fusion.22), channel_id=1, source_target_pairs={{2,0},{3,1},{6,4},{7,5},{10,8},{11,9},{14,12},{15,13},{18,16},{19,... | collective-permute-start | bytes 1769480 | tf_op jit(solution)/shard_map/ppermute | solution.py:276
  116.0 20.2 %collective-permute-start.31 = (bf16[64,1152]{1,0:T(8,128)(2,1)S(1)}, bf16[64,1152]{1,0:T(8,128)(2,1)S(1)}, u32[]{:S(2)}, u32[]{:S(2)}) collective-permute-start(bf16[64,1152]{1,0:T(8,128)(2,1)S(1)} %get-tuple-element.45), channel_id=1, source_target_pairs={{0,8},{4,12},{8,0},{12,4},{1,9},{5,13},{9,1},{13,5},{2,10},{6,14},... | collective-permute-start | bytes 442376 | tf_op jit(solution)/shard_map/ppermute | solution.py:15
  117.2 19.0 %collective-permute-start.30 = (bf16[64,1152]{1,0:T(8,128)(2,1)S(1)}, bf16[64,1152]{1,0:T(8,128)(2,1)S(1)}, u32[]{:S(2)}, u32[]{:S(2)}) collective-permute-start(bf16[64,1152]{1,0:T(8,128)(2,1)S(1)} %get-tuple-element.45), channel_id=1, source_target_pairs={{0,4},{4,8},{8,12},{12,0},{1,5},{5,9},{9,13},{13,1},{2,6},{6,10},{... | collective-permute-start | bytes 442376 | tf_op jit(solution)/shard_map/ppermute | solution.py:15
  118.3 13.4 %collective-permute-start.18 = (bf16[64,1152]{1,0:T(8,128)(2,1)S(1)}, bf16[64,1152]{1,0:T(8,128)(2,1)S(1)}, u32[]{:S(2)}, u32[]{:S(2)}) collective-permute-start(bf16[64,1152]{1,0:T(8,128)(2,1)S(1)} %get-tuple-element.45), channel_id=1, source_target_pairs={{0,12},{4,0},{8,4},{12,8},{1,13},{5,1},{9,5},{13,9},{2,14},{6,2},{... | collective-permute-start | bytes 442376 | tf_op jit(solution)/shard_map/ppermute | solution.py:15
  121.2 1.4 collective-permute-start.25
  131.8 7.6 %collective-permute-start.29 = (bf16[64,1152]{1,0:T(8,128)(2,1)S(1)}, bf16[64,1152]{1,0:T(8,128)(2,1)S(1)}, u32[]{:S(2)}, u32[]{:S(2)}) collective-permute-start(bf16[64,1152]{1,0:T(8,128)(2,1)S(1)} %get-tuple-element.51), channel_id=1, source_target_pairs={{0,12},{4,0},{8,4},{12,8},{1,13},{5,1},{9,5},{13,9},{2,14},{6,2},{... | collective-permute-start | bytes 442376 | tf_op jit(solution)/shard_map/ppermute | solution.py:15
  133.4 14.4 %collective-permute-start.28 = (bf16[64,1152]{1,0:T(8,128)(2,1)S(1)}, bf16[64,1152]{1,0:T(8,128)(2,1)S(1)}, u32[]{:S(2)}, u32[]{:S(2)}) collective-permute-start(bf16[64,1152]{1,0:T(8,128)(2,1)S(1)} %get-tuple-element.51), channel_id=1, source_target_pairs={{0,8},{4,12},{8,0},{12,4},{1,9},{5,13},{9,1},{13,5},{2,10},{6,14},... | collective-permute-start | bytes 442376 | tf_op jit(solution)/shard_map/ppermute | solution.py:15
  134.3 13.5 %collective-permute-start.27 = (bf16[64,1152]{1,0:T(8,128)(2,1)S(1)}, bf16[64,1152]{1,0:T(8,128)(2,1)S(1)}, u32[]{:S(2)}, u32[]{:S(2)}) collective-permute-start(bf16[64,1152]{1,0:T(8,128)(2,1)S(1)} %get-tuple-element.51), channel_id=1, source_target_pairs={{0,4},{4,8},{8,12},{12,0},{1,5},{5,9},{9,13},{13,1},{2,6},{6,10},{... | collective-permute-start | bytes 442376 | tf_op jit(solution)/shard_map/ppermute | solution.py:15
  153.5 8.5 %collective-permute-start.32 = (bf16[256,2048]{1,0:T(8,128)(2,1)S(1)}, bf16[256,2048]{1,0:T(8,128)(2,1)S(1)}, u32[]{:S(2)}, u32[]{:S(2)}) collective-permute-start(bf16[256,2048]{1,0:T(8,128)(2,1)S(1)} %add_convert_fusion.mine_ref), channel_id=1, source_target_pairs={{0,1},{1,0},{2,3},{3,2},{4,5},{5,4},{6,7},{7,6},{8,9},{9,8},{10,11... | collective-permute-start | bytes 3145736 | tf_op jit(solution)/shard_map/ppermute | solution.py:15
  (13 other events, 155.1 us)

commit v3 on v2

--- a/solution.py
+++ b/solution.py
@@ -15,6 +15,10 @@
     return lax.ppermute(block, axis, [(i, (i + distance) % count) for i in range(count)])
 
 
+def swapped(block, axis, distance):
+    return lax.ppermute(block, axis, [(i, i ^ distance) for i in range(lax.axis_size(axis))])
+
+
 def dot_last(left, right):
     return lax.dot_general(
         left, right, (((1,), (1,)), ((), ())), preferred_element_type=jnp.float32
@@ -27,8 +31,18 @@
     )
 
 
-def shift_order(count):
-    return sorted(range(1, count), key=lambda k: -min(k, count - k))
+def spread(block, axis, doubling):
+    count = lax.axis_size(axis)
+    held = {0: block}
+    if doubling:
+        distance = count // 2
+        while distance:
+            held.update({j ^ distance: swapped(held[j], axis, distance) for j in list(held)})
+            distance //= 2
+    else:
+        for k in reversed(range(1, count)):
+            held[k] = swapped(block, axis, k)
+    return [held[j] for j in range(count)]
 
 
 def vmem_params():
@@ -169,7 +183,8 @@
     block_rows = rows_each * lax.axis_size("row")
     total_rows = block_rows * feat_count
     loss_scale = float(total_rows) ** (-0.5)
-    order = shift_order(feat_count)
+    others = range(1, feat_count)
+    near = min(1, feat_count - 1)
 
     def to_half(block):
         left, right = block[:, :half], block[:, half:]
@@ -199,19 +214,17 @@
 
     own_layer = jnp.where(leading, resid_buf[:, 0], resid_buf[:, layers - 1])
     own_block = to_half(own_layer)
-    arrived = {0: own_block}
-    for k in order:
-        arrived[k] = shifted(own_block, "feat", k)
+    arrived = spread(own_block, "feat", True)
     own_mlp, sent_block = lax.optimization_barrier((mlp_out, own_block))
     mlp_half = [to_half(own_mlp[:, t]) for t in range(layers)]
     mlp_half, dec_weight = lax.optimization_barrier((mlp_half, dec_weight))
     slots = jnp.swapaxes(dec_weight[0], 0, 1)
-    buffered = jnp.concatenate([arrived[k] for k in range(feat_count)], axis=0)
+    buffered = jnp.concatenate(arrived, axis=0)
     buffered, slots, enc_weight = lax.optimization_barrier((buffered, slots, enc_weight))
     blocks = shuffle.reshape(feat_count, block_rows)
-    relative = (feat_pos - jnp.arange(feat_count)) % feat_count
+    relative = feat_pos ^ jnp.arange(feat_count)
     wanted = jnp.take(blocks, relative, axis=0).reshape(total_rows)
-    place = ((feat_pos - wanted // block_rows) % feat_count) * block_rows + wanted % block_rows
+    place = (feat_pos ^ (wanted // block_rows)) * block_rows + wanted % block_rows
     picks = (place[:, None] == jnp.arange(total_rows)[None]).astype(bf16)
     inputs = jnp.dot(picks, buffered, preferred_element_type=f32).astype(bf16)
 
@@ -230,18 +243,17 @@
     low, high = slice(0, piece), slice(piece, half)
 
     def rows_of(array, k):
-        j = (feat_count - k) % feat_count
-        return array[j * block_rows : (j + 1) * block_rows]
+        return array[k * block_rows : (k + 1) * block_rows]
 
     def move(pick):
         arriving = [None] * feat_count
-        for k in order:
-            arriving[k] = shifted(pick(k), "feat", k)
+        for k in reversed(others):
+            arriving[k] = swapped(pick(k), "feat", k)
         return arriving
 
     def reduced(partial, arriving):
         total = rows_of(partial, 0).astype(f32)
-        for k in order:
+        for k in others:
             total = total + arriving[k].astype(f32)
         return section_total(total)
 
@@ -256,7 +268,6 @@
     low_part = jnp.where(leading, next_part[:, low].astype(f32), own_part[:, low])
     low_sent = low_part.astype(bf16)
     low_moved = move(lambda k: rows_of(low_sent, k))
-    near = order[-1]
     low_moved[near], carried = lax.optimization_barrier((low_moved[near], carried))
     second_part = jnp.where(leading, own_part[:, low], own_part[:, high] + carried.astype(f32))
     second_sent = second_part.astype(bf16)
@@ -272,7 +283,7 @@
     high_sent = own_part[:, high].astype(bf16)
     third_moved = move(lambda k: jnp.where(leading, rows_of(high_sent, k), second_error))
     third_moved[near], fourth = lax.optimization_barrier((third_moved[near], last_low))
-    fourth_moved = move(lambda k: fourth)
+    fourth_moved = spread(fourth, "feat", True)
     last_high_all = lax.ppermute(joined(second_error, third_moved), "layer", backward)
     third_high_all = joined(second_error, third_moved)
     third_sum = reduced(own_part[:, high], third_moved)
@@ -284,7 +295,7 @@
     fourth_moved[near], other_half, fifth = lax.optimization_barrier(
         (fourth_moved[near], other_half, second_error)
     )
-    fifth_moved = move(lambda k: fifth)
+    fifth_moved = spread(fifth, "feat", True)
     fourth_all = joined(fourth, fourth_moved)
     first_rows = jnp.concatenate(
         [jnp.where(leading, recon_low, other_half), jnp.where(leading, recon_high, lead_high)], axis=1
@@ -292,18 +303,18 @@
     last_rows = jnp.concatenate(
         [recon_last_low.astype(bf16), jnp.where(leading, other_half, recon_low)], axis=1
     )
-    output = pair_call(from_half(first_rows), from_half(last_rows))
     empty = jnp.zeros((total_rows, piece), bf16)
     next_low = jnp.where(leading, fourth_all, empty)
     next_high = jnp.where(leading, last_high_all, empty)
     next_terms = dot_last(jnp.concatenate([next_low, next_high], axis=1), slots[1])
-    fifth_moved[near], next_terms, output, live, sixth = lax.optimization_barrier(
-        (fifth_moved[near], next_terms, output, live, third_error)
-    )
-    sixth_moved = move(lambda k: sixth)
+    fifth_moved[near], next_terms, first_rows, last_rows, live, sixth = lax.optimization_barrier(
+        (fifth_moved[near], next_terms, first_rows, last_rows, live, third_error)
+    )
+    sixth_moved = spread(sixth, "feat", False)
 
     own_low = jnp.where(leading, joined(second_error, fifth_moved), fourth_all)
-    sixth_moved[near], own_low = lax.optimization_barrier((sixth_moved[near], own_low))
+    output = pair_call(from_half(first_rows), from_half(last_rows))
+    output, own_low = lax.optimization_barrier((output, own_low))
     dec_low = dec_grad_call(features, own_low, next_low, loss_scale, 0, CHUNKS)
     early = next_terms
     sixth_moved, dec_low, early = lax.optimization_barrier((sixth_moved[1:], dec_low, early))

time: 171 us -> 165 us (0.965); the launches traced: 168 us -> 165 us
  starting transfers between devices: 54.7 us -> 42.2 us
  waiting for transfers between devices: 38.2 us -> 46.9 us
    ppermute x30 -> x9, starting transfers between devices: 42.4 us -> 5.61 us  [shifted(): lax.ppermute(block, axis, [(i, (i + distance) % count) for i in range(cou...]
    ppermute x0 -> x21, waiting for transfers between devices: none -> 36.3 us  [swapped(): lax.ppermute(block, axis, [(i, i ^ distance) for i in range(lax.axis_size...]
    ppermute x0 -> x21, starting transfers between devices: none -> 28.4 us  [swapped(): lax.ppermute(block, axis, [(i, i ^ distance) for i in range(lax.axis_size...]
    ppermute x30 -> x9, waiting for transfers between devices: 32 us -> 6.13 us  [shifted(): lax.ppermute(block, axis, [(i, (i + distance) % count) for i in range(cou...]
    ppermute x1, starting transfers between devices: 6.67 us -> 2.59 us  [on_device(): lead_high = lax.ppermute(recon_high, 'layer', forward)]
  transfers between devices with their start and end apart: 33 -> 33, of which waited for: 16 -> 17; matrix products, arithmetic and copies ran while one was open for 17% -> 17% of each run, Pallas kernels for 11% -> 11%
where the time goes in v3:
time: 165 us
  waiting for transfers between devices  46.9 us (28%)
  starting transfers between devices  42.2 us (26%)
  Pallas kernels  29.6 us (18%)
  local copies, waits for them, and re-layouts  18.7 us (11%)
  matrix products  17.5 us (11%)
  other arithmetic  8.56 us (5%)
    ppermute x21, waiting for transfers between devices, swapped(): lax.ppermute(block, axis, [(i, i ^ distance) for i in range(lax.axis_size...  36.3 us
    ppermute x21, starting transfers between devices, swapped(): lax.ppermute(block, axis, [(i, i ^ distance) for i in range(lax.axis_size...  28.4 us
    pallas_call x2, Pallas kernels, dec_grad_call(): pl.pallas_call(functools.partial(dec_grad_kernel, scale), grid=(count //...  16.7 us
    optimization_barrier x1, local copies, waits for them, and re-layouts, on_device(): mlp_half, dec_weight = lax.optimization_barrier((mlp_half, dec_weight))  12.3 us
    dot_general x2, matrix products, dot_last(): lax.dot_general(left, right, (((1,), (1,)), ((), ())), preferred_element_...  11.6 us
    ppermute x9, waiting for transfers between devices, shifted(): lax.ppermute(block, axis, [(i, (i + distance) % count) for i in range(cou...  6.13 us
    pallas_call x1, Pallas kernels, encoder_call(): pl.pallas_call(encoder_kernel, in_specs=[pl.BlockSpec(memory_space=pltpu....  5.91 us
    pallas_call x1, Pallas kernels, enc_grad_call(): pl.pallas_call(functools.partial(enc_grad_kernel, scale), grid=(count //...  5.8 us
  transfers between devices with their start and end apart: 33, of which 17 were waited for; matrix products, arithmetic and copies ran while one was open for 17% of the time, Pallas kernels for 11%

profile of v3, /device:TPU:0, one launch (start us, length us, event | category | flops | bytes accessed | tf_op | source)
XLA Modules:
  0.0 164.7 jit_solution(535470766833846777)
XLA Ops:
  0.6 2.4 %fusion.54 = (bf16[32,1,4608]{2,1,0:T(2,128)(2,1)S(1)}, bf16[32,1,4608]{2,1,0:T(2,128)(2,1)S(1)}) fusion(bf16[32,2,4608]{2,1,0:T(2,128)(2,1)} %param.7), kind=kLoop, calls=%fused_computation.128 | loop fusion | bytes 1179648 | tf_op jit(solution)/shard_map/slice | solution.py:215
  4.8 4.0 %collective-permute-start.2 = (bf16[64,2304]{1,0:T(8,128)(2,1)S(1)}, bf16[64,2304]{1,0:T(8,128)(2,1)S(1)}, u32[]{:S(2)}, u32[]{:S(2)}) collective-permute-start(bf16[64,2304]{1,0:T(8,128)(2,1)S(1)} %pad_maximum_fusion.2), channel_id=1, source_target_pairs={{0,8},{4,12},{8,0},{12,4},{1,9},{5,13},{9,1},{13,5},{2,10},{6,14},... | collective-permute-start | bytes 884744 | tf_op jit(solution)/shard_map/ppermute | solution.py:19
  8.9 1.6 collective-permute-start.1
  13.1 12.3 %copy.28 = bf16[1,2048,2,2304]{3,1,2,0:T(8,128)(2,1)S(1)} copy(bf16[1,2048,2,2304]{3,2,1,0:T(2,128)(2,1)} %param.11) | data formatting | bytes 37748736 | tf_op jit(solution)/shard_map/optimization_barrier | solution.py:220
  26.0 8.8 %collective-permute-done.3 = bf16[64,2304]{1,0:T(8,128)(2,1)S(1)} collective-permute-done((bf16[64,2304]{1,0:T(8,128)(2,1)S(1)}, bf16[64,2304]{1,0:T(8,128)(2,1)S(1)}, u32[]{:S(2)}, u32[]{:S(2)}) %collective-permute-start.3) | collective-permute-done | bytes 294944 | tf_op jit(solution)/shard_map/ppermute | solution.py:19
  35.4 5.9 %shard_map.102 = f32[256,2048]{1,0:T(8,128)S(1)} custom-call(bf16[256,2304]{1,0:T(8,128)(2,1)S(1)} %convolution_convert_fusion.inputs_ref, bf16[2048,2304]{1,0:T(8,128)(2,1)S(1)} %bitcast.38), custom_call_target="tpu_custom_call" | custom-call | tf_op jit(solution)/shard_map/pallas_call | solution.py:70
  41.4 4.1 %collective-permute-done.6 = f32[256,2048]{1,0:T(8,128)S(1)} collective-permute-done((f32[256,2048]{1,0:T(8,128)S(1)}, f32[256,2048]{1,0:T(8,128)S(1)}, u32[]{:S(2)}, u32[]{:S(2)}) %collective-permute-start.6) | collective-permute-done | bytes 2097184 | tf_op jit(solution)/shard_map/ppermute | solution.py:15
  46.4 2.7 %fusion.12 = bf16[256,2304]{1,0:T(8,128)(2,1)S(1)} fusion(bf16[256,2048]{1,0:T(8,128)(2,1)S(1)} %maximum_convert_fusion.features_ref, bf16[2,2048,2304]{2,1,0:T(8,128)(2,1)S(1)} %bitcast.40), kind=kOutput, calls=%fused_computation.14 | convolution fusion | flops 2416508928 | bytes 11665408 | tf_op jit(solution)/shard_map/dot_general | solution.py:239
  49.1 2.7 %fusion.6 = f32[256,2304]{1,0:T(8,128)S(1)} fusion(bf16[256,2048]{1,0:T(8,128)(2,1)S(1)} %maximum_convert_fusion.features_ref, bf16[2,2048,2304]{2,1,0:T(8,128)(2,1)S(1)} %bitcast.41), kind=kOutput, calls=%fused_computation.8 | convolution fusion | flops 2415919104 | bytes 12845056 | tf_op jit(solution)/shard_map/dot_general | solution.py:240
  52.7 4.3 %collective-permute-start.8 = (bf16[256,1152]{1,0:T(8,128)(2,1)}, bf16[256,1152]{1,0:T(8,128)(2,1)}, u32[]{:S(2)}, u32[]{:S(2)}) collective-permute-start(bf16[256,1152]{1,0:T(8,128)(2,1)} %slice.181), channel_id=1, source_target_pairs={{0,2},{1,3},{4,6},{5,7},{8,10},{9,11},{12,14},{13,15},{16,18},{17,... | collective-permute-start | bytes 1769480 | tf_op jit(solution)/shard_map/ppermute | solution.py:267
  61.3 3.6 %collective-permute-start.14 = (bf16[64,1152]{1,0:T(8,128)(2,1)S(1)}, bf16[64,1152]{1,0:T(8,128)(2,1)S(1)}, u32[]{:S(2)}, u32[]{:S(2)}) collective-permute-start(bf16[64,1152]{1,0:T(8,128)(2,1)S(1)} %get-tuple-element.86), channel_id=1, source_target_pairs={{0,12},{4,8},{8,4},{12,0},{1,13},{5,9},{9,5},{13,1},{2,14},{6,10},... | collective-permute-start | bytes 442376 | tf_op jit(solution)/shard_map/ppermute | solution.py:19
  66.0 3.5 %collective-permute-done.8 = bf16[256,1152]{1,0:T(8,128)(2,1)} collective-permute-done((bf16[256,1152]{1,0:T(8,128)(2,1)}, bf16[256,1152]{1,0:T(8,128)(2,1)}, u32[]{:S(2)}, u32[]{:S(2)}) %collective-permute-start.8) | collective-permute-done | bytes 589856 | tf_op jit(solution)/shard_map/ppermute | solution.py:267
  69.5 2.0 %fusion.50 = (bf16[256,1152]{1,0:T(8,128)(2,1)S(1)}, f32[256,1152]{1,0:T(8,128)S(1)}) fusion(bf16[256,1152]{1,0:T(8,128)(2,1)} %collective-permute-done.8, f32[256,2304]{1,0:T(8,128)} %copy-done.1, pred[]{:T(512)S(6)} %lt.27), kind=kLoop, calls=%fused_computation.124 | loop fusion | flops 1179648 | bytes 4718593 | tf_op jit(solution)/shard_map/convert_element_type | solution.py:273
  72.0 1.3 collective-permute-start.11
  73.3 1.7 %collective-permute-start.10 = (bf16[64,1152]{1,0:T(8,128)(2,1)S(1)}, bf16[64,1152]{1,0:T(8,128)(2,1)S(1)}, u32[]{:S(2)}, u32[]{:S(2)}) collective-permute-start(bf16[64,1152]{1,0:T(8,128)(2,1)S(1)} %get-tuple-element.90), channel_id=1, source_target_pairs={{0,8},{4,12},{8,0},{12,4},{1,9},{5,13},{9,1},{13,5},{2,10},{6,14},... | collective-permute-start | bytes 442376 | tf_op jit(solution)/shard_map/ppermute | solution.py:19
  76.1 2.5 %collective-permute-start.15 = (f32[64,1152]{1,0:T(8,128)S(1)}, f32[64,1152]{1,0:T(8,128)S(1)}, u32[]{:S(2)}, u32[]{:S(2)}) collective-permute-start(f32[64,1152]{1,0:T(8,128)S(1)} %fusion.36), channel_id=1, source_target_pairs={{0,2},{2,0},{1,3},{3,1},{4,6},{6,4},{5,7},{7,5},{8,10},{10,8},{9,1... | collective-permute-start | bytes 884744 | tf_op jit(solution)/shard_map/ppermute | solution.py:15
  80.8 8.6 %collective-permute-done.10 = bf16[64,1152]{1,0:T(8,128)(2,1)S(1)} collective-permute-done((bf16[64,1152]{1,0:T(8,128)(2,1)S(1)}, bf16[64,1152]{1,0:T(8,128)(2,1)S(1)}, u32[]{:S(2)}, u32[]{:S(2)}) %collective-permute-start.10) | collective-permute-done | bytes 147488 | tf_op jit(solution)/shard_map/ppermute | solution.py:19
  90.9 3.1 %collective-permute-start.21 = (bf16[64,1152]{1,0:T(8,128)(2,1)S(1)}, bf16[64,1152]{1,0:T(8,128)(2,1)S(1)}, u32[]{:S(2)}, u32[]{:S(2)}) collective-permute-start(bf16[64,1152]{1,0:T(8,128)(2,1)S(1)} %get-tuple-element.69), channel_id=1, source_target_pairs={{0,8},{4,12},{8,0},{12,4},{1,9},{5,13},{9,1},{13,5},{2,10},{6,14},... | collective-permute-start | bytes 442376 | tf_op jit(solution)/shard_map/ppermute | solution.py:19
  95.2 6.6 %collective-permute-done.12 = bf16[64,1152]{1,0:T(8,128)(2,1)S(1)} collective-permute-done((bf16[64,1152]{1,0:T(8,128)(2,1)S(1)}, bf16[64,1152]{1,0:T(8,128)(2,1)S(1)}, u32[]{:S(2)}, u32[]{:S(2)}) %collective-permute-start.12) | collective-permute-done | bytes 147488 | tf_op jit(solution)/shard_map/ppermute | solution.py:19
  101.8 2.0 %collective-permute-start.16 = (bf16[64,1152]{1,0:T(8,128)(2,1)S(1)}, bf16[64,1152]{1,0:T(8,128)(2,1)S(1)}, u32[]{:S(2)}, u32[]{:S(2)}) collective-permute-start(bf16[64,1152]{1,0:T(8,128)(2,1)S(1)} %get-tuple-element.45), channel_id=1, source_target_pairs={{0,4},{4,0},{8,12},{12,8},{1,5},{5,1},{9,13},{13,9},{2,6},{6,2},{1... | collective-permute-start | bytes 442376 | tf_op jit(solution)/shard_map/ppermute | solution.py:19
  104.9 2.6 %collective-permute-start.24 = (bf16[64,1152]{1,0:T(8,128)(2,1)S(1)}, bf16[64,1152]{1,0:T(8,128)(2,1)S(1)}, u32[]{:S(2)}, u32[]{:S(2)}) collective-permute-start(bf16[64,1152]{1,0:T(8,128)(2,1)S(1)} %get-tuple-element.80), channel_id=1, source_target_pairs={{0,2},{1,3},{4,6},{5,7},{8,10},{9,11},{12,14},{13,15},{16,18},{17,... | collective-permute-start | bytes 442376 | tf_op jit(solution)/shard_map/ppermute | solution.py:294
  108.9 3.2 %collective-permute-done.16 = bf16[64,1152]{1,0:T(8,128)(2,1)S(1)} collective-permute-done((bf16[64,1152]{1,0:T(8,128)(2,1)S(1)}, bf16[64,1152]{1,0:T(8,128)(2,1)S(1)}, u32[]{:S(2)}, u32[]{:S(2)}) %collective-permute-start.16) | collective-permute-done | bytes 147488 | tf_op jit(solution)/shard_map/ppermute | solution.py:19
  112.0 3.0 %collective-permute-start.18 = (bf16[64,1152]{1,0:T(8,128)(2,1)S(1)}, bf16[64,1152]{1,0:T(8,128)(2,1)S(1)}, u32[]{:S(2)}, u32[]{:S(2)}) collective-permute-start(bf16[64,1152]{1,0:T(8,128)(2,1)S(1)} %get-tuple-element.46), channel_id=1, source_target_pairs={{0,4},{4,0},{8,12},{12,8},{1,5},{5,1},{9,13},{13,9},{2,6},{6,2},{1... | collective-permute-start | bytes 442376 | tf_op jit(solution)/shard_map/ppermute | solution.py:19
  115.3 4.2 %collective-permute-done.27 = bf16[64,1152]{1,0:T(8,128)(2,1)S(1)} collective-permute-done((bf16[64,1152]{1,0:T(8,128)(2,1)S(1)}, bf16[64,1152]{1,0:T(8,128)(2,1)S(1)}, u32[]{:S(2)}, u32[]{:S(2)}) %collective-permute-start.27) | collective-permute-done | bytes 147488 | tf_op jit(solution)/shard_map/ppermute | solution.py:19
  119.8 1.7 %collective-permute-done.20 = bf16[64,1152]{1,0:T(8,128)(2,1)S(1)} collective-permute-done((bf16[64,1152]{1,0:T(8,128)(2,1)S(1)}, bf16[64,1152]{1,0:T(8,128)(2,1)S(1)}, u32[]{:S(2)}, u32[]{:S(2)}) %collective-permute-start.20) | collective-permute-done | bytes 147488 | tf_op jit(solution)/shard_map/ppermute | solution.py:19
  122.7 5.2 %fusion = f32[256,2048]{1,0:T(8,128)S(1)} fusion(bf16[2,2048,2304]{2,1,0:T(8,128)(2,1)} %bitcast.42, bf16[256,1152]{1,0:T(8,128)(2,1)S(1)} %broadcast_select_fusion.next_ref, bf16[256,1152]{1,0:T(8,128)(2,1)S(1)} %broadcast_select_fusion.1.next_ref), kind=kOutput, calls=%fused_computation.2 | convolution fusion | flops 2418278400 | bytes 12713984 | tf_op jit(solution)/shard_map/dot_general | solution.py:23
  127.9 2.3 %collective-permute-start.31 = (bf16[64,1152]{1,0:T(8,128)(2,1)S(1)}, bf16[64,1152]{1,0:T(8,128)(2,1)S(1)}, u32[]{:S(2)}, u32[]{:S(2)}) collective-permute-start(bf16[64,1152]{1,0:T(8,128)(2,1)S(1)} %get-tuple-element.55), channel_id=1, source_target_pairs={{0,12},{4,8},{8,4},{12,0},{1,13},{5,9},{9,5},{13,1},{2,14},{6,10},... | collective-permute-start | bytes 442376 | tf_op jit(solution)/shard_map/ppermute | solution.py:19
  130.2 2.1 %collective-permute-start.29 = (bf16[64,1152]{1,0:T(8,128)(2,1)S(1)}, bf16[64,1152]{1,0:T(8,128)(2,1)S(1)}, u32[]{:S(2)}, u32[]{:S(2)}) collective-permute-start(bf16[64,1152]{1,0:T(8,128)(2,1)S(1)} %get-tuple-element.55), channel_id=1, source_target_pairs={{0,4},{4,0},{8,12},{12,8},{1,5},{5,1},{9,13},{13,9},{2,6},{6,2},{1... | collective-permute-start | bytes 442376 | tf_op jit(solution)/shard_map/ppermute | solution.py:19
  135.2 8.4 %shard_map.104.rest_0_ = bf16[2048,2,2304]{2,1,0:T(2,128)(2,1)} custom-call(bf16[256,2048]{1,0:T(8,128)(2,1)S(1)} %maximum_convert_fusion.features_ref, bf16[256,1152]{1,0:T(8,128)(2,1)S(1)} %fusion.31.own_ref, bf16[256,1152]{1,0:T(8,128)(2,1)S(1)} %broadcast_select_fusion.1.next_ref), custom_call_target="tpu_custom_call" | custom-call | flops 2415919104 | bytes 11665408 | tf_op jit(solution)/shard_map/pallas_call | solution.py:120
  143.8 6.4 %fusion.18.mine_ref = bf16[256,2048]{1,0:T(8,128)(2,1)S(1)} fusion(f32[256,2048]{1,0:T(8,128)S(1)} %fusion, bf16[2,2048,2304]{2,1,0:T(8,128)(2,1)} %bitcast.43, bf16[256,1152]{1,0:T(8,128)(2,1)S(1)} %maximum_select_fusion.own_ref, bf16[256,1152]{1,0:T(8,128)(2,1)S(1)} %fusion.31.own_ref), kind=kOutput, calls=%fused_computation.17 | convolution fusion | flops 2419326976 | bytes 13762560 | tf_op jit(solution)/shard_map/dot_general | solution.py:23
  150.5 8.4 %shard_map.106 = bf16[2048,2,2304]{2,1,0:T(2,128)(2,1)} custom-call(bf16[256,2048]{1,0:T(8,128)(2,1)S(1)} %maximum_convert_fusion.features_ref, bf16[256,1152]{1,0:T(8,128)(2,1)S(1)} %maximum_select_fusion.own_ref, bf16[256,1152]{1,0:T(8,128)(2,1)S(1)} %broadcast_select_fusion.next_ref, ...), custom_call_target="tpu_custom_call", output_to_operand_aliasing={{}: (3, {})} | custom-call | flops 2415919104 | bytes 11665408 | tf_op jit(solution)/shard_map/pallas_call | solution.py:120
  158.8 5.8 %shard_map.105 = (bf16[2048,2304]{1,0:T(8,128)(2,1)}, f32[1,2048]{1,0:T(1,128)}) custom-call(bf16[256,2048]{1,0:T(8,128)(2,1)S(1)} %fusion.18.mine_ref, bf16[256,2048]{1,0:T(8,128)(2,1)S(1)} %collective-permute-done.32.other_ref, bf16[256,2048]{1,0:T(8,128)(2,1)S(1)} %compare_convert_fusion.live_ref, bf16[256,2304]{1,0:T(8,128)(2,1)S(1)} %convolution_convert_fusion.inputs_ref), custom_call_target="tpu_custom_call" | custom-call | flops 2415919104 | bytes 13762560 | tf_op jit(solution)/shard_map/pallas_call | solution.py:148
  (128 shorter events, 26.4 us)
Async XLA Ops:
  3.2 1.5 collective-permute-start
  4.8 20.6 %collective-permute-start.2 = (bf16[64,2304]{1,0:T(8,128)(2,1)S(1)}, bf16[64,2304]{1,0:T(8,128)(2,1)S(1)}, u32[]{:S(2)}, u32[]{:S(2)}) collective-permute-start(bf16[64,2304]{1,0:T(8,128)(2,1)S(1)} %pad_maximum_fusion.2), channel_id=1, source_target_pairs={{0,8},{4,12},{8,0},{12,4},{1,9},{5,13},{9,1},{13,5},{2,10},{6,14},... | collective-permute-start | bytes 884744 | tf_op jit(solution)/shard_map/ppermute | solution.py:19
  8.9 17.1 %collective-permute-start.1 = (bf16[64,2304]{1,0:T(8,128)(2,1)S(1)}, bf16[64,2304]{1,0:T(8,128)(2,1)S(1)}, u32[]{:S(2)}, u32[]{:S(2)}) collective-permute-start(bf16[64,2304]{1,0:T(8,128)(2,1)S(1)} %pad_maximum_fusion.2), channel_id=1, source_target_pairs={{0,4},{4,0},{8,12},{12,8},{1,5},{5,1},{9,13},{13,9},{2,6},{6,2},{1... | collective-permute-start | bytes 884744 | tf_op jit(solution)/shard_map/ppermute | solution.py:19
  10.7 1.6 collective-permute-start.5
  25.4 9.3 %collective-permute-start.3 = (bf16[64,2304]{1,0:T(8,128)(2,1)S(1)}, bf16[64,2304]{1,0:T(8,128)(2,1)S(1)}, u32[]{:S(2)}, u32[]{:S(2)}) collective-permute-start(bf16[64,2304]{1,0:T(8,128)(2,1)S(1)} %collective-permute-done.2), channel_id=1, source_target_pairs={{0,4},{4,0},{8,12},{12,8},{1,5},{5,1},{9,13},{13,9},{2,6},{6,2},{1... | collective-permute-start | bytes 884744 | tf_op jit(solution)/shard_map/ppermute | solution.py:19
  41.3 4.2 %collective-permute-start.6 = (f32[256,2048]{1,0:T(8,128)S(1)}, f32[256,2048]{1,0:T(8,128)S(1)}, u32[]{:S(2)}, u32[]{:S(2)}) collective-permute-start(f32[256,2048]{1,0:T(8,128)S(1)} %shard_map.102), channel_id=1, source_target_pairs={{0,1},{1,0},{2,3},{3,2},{4,5},{5,4},{6,7},{7,6},{8,9},{9,8},{10,11... | collective-permute-start | bytes 6291464 | tf_op jit(solution)/shard_map/ppermute | solution.py:15
  52.7 16.7 %collective-permute-start.8 = (bf16[256,1152]{1,0:T(8,128)(2,1)}, bf16[256,1152]{1,0:T(8,128)(2,1)}, u32[]{:S(2)}, u32[]{:S(2)}) collective-permute-start(bf16[256,1152]{1,0:T(8,128)(2,1)} %slice.181), channel_id=1, source_target_pairs={{0,2},{1,3},{4,6},{5,7},{8,10},{9,11},{12,14},{13,15},{16,18},{17,... | collective-permute-start | bytes 1769480 | tf_op jit(solution)/shard_map/ppermute | solution.py:267
  59.0 7.0 %collective-permute-start.7 = (bf16[64,1152]{1,0:T(8,128)(2,1)}, bf16[64,1152]{1,0:T(8,128)(2,1)}, u32[]{:S(2)}, u32[]{:S(2)}) collective-permute-start(bf16[64,1152]{1,0:T(8,128)(2,1)} %get-tuple-element.87), channel_id=1, source_target_pairs={{0,4},{4,0},{8,12},{12,8},{1,5},{5,1},{9,13},{13,9},{2,6},{6,2},{1... | collective-permute-start | bytes 442376 | tf_op jit(solution)/shard_map/ppermute | solution.py:19
  60.9 14.2 %collective-permute-start.13 = (bf16[64,1152]{1,0:T(8,128)(2,1)S(1)}, bf16[64,1152]{1,0:T(8,128)(2,1)S(1)}, u32[]{:S(2)}, u32[]{:S(2)}) collective-permute-start(bf16[64,1152]{1,0:T(8,128)(2,1)S(1)} %copy-done.5), channel_id=1, source_target_pairs={{0,8},{4,12},{8,0},{12,4},{1,9},{5,13},{9,1},{13,5},{2,10},{6,14},... | collective-permute-start | bytes 442376 | tf_op jit(solution)/shard_map/ppermute | solution.py:19
  61.3 13.8 %collective-permute-start.14 = (bf16[64,1152]{1,0:T(8,128)(2,1)S(1)}, bf16[64,1152]{1,0:T(8,128)(2,1)S(1)}, u32[]{:S(2)}, u32[]{:S(2)}) collective-permute-start(bf16[64,1152]{1,0:T(8,128)(2,1)S(1)} %get-tuple-element.86), channel_id=1, source_target_pairs={{0,12},{4,8},{8,4},{12,0},{1,13},{5,9},{9,5},{13,1},{2,14},{6,10},... | collective-permute-start | bytes 442376 | tf_op jit(solution)/shard_map/ppermute | solution.py:19
  71.5 8.5 %collective-permute-start.9 = (bf16[64,1152]{1,0:T(8,128)(2,1)S(1)}, bf16[64,1152]{1,0:T(8,128)(2,1)S(1)}, u32[]{:S(2)}, u32[]{:S(2)}) collective-permute-start(bf16[64,1152]{1,0:T(8,128)(2,1)S(1)} %get-tuple-element.88), channel_id=1, source_target_pairs={{0,4},{4,0},{8,12},{12,8},{1,5},{5,1},{9,13},{13,9},{2,6},{6,2},{1... | collective-permute-start | bytes 442376 | tf_op jit(solution)/shard_map/ppermute | solution.py:19
  72.0 8.8 %collective-permute-start.11 = (bf16[64,1152]{1,0:T(8,128)(2,1)S(1)}, bf16[64,1152]{1,0:T(8,128)(2,1)S(1)}, u32[]{:S(2)}, u32[]{:S(2)}) collective-permute-start(bf16[64,1152]{1,0:T(8,128)(2,1)S(1)} %get-tuple-element.89), channel_id=1, source_target_pairs={{0,12},{4,8},{8,4},{12,0},{1,13},{5,9},{9,5},{13,1},{2,14},{6,10},... | collective-permute-start | bytes 442376 | tf_op jit(solution)/shard_map/ppermute | solution.py:19
  73.3 16.1 %collective-permute-start.10 = (bf16[64,1152]{1,0:T(8,128)(2,1)S(1)}, bf16[64,1152]{1,0:T(8,128)(2,1)S(1)}, u32[]{:S(2)}, u32[]{:S(2)}) collective-permute-start(bf16[64,1152]{1,0:T(8,128)(2,1)S(1)} %get-tuple-element.90), channel_id=1, source_target_pairs={{0,8},{4,12},{8,0},{12,4},{1,9},{5,13},{9,1},{13,5},{2,10},{6,14},... | collective-permute-start | bytes 442376 | tf_op jit(solution)/shard_map/ppermute | solution.py:19
  76.1 19.0 %collective-permute-start.15 = (f32[64,1152]{1,0:T(8,128)S(1)}, f32[64,1152]{1,0:T(8,128)S(1)}, u32[]{:S(2)}, u32[]{:S(2)}) collective-permute-start(f32[64,1152]{1,0:T(8,128)S(1)} %fusion.36), channel_id=1, source_target_pairs={{0,2},{2,0},{1,3},{3,1},{4,6},{6,4},{5,7},{7,5},{8,10},{10,8},{9,1... | collective-permute-start | bytes 884744 | tf_op jit(solution)/shard_map/ppermute | solution.py:15
  89.6 14.2 %collective-permute-start.22 = (bf16[64,1152]{1,0:T(8,128)(2,1)S(1)}, bf16[64,1152]{1,0:T(8,128)(2,1)S(1)}, u32[]{:S(2)}, u32[]{:S(2)}) collective-permute-start(bf16[64,1152]{1,0:T(8,128)(2,1)S(1)} %get-tuple-element.81), channel_id=1, source_target_pairs={{0,12},{4,8},{8,4},{12,0},{1,13},{5,9},{9,5},{13,1},{2,14},{6,10},... | collective-permute-start | bytes 442376 | tf_op jit(solution)/shard_map/ppermute | solution.py:19
  90.9 10.9 %collective-permute-start.12 = (bf16[64,1152]{1,0:T(8,128)(2,1)S(1)}, bf16[64,1152]{1,0:T(8,128)(2,1)S(1)}, u32[]{:S(2)}, u32[]{:S(2)}) collective-permute-start(bf16[64,1152]{1,0:T(8,128)(2,1)S(1)} %get-tuple-element.82), channel_id=1, source_target_pairs={{0,4},{4,0},{8,12},{12,8},{1,5},{5,1},{9,13},{13,9},{2,6},{6,2},{1... | collective-permute-start | bytes 442376 | tf_op jit(solution)/shard_map/ppermute | solution.py:19
  90.9 12.9 %collective-permute-start.21 = (bf16[64,1152]{1,0:T(8,128)(2,1)S(1)}, bf16[64,1152]{1,0:T(8,128)(2,1)S(1)}, u32[]{:S(2)}, u32[]{:S(2)}) collective-permute-start(bf16[64,1152]{1,0:T(8,128)(2,1)S(1)} %get-tuple-element.69), channel_id=1, source_target_pairs={{0,8},{4,12},{8,0},{12,4},{1,9},{5,13},{9,1},{13,5},{2,10},{6,14},... | collective-permute-start | bytes 442376 | tf_op jit(solution)/shard_map/ppermute | solution.py:19
  94.2 14.7 %collective-permute-start.17 = (bf16[64,1152]{1,0:T(8,128)(2,1)S(1)}, bf16[64,1152]{1,0:T(8,128)(2,1)S(1)}, u32[]{:S(2)}, u32[]{:S(2)}) collective-permute-start(bf16[64,1152]{1,0:T(8,128)(2,1)S(1)} %fusion.48), channel_id=1, source_target_pairs={{0,2},{2,0},{1,3},{3,1},{4,6},{6,4},{5,7},{7,5},{8,10},{10,8},{9,1... | collective-permute-start | bytes 442376 | tf_op jit(solution)/shard_map/ppermute | solution.py:15
  101.8 13.4 %collective-permute-start.19 = (bf16[64,1152]{1,0:T(8,128)(2,1)S(1)}, bf16[64,1152]{1,0:T(8,128)(2,1)S(1)}, u32[]{:S(2)}, u32[]{:S(2)}) collective-permute-start(bf16[64,1152]{1,0:T(8,128)(2,1)S(1)} %get-tuple-element.45), channel_id=1, source_target_pairs={{0,8},{4,12},{8,0},{12,4},{1,9},{5,13},{9,1},{13,5},{2,10},{6,14},... | collective-permute-start | bytes 442376 | tf_op jit(solution)/shard_map/ppermute | solution.py:19
  101.8 10.2 %collective-permute-start.16 = (bf16[64,1152]{1,0:T(8,128)(2,1)S(1)}, bf16[64,1152]{1,0:T(8,128)(2,1)S(1)}, u32[]{:S(2)}, u32[]{:S(2)}) collective-permute-start(bf16[64,1152]{1,0:T(8,128)(2,1)S(1)} %get-tuple-element.45), channel_id=1, source_target_pairs={{0,4},{4,0},{8,12},{12,8},{1,5},{5,1},{9,13},{13,9},{2,6},{6,2},{1... | collective-permute-start | bytes 442376 | tf_op jit(solution)/shard_map/ppermute | solution.py:19
  104.9 10.2 %collective-permute-start.24 = (bf16[64,1152]{1,0:T(8,128)(2,1)S(1)}, bf16[64,1152]{1,0:T(8,128)(2,1)S(1)}, u32[]{:S(2)}, u32[]{:S(2)}) collective-permute-start(bf16[64,1152]{1,0:T(8,128)(2,1)S(1)} %get-tuple-element.80), channel_id=1, source_target_pairs={{0,2},{1,3},{4,6},{5,7},{8,10},{9,11},{12,14},{13,15},{16,18},{17,... | collective-permute-start | bytes 442376 | tf_op jit(solution)/shard_map/ppermute | solution.py:294
  107.5 15.0 %collective-permute-start.23 = (bf16[256,1152]{1,0:T(8,128)(2,1)S(1)}, bf16[256,1152]{1,0:T(8,128)(2,1)S(1)}, u32[]{:S(2)}, u32[]{:S(2)}) collective-permute-start(bf16[256,1152]{1,0:T(8,128)(2,1)S(1)} %fusion.28), channel_id=1, source_target_pairs={{2,0},{3,1},{6,4},{7,5},{10,8},{11,9},{14,12},{15,13},{18,16},{19,... | collective-permute-start | bytes 1769480 | tf_op jit(solution)/shard_map/ppermute | solution.py:287
  112.0 7.5 %collective-permute-start.27 = (bf16[64,1152]{1,0:T(8,128)(2,1)S(1)}, bf16[64,1152]{1,0:T(8,128)(2,1)S(1)}, u32[]{:S(2)}, u32[]{:S(2)}) collective-permute-start(bf16[64,1152]{1,0:T(8,128)(2,1)S(1)} %get-tuple-element.46), channel_id=1, source_target_pairs={{0,8},{4,12},{8,0},{12,4},{1,9},{5,13},{9,1},{13,5},{2,10},{6,14},... | collective-permute-start | bytes 442376 | tf_op jit(solution)/shard_map/ppermute | solution.py:19
  112.0 15.9 %collective-permute-start.18 = (bf16[64,1152]{1,0:T(8,128)(2,1)S(1)}, bf16[64,1152]{1,0:T(8,128)(2,1)S(1)}, u32[]{:S(2)}, u32[]{:S(2)}) collective-permute-start(bf16[64,1152]{1,0:T(8,128)(2,1)S(1)} %get-tuple-element.46), channel_id=1, source_target_pairs={{0,4},{4,0},{8,12},{12,8},{1,5},{5,1},{9,13},{13,9},{2,6},{6,2},{1... | collective-permute-start | bytes 442376 | tf_op jit(solution)/shard_map/ppermute | solution.py:19
  115.2 6.3 %collective-permute-start.20 = (bf16[64,1152]{1,0:T(8,128)(2,1)S(1)}, bf16[64,1152]{1,0:T(8,128)(2,1)S(1)}, u32[]{:S(2)}, u32[]{:S(2)}) collective-permute-start(bf16[64,1152]{1,0:T(8,128)(2,1)S(1)} %collective-permute-done.19), channel_id=1, source_target_pairs={{0,4},{4,0},{8,12},{12,8},{1,5},{5,1},{9,13},{13,9},{2,6},{6,2},{1... | collective-permute-start | bytes 442376 | tf_op jit(solution)/shard_map/ppermute | solution.py:19
  119.6 12.9 %collective-permute-start.28 = (bf16[64,1152]{1,0:T(8,128)(2,1)S(1)}, bf16[64,1152]{1,0:T(8,128)(2,1)S(1)}, u32[]{:S(2)}, u32[]{:S(2)}) collective-permute-start(bf16[64,1152]{1,0:T(8,128)(2,1)S(1)} %collective-permute-done.27), channel_id=1, source_target_pairs={{0,4},{4,0},{8,12},{12,8},{1,5},{5,1},{9,13},{13,9},{2,6},{6,2},{1... | collective-permute-start | bytes 442376 | tf_op jit(solution)/shard_map/ppermute | solution.py:19
  127.9 15.7 %collective-permute-start.31 = (bf16[64,1152]{1,0:T(8,128)(2,1)S(1)}, bf16[64,1152]{1,0:T(8,128)(2,1)S(1)}, u32[]{:S(2)}, u32[]{:S(2)}) collective-permute-start(bf16[64,1152]{1,0:T(8,128)(2,1)S(1)} %get-tuple-element.55), channel_id=1, source_target_pairs={{0,12},{4,8},{8,4},{12,0},{1,13},{5,9},{9,5},{13,1},{2,14},{6,10},... | collective-permute-start | bytes 442376 | tf_op jit(solution)/shard_map/ppermute | solution.py:19
  130.2 13.3 %collective-permute-start.30 = (bf16[64,1152]{1,0:T(8,128)(2,1)S(1)}, bf16[64,1152]{1,0:T(8,128)(2,1)S(1)}, u32[]{:S(2)}, u32[]{:S(2)}) collective-permute-start(bf16[64,1152]{1,0:T(8,128)(2,1)S(1)} %get-tuple-element.55), channel_id=1, source_target_pairs={{0,8},{4,12},{8,0},{12,4},{1,9},{5,13},{9,1},{13,5},{2,10},{6,14},... | collective-permute-start | bytes 442376 | tf_op jit(solution)/shard_map/ppermute | solution.py:19
  130.2 13.3 %collective-permute-start.29 = (bf16[64,1152]{1,0:T(8,128)(2,1)S(1)}, bf16[64,1152]{1,0:T(8,128)(2,1)S(1)}, u32[]{:S(2)}, u32[]{:S(2)}) collective-permute-start(bf16[64,1152]{1,0:T(8,128)(2,1)S(1)} %get-tuple-element.55), channel_id=1, source_target_pairs={{0,4},{4,0},{8,12},{12,8},{1,5},{5,1},{9,13},{13,9},{2,6},{6,2},{1... | collective-permute-start | bytes 442376 | tf_op jit(solution)/shard_map/ppermute | solution.py:19
  132.4 1.4 collective-permute-start.26
  132.5 1.6 collective-permute-start.25
  150.1 8.7 %collective-permute-start.32 = (bf16[256,2048]{1,0:T(8,128)(2,1)S(1)}, bf16[256,2048]{1,0:T(8,128)(2,1)S(1)}, u32[]{:S(2)}, u32[]{:S(2)}) collective-permute-start(bf16[256,2048]{1,0:T(8,128)(2,1)S(1)} %fusion.18.mine_ref), channel_id=1, source_target_pairs={{0,1},{1,0},{2,3},{3,2},{4,5},{5,4},{6,7},{7,6},{8,9},{9,8},{10,11... | collective-permute-start | bytes 3145736 | tf_op jit(solution)/shard_map/ppermute | solution.py:15
  (13 other events, 161.2 us)

commit v4 on v3

--- a/solution.py
+++ b/solution.py
@@ -49,10 +49,11 @@
     return pltpu.CompilerParams(vmem_limit_bytes=24 * 1024 * 1024)
 
 
-def encoder_kernel(inputs_ref, weight_ref, out_ref):
-    count, half = weight_ref.shape
-    rows = inputs_ref.shape[0]
+def encoder_kernel(part, inputs_ref, weight_ref, out_ref):
+    rows, count = out_ref.shape
+    half = weight_ref.shape[1]
     block = min(256, count)
+    first = part * (count // block)
 
     def product(weight_block, out_block):
         out_block[...] = dot_last(inputs_ref[...], weight_block[...])
@@ -60,15 +61,15 @@
     pltpu.emit_pipeline(
         product,
         grid=(count // block,),
-        in_specs=[pl.BlockSpec((block, half), lambda i: (i, 0))],
+        in_specs=[pl.BlockSpec((block, half), lambda i: (first + i, 0))],
         out_specs=[pl.BlockSpec((rows, block), lambda i: (0, i))],
     )(weight_ref, out_ref)
 
 
-def encoder_call(inputs, weight):
-    rows, count = inputs.shape[0], weight.shape[0]
+def encoder_call(inputs, weight, part, parts):
+    rows, count = inputs.shape[0], weight.shape[0] // parts
     return pl.pallas_call(
-        encoder_kernel,
+        functools.partial(encoder_kernel, part),
         in_specs=[
             pl.BlockSpec(memory_space=pltpu.VMEM),
             pl.BlockSpec(memory_space=pltpu.HBM),
@@ -230,8 +231,13 @@
 
     bias_half = lax.dynamic_slice_in_dim(dec_bias, row_pos * half, half, axis=1)
 
-    partial_pre = encoder_call(inputs, enc_weight[0])
-    pre = partial_pre + shifted(partial_pre, "row", 1) + enc_bias
+    feature_count = enc_weight.shape[1]
+    parts = 2 if feature_count % 512 == 0 else 1
+    sums = []
+    for part in range(parts):
+        partial_pre = encoder_call(inputs, enc_weight[0], part, parts)
+        sums.append(partial_pre + shifted(partial_pre, "row", 1))
+    pre = jnp.concatenate(sums, axis=1) + enc_bias
     features, live = lax.optimization_barrier(
         (jnp.maximum(pre, 0.0).astype(bf16), (pre > 0).astype(bf16))
     )
@@ -264,10 +270,11 @@
         return (recon - mlp_half[t][:, cols].astype(f32)).astype(bf16)
 
     last = layers - 1
-    carried = lax.ppermute(next_part[:, high], "layer", forward)
     low_part = jnp.where(leading, next_part[:, low].astype(f32), own_part[:, low])
     low_sent = low_part.astype(bf16)
+    low_sent, next_high_part = lax.optimization_barrier((low_sent, next_part[:, high]))
     low_moved = move(lambda k: rows_of(low_sent, k))
+    carried = lax.ppermute(next_high_part, "layer", forward)
     low_moved[near], carried = lax.optimization_barrier((low_moved[near], carried))
     second_part = jnp.where(leading, own_part[:, low], own_part[:, high] + carried.astype(f32))
     second_sent = second_part.astype(bf16)

time: 165 us -> 164 us (level)
  waiting for transfers between devices: 46.9 us -> 37.9 us
  starting transfers between devices: 42.2 us -> 50.5 us
    ppermute x21, waiting for transfers between devices: 36.3 us -> 28.6 us  [swapped(): lax.ppermute(block, axis, [(i, i ^ distance) for i in range(lax.axis_size...]
    ppermute x21, starting transfers between devices: 28.4 us -> 35.2 us  [swapped(): lax.ppermute(block, axis, [(i, i ^ distance) for i in range(lax.axis_size...]
    ppermute x9 -> x10, waiting for transfers between devices: 6.13 us -> 4.12 us  [shifted(): lax.ppermute(block, axis, [(i, (i + distance) % count) for i in range(cou...]
    ppermute x9 -> x10, starting transfers between devices: 5.61 us -> 7.51 us  [shifted(): lax.ppermute(block, axis, [(i, (i + distance) % count) for i in range(cou...]
    pallas_call x1 -> x2, Pallas kernels: 5.91 us -> 5.93 us  [encoder_call(): pl.pallas_call(functools.partial(encoder_kernel, part), in_specs=[pl.Bloc...]
  transfers between devices with their start and end apart: 33 -> 34, of which waited for: 17 -> 17; matrix products, arithmetic and copies ran while one was open for 17% -> 16% of each run, Pallas kernels for 11% -> 13%
where the time goes in v4:
time: 164 us
  starting transfers between devices  50.5 us (31%)
  waiting for transfers between devices  37.9 us (23%)
  Pallas kernels  29.5 us (18%)
  local copies, waits for them, and re-layouts  18.7 us (11%)
  matrix products  17.5 us (11%)
  other arithmetic  8.49 us (5%)
    ppermute x21, starting transfers between devices, swapped(): lax.ppermute(block, axis, [(i, i ^ distance) for i in range(lax.axis_size...  35.2 us
    ppermute x21, waiting for transfers between devices, swapped(): lax.ppermute(block, axis, [(i, i ^ distance) for i in range(lax.axis_size...  28.6 us
    pallas_call x2, Pallas kernels, dec_grad_call(): pl.pallas_call(functools.partial(dec_grad_kernel, scale), grid=(count //...  16.7 us
    optimization_barrier x1, local copies, waits for them, and re-layouts, on_device(): mlp_half, dec_weight = lax.optimization_barrier((mlp_half, dec_weight))  12.3 us
    dot_general x2, matrix products, dot_last(): lax.dot_general(left, right, (((1,), (1,)), ((), ())), preferred_element_...  11.6 us
    ppermute x10, starting transfers between devices, shifted(): lax.ppermute(block, axis, [(i, (i + distance) % count) for i in range(cou...  7.51 us
    pallas_call x2, Pallas kernels, encoder_call(): pl.pallas_call(functools.partial(encoder_kernel, part), in_specs=[pl.Bloc...  5.93 us
    pallas_call x1, Pallas kernels, enc_grad_call(): pl.pallas_call(functools.partial(enc_grad_kernel, scale), grid=(count //...  5.8 us
  transfers between devices with their start and end apart: 34, of which 17 were waited for; matrix products, arithmetic and copies ran while one was open for 16% of the time, Pallas kernels for 13%

profile of v4, /device:TPU:0, one launch (start us, length us, event | category | flops | bytes accessed | tf_op | source)
XLA Modules:
  0.0 163.9 jit_solution(11298473611718041300)
XLA Ops:
  0.6 2.4 %fusion.54 = (bf16[32,1,4608]{2,1,0:T(2,128)(2,1)S(1)}, bf16[32,1,4608]{2,1,0:T(2,128)(2,1)S(1)}) fusion(bf16[32,2,4608]{2,1,0:T(2,128)(2,1)} %param.7), kind=kLoop, calls=%fused_computation.128 | loop fusion | bytes 1179648 | tf_op jit(solution)/shard_map/slice | solution.py:216
  4.8 4.0 %collective-permute-start.2 = (bf16[64,2304]{1,0:T(8,128)(2,1)S(1)}, bf16[64,2304]{1,0:T(8,128)(2,1)S(1)}, u32[]{:S(2)}, u32[]{:S(2)}) collective-permute-start(bf16[64,2304]{1,0:T(8,128)(2,1)S(1)} %pad_maximum_fusion.2), channel_id=1, source_target_pairs={{0,8},{4,12},{8,0},{12,4},{1,9},{5,13},{9,1},{13,5},{2,10},{6,14},... | collective-permute-start | bytes 884744 | tf_op jit(solution)/shard_map/ppermute | solution.py:19
  8.9 1.6 collective-permute-start.1
  13.1 12.3 %copy.28 = bf16[1,2048,2,2304]{3,1,2,0:T(8,128)(2,1)S(1)} copy(bf16[1,2048,2,2304]{3,2,1,0:T(2,128)(2,1)} %param.11) | data formatting | bytes 37748736 | tf_op jit(solution)/shard_map/optimization_barrier | solution.py:221
  26.0 8.8 %collective-permute-done.3 = bf16[64,2304]{1,0:T(8,128)(2,1)S(1)} collective-permute-done((bf16[64,2304]{1,0:T(8,128)(2,1)S(1)}, bf16[64,2304]{1,0:T(8,128)(2,1)S(1)}, u32[]{:S(2)}, u32[]{:S(2)}) %collective-permute-start.3) | collective-permute-done | bytes 294944 | tf_op jit(solution)/shard_map/ppermute | solution.py:19
  35.4 3.0 %shard_map.102 = f32[256,1024]{1,0:T(8,128)S(1)} custom-call(bf16[256,2304]{1,0:T(8,128)(2,1)S(1)} %convolution_convert_fusion.inputs_ref, bf16[2048,2304]{1,0:T(8,128)(2,1)S(1)} %bitcast.38), custom_call_target="tpu_custom_call" | custom-call | tf_op jit(solution)/shard_map/pallas_call | solution.py:71
  38.4 3.0 %shard_map.103 = f32[256,1024]{1,0:T(8,128)S(1)} custom-call(bf16[256,2304]{1,0:T(8,128)(2,1)S(1)} %convolution_convert_fusion.inputs_ref, bf16[2048,2304]{1,0:T(8,128)(2,1)S(1)} %bitcast.39), custom_call_target="tpu_custom_call" | custom-call | tf_op jit(solution)/shard_map/pallas_call | solution.py:71
  42.1 2.1 %collective-permute-done.7 = f32[256,1024]{1,0:T(8,128)S(1)} collective-permute-done((f32[256,1024]{1,0:T(8,128)S(1)}, f32[256,1024]{1,0:T(8,128)S(1)}, u32[]{:S(2)}, u32[]{:S(2)}) %collective-permute-start.7) | collective-permute-done | bytes 1048608 | tf_op jit(solution)/shard_map/ppermute | solution.py:15
  44.9 2.7 %fusion.12 = bf16[256,2304]{1,0:T(8,128)(2,1)S(1)} fusion(bf16[256,2048]{1,0:T(8,128)(2,1)S(1)} %maximum_convert_fusion.features_ref, bf16[2,2048,2304]{2,1,0:T(8,128)(2,1)S(1)} %bitcast.41), kind=kOutput, calls=%fused_computation.14 | convolution fusion | flops 2416508928 | bytes 11665408 | tf_op jit(solution)/shard_map/dot_general | solution.py:245
  47.6 2.7 %fusion.6 = f32[256,2304]{1,0:T(8,128)S(1)} fusion(bf16[256,2048]{1,0:T(8,128)(2,1)S(1)} %maximum_convert_fusion.features_ref, bf16[2,2048,2304]{2,1,0:T(8,128)(2,1)S(1)} %bitcast.42), kind=kOutput, calls=%fused_computation.8 | convolution fusion | flops 2415919104 | bytes 12845056 | tf_op jit(solution)/shard_map/dot_general | solution.py:246
  52.4 4.2 %collective-permute-start.9 = (bf16[256,1152]{1,0:T(8,128)(2,1)}, bf16[256,1152]{1,0:T(8,128)(2,1)}, u32[]{:S(2)}, u32[]{:S(2)}) collective-permute-start(bf16[256,1152]{1,0:T(8,128)(2,1)} %slice.180), channel_id=1, source_target_pairs={{0,2},{1,3},{4,6},{5,7},{8,10},{9,11},{12,14},{13,15},{16,18},{17,... | collective-permute-start | bytes 1769480 | tf_op jit(solution)/shard_map/ppermute | solution.py:277
  59.7 3.6 %collective-permute-start.15 = (bf16[64,1152]{1,0:T(8,128)(2,1)S(1)}, bf16[64,1152]{1,0:T(8,128)(2,1)S(1)}, u32[]{:S(2)}, u32[]{:S(2)}) collective-permute-start(bf16[64,1152]{1,0:T(8,128)(2,1)S(1)} %get-tuple-element.90), channel_id=1, source_target_pairs={{0,12},{4,8},{8,4},{12,0},{1,13},{5,9},{9,5},{13,1},{2,14},{6,10},... | collective-permute-start | bytes 442376 | tf_op jit(solution)/shard_map/ppermute | solution.py:19
  64.6 4.6 %collective-permute-done.9 = bf16[256,1152]{1,0:T(8,128)(2,1)} collective-permute-done((bf16[256,1152]{1,0:T(8,128)(2,1)}, bf16[256,1152]{1,0:T(8,128)(2,1)}, u32[]{:S(2)}, u32[]{:S(2)}) %collective-permute-start.9) | collective-permute-done | bytes 589856 | tf_op jit(solution)/shard_map/ppermute | solution.py:277
  69.2 2.0 %fusion.50 = (bf16[256,1152]{1,0:T(8,128)(2,1)S(1)}, f32[256,1152]{1,0:T(8,128)S(1)}) fusion(bf16[256,1152]{1,0:T(8,128)(2,1)} %collective-permute-done.9, f32[256,2304]{1,0:T(8,128)} %copy-done.1, pred[]{:T(512)S(6)} %lt.27), kind=kLoop, calls=%fused_computation.124 | loop fusion | flops 1179648 | bytes 4718593 | tf_op jit(solution)/shard_map/convert_element_type | solution.py:280
  73.1 1.7 %collective-permute-start.11 = (bf16[64,1152]{1,0:T(8,128)(2,1)S(1)}, bf16[64,1152]{1,0:T(8,128)(2,1)S(1)}, u32[]{:S(2)}, u32[]{:S(2)}) collective-permute-start(bf16[64,1152]{1,0:T(8,128)(2,1)S(1)} %get-tuple-element.94), channel_id=1, source_target_pairs={{0,8},{4,12},{8,0},{12,4},{1,9},{5,13},{9,1},{13,5},{2,10},{6,14},... | collective-permute-start | bytes 442376 | tf_op jit(solution)/shard_map/ppermute | solution.py:19
  75.9 2.5 %collective-permute-start.16 = (f32[64,1152]{1,0:T(8,128)S(1)}, f32[64,1152]{1,0:T(8,128)S(1)}, u32[]{:S(2)}, u32[]{:S(2)}) collective-permute-start(f32[64,1152]{1,0:T(8,128)S(1)} %fusion.36), channel_id=1, source_target_pairs={{0,2},{2,0},{1,3},{3,1},{4,6},{6,4},{5,7},{7,5},{8,10},{10,8},{9,1... | collective-permute-start | bytes 884744 | tf_op jit(solution)/shard_map/ppermute | solution.py:15
  79.0 1.6 %collective-permute-done.12 = bf16[64,1152]{1,0:T(8,128)(2,1)S(1)} collective-permute-done((bf16[64,1152]{1,0:T(8,128)(2,1)S(1)}, bf16[64,1152]{1,0:T(8,128)(2,1)S(1)}, u32[]{:S(2)}, u32[]{:S(2)}) %collective-permute-start.12) | collective-permute-done | bytes 147488 | tf_op jit(solution)/shard_map/ppermute | solution.py:19
  80.6 7.4 %collective-permute-done.11 = bf16[64,1152]{1,0:T(8,128)(2,1)S(1)} collective-permute-done((bf16[64,1152]{1,0:T(8,128)(2,1)S(1)}, bf16[64,1152]{1,0:T(8,128)(2,1)S(1)}, u32[]{:S(2)}, u32[]{:S(2)}) %collective-permute-start.11) | collective-permute-done | bytes 147488 | tf_op jit(solution)/shard_map/ppermute | solution.py:19
  89.6 3.1 %collective-permute-start.22 = (bf16[64,1152]{1,0:T(8,128)(2,1)S(1)}, bf16[64,1152]{1,0:T(8,128)(2,1)S(1)}, u32[]{:S(2)}, u32[]{:S(2)}) collective-permute-start(bf16[64,1152]{1,0:T(8,128)(2,1)S(1)} %get-tuple-element.73), channel_id=1, source_target_pairs={{0,8},{4,12},{8,0},{12,4},{1,9},{5,13},{9,1},{13,5},{2,10},{6,14},... | collective-permute-start | bytes 442376 | tf_op jit(solution)/shard_map/ppermute | solution.py:19
  92.7 2.2 %collective-permute-start.18 = (bf16[64,1152]{1,0:T(8,128)(2,1)S(1)}, bf16[64,1152]{1,0:T(8,128)(2,1)S(1)}, u32[]{:S(2)}, u32[]{:S(2)}) collective-permute-start(bf16[64,1152]{1,0:T(8,128)(2,1)S(1)} %fusion.48), channel_id=1, source_target_pairs={{0,2},{2,0},{1,3},{3,1},{4,6},{6,4},{5,7},{7,5},{8,10},{10,8},{9,1... | collective-permute-start | bytes 442376 | tf_op jit(solution)/shard_map/ppermute | solution.py:15
  95.1 5.6 %collective-permute-done.13 = bf16[64,1152]{1,0:T(8,128)(2,1)S(1)} collective-permute-done((bf16[64,1152]{1,0:T(8,128)(2,1)S(1)}, bf16[64,1152]{1,0:T(8,128)(2,1)S(1)}, u32[]{:S(2)}, u32[]{:S(2)}) %collective-permute-start.13) | collective-permute-done | bytes 147488 | tf_op jit(solution)/shard_map/ppermute | solution.py:19
  100.7 2.2 %collective-permute-start.17 = (bf16[64,1152]{1,0:T(8,128)(2,1)S(1)}, bf16[64,1152]{1,0:T(8,128)(2,1)S(1)}, u32[]{:S(2)}, u32[]{:S(2)}) collective-permute-start(bf16[64,1152]{1,0:T(8,128)(2,1)S(1)} %get-tuple-element.49), channel_id=1, source_target_pairs={{0,4},{4,0},{8,12},{12,8},{1,5},{5,1},{9,13},{13,9},{2,6},{6,2},{1... | collective-permute-start | bytes 442376 | tf_op jit(solution)/shard_map/ppermute | solution.py:19
  104.0 2.3 %collective-permute-start.25 = (bf16[64,1152]{1,0:T(8,128)(2,1)S(1)}, bf16[64,1152]{1,0:T(8,128)(2,1)S(1)}, u32[]{:S(2)}, u32[]{:S(2)}) collective-permute-start(bf16[64,1152]{1,0:T(8,128)(2,1)S(1)} %get-tuple-element.84), channel_id=1, source_target_pairs={{0,2},{1,3},{4,6},{5,7},{8,10},{9,11},{12,14},{13,15},{16,18},{17,... | collective-permute-start | bytes 442376 | tf_op jit(solution)/shard_map/ppermute | solution.py:301
  107.7 1.6 collective-permute-done.17
  110.0 4.9 %collective-permute-start.19 = (bf16[64,1152]{1,0:T(8,128)(2,1)S(1)}, bf16[64,1152]{1,0:T(8,128)(2,1)S(1)}, u32[]{:S(2)}, u32[]{:S(2)}) collective-permute-start(bf16[64,1152]{1,0:T(8,128)(2,1)S(1)} %get-tuple-element.50), channel_id=1, source_target_pairs={{0,4},{4,0},{8,12},{12,8},{1,5},{5,1},{9,13},{13,9},{2,6},{6,2},{1... | collective-permute-start | bytes 442376 | tf_op jit(solution)/shard_map/ppermute | solution.py:19
  115.5 4.2 %collective-permute-start.29 = (bf16[64,1152]{1,0:T(8,128)(2,1)S(1)}, bf16[64,1152]{1,0:T(8,128)(2,1)S(1)}, u32[]{:S(2)}, u32[]{:S(2)}) collective-permute-start(bf16[64,1152]{1,0:T(8,128)(2,1)S(1)} %collective-permute-done.28), channel_id=1, source_target_pairs={{0,4},{4,0},{8,12},{12,8},{1,5},{5,1},{9,13},{13,9},{2,6},{6,2},{1... | collective-permute-start | bytes 442376 | tf_op jit(solution)/shard_map/ppermute | solution.py:19
  121.9 5.2 %fusion = f32[256,2048]{1,0:T(8,128)S(1)} fusion(bf16[2,2048,2304]{2,1,0:T(8,128)(2,1)} %bitcast.43, bf16[256,1152]{1,0:T(8,128)(2,1)S(1)} %broadcast_select_fusion.next_ref, bf16[256,1152]{1,0:T(8,128)(2,1)S(1)} %broadcast_select_fusion.1.next_ref), kind=kOutput, calls=%fused_computation.2 | convolution fusion | flops 2418278400 | bytes 12713984 | tf_op jit(solution)/shard_map/dot_general | solution.py:23
  127.2 3.0 %collective-permute-start.32 = (bf16[64,1152]{1,0:T(8,128)(2,1)S(1)}, bf16[64,1152]{1,0:T(8,128)(2,1)S(1)}, u32[]{:S(2)}, u32[]{:S(2)}) collective-permute-start(bf16[64,1152]{1,0:T(8,128)(2,1)S(1)} %get-tuple-element.59), channel_id=1, source_target_pairs={{0,12},{4,8},{8,4},{12,0},{1,13},{5,9},{9,5},{13,1},{2,14},{6,10},... | collective-permute-start | bytes 442376 | tf_op jit(solution)/shard_map/ppermute | solution.py:19
  134.5 8.4 %shard_map.105.rest_0_ = bf16[2048,2,2304]{2,1,0:T(2,128)(2,1)} custom-call(bf16[256,2048]{1,0:T(8,128)(2,1)S(1)} %maximum_convert_fusion.features_ref, bf16[256,1152]{1,0:T(8,128)(2,1)S(1)} %fusion.31.own_ref, bf16[256,1152]{1,0:T(8,128)(2,1)S(1)} %broadcast_select_fusion.1.next_ref), custom_call_target="tpu_custom_call" | custom-call | flops 2415919104 | bytes 11665408 | tf_op jit(solution)/shard_map/pallas_call | solution.py:121
  143.0 6.4 %fusion.18.mine_ref = bf16[256,2048]{1,0:T(8,128)(2,1)S(1)} fusion(f32[256,2048]{1,0:T(8,128)S(1)} %fusion, bf16[2,2048,2304]{2,1,0:T(8,128)(2,1)} %bitcast.44, bf16[256,1152]{1,0:T(8,128)(2,1)S(1)} %maximum_select_fusion.own_ref, bf16[256,1152]{1,0:T(8,128)(2,1)S(1)} %fusion.31.own_ref), kind=kOutput, calls=%fused_computation.17 | convolution fusion | flops 2419326976 | bytes 13762560 | tf_op jit(solution)/shard_map/dot_general | solution.py:23
  149.8 8.4 %shard_map.107 = bf16[2048,2,2304]{2,1,0:T(2,128)(2,1)} custom-call(bf16[256,2048]{1,0:T(8,128)(2,1)S(1)} %maximum_convert_fusion.features_ref, bf16[256,1152]{1,0:T(8,128)(2,1)S(1)} %maximum_select_fusion.own_ref, bf16[256,1152]{1,0:T(8,128)(2,1)S(1)} %broadcast_select_fusion.next_ref, ...), custom_call_target="tpu_custom_call", output_to_operand_aliasing={{}: (3, {})} | custom-call | flops 2415919104 | bytes 11665408 | tf_op jit(solution)/shard_map/pallas_call | solution.py:121
  158.1 5.8 %shard_map.106 = (bf16[2048,2304]{1,0:T(8,128)(2,1)}, f32[1,2048]{1,0:T(1,128)}) custom-call(bf16[256,2048]{1,0:T(8,128)(2,1)S(1)} %fusion.18.mine_ref, bf16[256,2048]{1,0:T(8,128)(2,1)S(1)} %collective-permute-done.33.other_ref, bf16[256,2048]{1,0:T(8,128)(2,1)S(1)} %compare_convert_fusion.live_ref, bf16[256,2304]{1,0:T(8,128)(2,1)S(1)} %convolution_convert_fusion.inputs_ref), custom_call_target="tpu_custom_call" | custom-call | flops 2415919104 | bytes 13762560 | tf_op jit(solution)/shard_map/pallas_call | solution.py:149
  (133 shorter events, 29.3 us)
Async XLA Ops:
  3.2 1.5 collective-permute-start
  4.8 20.6 %collective-permute-start.2 = (bf16[64,2304]{1,0:T(8,128)(2,1)S(1)}, bf16[64,2304]{1,0:T(8,128)(2,1)S(1)}, u32[]{:S(2)}, u32[]{:S(2)}) collective-permute-start(bf16[64,2304]{1,0:T(8,128)(2,1)S(1)} %pad_maximum_fusion.2), channel_id=1, source_target_pairs={{0,8},{4,12},{8,0},{12,4},{1,9},{5,13},{9,1},{13,5},{2,10},{6,14},... | collective-permute-start | bytes 884744 | tf_op jit(solution)/shard_map/ppermute | solution.py:19
  8.9 17.1 %collective-permute-start.1 = (bf16[64,2304]{1,0:T(8,128)(2,1)S(1)}, bf16[64,2304]{1,0:T(8,128)(2,1)S(1)}, u32[]{:S(2)}, u32[]{:S(2)}) collective-permute-start(bf16[64,2304]{1,0:T(8,128)(2,1)S(1)} %pad_maximum_fusion.2), channel_id=1, source_target_pairs={{0,4},{4,0},{8,12},{12,8},{1,5},{5,1},{9,13},{13,9},{2,6},{6,2},{1... | collective-permute-start | bytes 884744 | tf_op jit(solution)/shard_map/ppermute | solution.py:19
  10.7 1.6 collective-permute-start.5
  25.4 9.3 %collective-permute-start.3 = (bf16[64,2304]{1,0:T(8,128)(2,1)S(1)}, bf16[64,2304]{1,0:T(8,128)(2,1)S(1)}, u32[]{:S(2)}, u32[]{:S(2)}) collective-permute-start(bf16[64,2304]{1,0:T(8,128)(2,1)S(1)} %collective-permute-done.2), channel_id=1, source_target_pairs={{0,4},{4,0},{8,12},{12,8},{1,5},{5,1},{9,13},{13,9},{2,6},{6,2},{1... | collective-permute-start | bytes 884744 | tf_op jit(solution)/shard_map/ppermute | solution.py:19
  38.3 3.6 %collective-permute-start.6 = (f32[256,1024]{1,0:T(8,128)S(1)}, f32[256,1024]{1,0:T(8,128)S(1)}, u32[]{:S(2)}, u32[]{:S(2)}) collective-permute-start(f32[256,1024]{1,0:T(8,128)S(1)} %shard_map.102), channel_id=1, source_target_pairs={{0,1},{1,0},{2,3},{3,2},{4,5},{5,4},{6,7},{7,6},{8,9},{9,8},{10,11... | collective-permute-start | bytes 3145736 | tf_op jit(solution)/shard_map/ppermute | solution.py:15
  41.4 2.8 %collective-permute-start.7 = (f32[256,1024]{1,0:T(8,128)S(1)}, f32[256,1024]{1,0:T(8,128)S(1)}, u32[]{:S(2)}, u32[]{:S(2)}) collective-permute-start(f32[256,1024]{1,0:T(8,128)S(1)} %shard_map.103), channel_id=1, source_target_pairs={{0,1},{1,0},{2,3},{3,2},{4,5},{5,4},{6,7},{7,6},{8,9},{9,8},{10,11... | collective-permute-start | bytes 3145736 | tf_op jit(solution)/shard_map/ppermute | solution.py:15
  52.4 16.8 %collective-permute-start.9 = (bf16[256,1152]{1,0:T(8,128)(2,1)}, bf16[256,1152]{1,0:T(8,128)(2,1)}, u32[]{:S(2)}, u32[]{:S(2)}) collective-permute-start(bf16[256,1152]{1,0:T(8,128)(2,1)} %slice.180), channel_id=1, source_target_pairs={{0,2},{1,3},{4,6},{5,7},{8,10},{9,11},{12,14},{13,15},{16,18},{17,... | collective-permute-start | bytes 1769480 | tf_op jit(solution)/shard_map/ppermute | solution.py:277
  57.4 7.2 %collective-permute-start.8 = (bf16[64,1152]{1,0:T(8,128)(2,1)}, bf16[64,1152]{1,0:T(8,128)(2,1)}, u32[]{:S(2)}, u32[]{:S(2)}) collective-permute-start(bf16[64,1152]{1,0:T(8,128)(2,1)} %get-tuple-element.91), channel_id=1, source_target_pairs={{0,4},{4,0},{8,12},{12,8},{1,5},{5,1},{9,13},{13,9},{2,6},{6,2},{1... | collective-permute-start | bytes 442376 | tf_op jit(solution)/shard_map/ppermute | solution.py:19
  59.3 15.5 %collective-permute-start.14 = (bf16[64,1152]{1,0:T(8,128)(2,1)S(1)}, bf16[64,1152]{1,0:T(8,128)(2,1)S(1)}, u32[]{:S(2)}, u32[]{:S(2)}) collective-permute-start(bf16[64,1152]{1,0:T(8,128)(2,1)S(1)} %copy-done.5), channel_id=1, source_target_pairs={{0,8},{4,12},{8,0},{12,4},{1,9},{5,13},{9,1},{13,5},{2,10},{6,14},... | collective-permute-start | bytes 442376 | tf_op jit(solution)/shard_map/ppermute | solution.py:19
  59.7 15.1 %collective-permute-start.15 = (bf16[64,1152]{1,0:T(8,128)(2,1)S(1)}, bf16[64,1152]{1,0:T(8,128)(2,1)S(1)}, u32[]{:S(2)}, u32[]{:S(2)}) collective-permute-start(bf16[64,1152]{1,0:T(8,128)(2,1)S(1)} %get-tuple-element.90), channel_id=1, source_target_pairs={{0,12},{4,8},{8,4},{12,0},{1,13},{5,9},{9,5},{13,1},{2,14},{6,10},... | collective-permute-start | bytes 442376 | tf_op jit(solution)/shard_map/ppermute | solution.py:19
  71.3 7.7 %collective-permute-start.10 = (bf16[64,1152]{1,0:T(8,128)(2,1)S(1)}, bf16[64,1152]{1,0:T(8,128)(2,1)S(1)}, u32[]{:S(2)}, u32[]{:S(2)}) collective-permute-start(bf16[64,1152]{1,0:T(8,128)(2,1)S(1)} %get-tuple-element.92), channel_id=1, source_target_pairs={{0,4},{4,0},{8,12},{12,8},{1,5},{5,1},{9,13},{13,9},{2,6},{6,2},{1... | collective-permute-start | bytes 442376 | tf_op jit(solution)/shard_map/ppermute | solution.py:19
  71.8 8.8 %collective-permute-start.12 = (bf16[64,1152]{1,0:T(8,128)(2,1)S(1)}, bf16[64,1152]{1,0:T(8,128)(2,1)S(1)}, u32[]{:S(2)}, u32[]{:S(2)}) collective-permute-start(bf16[64,1152]{1,0:T(8,128)(2,1)S(1)} %get-tuple-element.93), channel_id=1, source_target_pairs={{0,12},{4,8},{8,4},{12,0},{1,13},{5,9},{9,5},{13,1},{2,14},{6,10},... | collective-permute-start | bytes 442376 | tf_op jit(solution)/shard_map/ppermute | solution.py:19
  73.1 14.9 %collective-permute-start.11 = (bf16[64,1152]{1,0:T(8,128)(2,1)S(1)}, bf16[64,1152]{1,0:T(8,128)(2,1)S(1)}, u32[]{:S(2)}, u32[]{:S(2)}) collective-permute-start(bf16[64,1152]{1,0:T(8,128)(2,1)S(1)} %get-tuple-element.94), channel_id=1, source_target_pairs={{0,8},{4,12},{8,0},{12,4},{1,9},{5,13},{9,1},{13,5},{2,10},{6,14},... | collective-permute-start | bytes 442376 | tf_op jit(solution)/shard_map/ppermute | solution.py:19
  75.9 19.1 %collective-permute-start.16 = (f32[64,1152]{1,0:T(8,128)S(1)}, f32[64,1152]{1,0:T(8,128)S(1)}, u32[]{:S(2)}, u32[]{:S(2)}) collective-permute-start(f32[64,1152]{1,0:T(8,128)S(1)} %fusion.36), channel_id=1, source_target_pairs={{0,2},{2,0},{1,3},{3,1},{4,6},{6,4},{5,7},{7,5},{8,10},{10,8},{9,1... | collective-permute-start | bytes 884744 | tf_op jit(solution)/shard_map/ppermute | solution.py:15
  88.2 14.7 %collective-permute-start.23 = (bf16[64,1152]{1,0:T(8,128)(2,1)S(1)}, bf16[64,1152]{1,0:T(8,128)(2,1)S(1)}, u32[]{:S(2)}, u32[]{:S(2)}) collective-permute-start(bf16[64,1152]{1,0:T(8,128)(2,1)S(1)} %get-tuple-element.85), channel_id=1, source_target_pairs={{0,12},{4,8},{8,4},{12,0},{1,13},{5,9},{9,5},{13,1},{2,14},{6,10},... | collective-permute-start | bytes 442376 | tf_op jit(solution)/shard_map/ppermute | solution.py:19
  89.6 11.1 %collective-permute-start.13 = (bf16[64,1152]{1,0:T(8,128)(2,1)S(1)}, bf16[64,1152]{1,0:T(8,128)(2,1)S(1)}, u32[]{:S(2)}, u32[]{:S(2)}) collective-permute-start(bf16[64,1152]{1,0:T(8,128)(2,1)S(1)} %get-tuple-element.86), channel_id=1, source_target_pairs={{0,4},{4,0},{8,12},{12,8},{1,5},{5,1},{9,13},{13,9},{2,6},{6,2},{1... | collective-permute-start | bytes 442376 | tf_op jit(solution)/shard_map/ppermute | solution.py:19
  89.6 13.3 %collective-permute-start.22 = (bf16[64,1152]{1,0:T(8,128)(2,1)S(1)}, bf16[64,1152]{1,0:T(8,128)(2,1)S(1)}, u32[]{:S(2)}, u32[]{:S(2)}) collective-permute-start(bf16[64,1152]{1,0:T(8,128)(2,1)S(1)} %get-tuple-element.73), channel_id=1, source_target_pairs={{0,8},{4,12},{8,0},{12,4},{1,9},{5,13},{9,1},{13,5},{2,10},{6,14},... | collective-permute-start | bytes 442376 | tf_op jit(solution)/shard_map/ppermute | solution.py:19
  92.7 15.0 %collective-permute-start.18 = (bf16[64,1152]{1,0:T(8,128)(2,1)S(1)}, bf16[64,1152]{1,0:T(8,128)(2,1)S(1)}, u32[]{:S(2)}, u32[]{:S(2)}) collective-permute-start(bf16[64,1152]{1,0:T(8,128)(2,1)S(1)} %fusion.48), channel_id=1, source_target_pairs={{0,2},{2,0},{1,3},{3,1},{4,6},{6,4},{5,7},{7,5},{8,10},{10,8},{9,1... | collective-permute-start | bytes 442376 | tf_op jit(solution)/shard_map/ppermute | solution.py:15
  100.7 14.4 %collective-permute-start.20 = (bf16[64,1152]{1,0:T(8,128)(2,1)S(1)}, bf16[64,1152]{1,0:T(8,128)(2,1)S(1)}, u32[]{:S(2)}, u32[]{:S(2)}) collective-permute-start(bf16[64,1152]{1,0:T(8,128)(2,1)S(1)} %get-tuple-element.49), channel_id=1, source_target_pairs={{0,8},{4,12},{8,0},{12,4},{1,9},{5,13},{9,1},{13,5},{2,10},{6,14},... | collective-permute-start | bytes 442376 | tf_op jit(solution)/shard_map/ppermute | solution.py:19
  100.7 8.6 %collective-permute-start.17 = (bf16[64,1152]{1,0:T(8,128)(2,1)S(1)}, bf16[64,1152]{1,0:T(8,128)(2,1)S(1)}, u32[]{:S(2)}, u32[]{:S(2)}) collective-permute-start(bf16[64,1152]{1,0:T(8,128)(2,1)S(1)} %get-tuple-element.49), channel_id=1, source_target_pairs={{0,4},{4,0},{8,12},{12,8},{1,5},{5,1},{9,13},{13,9},{2,6},{6,2},{1... | collective-permute-start | bytes 442376 | tf_op jit(solution)/shard_map/ppermute | solution.py:19
  104.0 11.0 %collective-permute-start.25 = (bf16[64,1152]{1,0:T(8,128)(2,1)S(1)}, bf16[64,1152]{1,0:T(8,128)(2,1)S(1)}, u32[]{:S(2)}, u32[]{:S(2)}) collective-permute-start(bf16[64,1152]{1,0:T(8,128)(2,1)S(1)} %get-tuple-element.84), channel_id=1, source_target_pairs={{0,2},{1,3},{4,6},{5,7},{8,10},{9,11},{12,14},{13,15},{16,18},{17,... | collective-permute-start | bytes 442376 | tf_op jit(solution)/shard_map/ppermute | solution.py:301
  106.4 15.5 %collective-permute-start.24 = (bf16[256,1152]{1,0:T(8,128)(2,1)S(1)}, bf16[256,1152]{1,0:T(8,128)(2,1)S(1)}, u32[]{:S(2)}, u32[]{:S(2)}) collective-permute-start(bf16[256,1152]{1,0:T(8,128)(2,1)S(1)} %fusion.28), channel_id=1, source_target_pairs={{2,0},{3,1},{6,4},{7,5},{10,8},{11,9},{14,12},{15,13},{18,16},{19,... | collective-permute-start | bytes 1769480 | tf_op jit(solution)/shard_map/ppermute | solution.py:294
  109.3 6.1 %collective-permute-start.28 = (bf16[64,1152]{1,0:T(8,128)(2,1)S(1)}, bf16[64,1152]{1,0:T(8,128)(2,1)S(1)}, u32[]{:S(2)}, u32[]{:S(2)}) collective-permute-start(bf16[64,1152]{1,0:T(8,128)(2,1)S(1)} %get-tuple-element.50), channel_id=1, source_target_pairs={{0,8},{4,12},{8,0},{12,4},{1,9},{5,13},{9,1},{13,5},{2,10},{6,14},... | collective-permute-start | bytes 442376 | tf_op jit(solution)/shard_map/ppermute | solution.py:19
  110.0 17.1 %collective-permute-start.19 = (bf16[64,1152]{1,0:T(8,128)(2,1)S(1)}, bf16[64,1152]{1,0:T(8,128)(2,1)S(1)}, u32[]{:S(2)}, u32[]{:S(2)}) collective-permute-start(bf16[64,1152]{1,0:T(8,128)(2,1)S(1)} %get-tuple-element.50), channel_id=1, source_target_pairs={{0,4},{4,0},{8,12},{12,8},{1,5},{5,1},{9,13},{13,9},{2,6},{6,2},{1... | collective-permute-start | bytes 442376 | tf_op jit(solution)/shard_map/ppermute | solution.py:19
  115.1 6.0 %collective-permute-start.21 = (bf16[64,1152]{1,0:T(8,128)(2,1)S(1)}, bf16[64,1152]{1,0:T(8,128)(2,1)S(1)}, u32[]{:S(2)}, u32[]{:S(2)}) collective-permute-start(bf16[64,1152]{1,0:T(8,128)(2,1)S(1)} %collective-permute-done.20), channel_id=1, source_target_pairs={{0,4},{4,0},{8,12},{12,8},{1,5},{5,1},{9,13},{13,9},{2,6},{6,2},{1... | collective-permute-start | bytes 442376 | tf_op jit(solution)/shard_map/ppermute | solution.py:19
  115.5 16.3 %collective-permute-start.29 = (bf16[64,1152]{1,0:T(8,128)(2,1)S(1)}, bf16[64,1152]{1,0:T(8,128)(2,1)S(1)}, u32[]{:S(2)}, u32[]{:S(2)}) collective-permute-start(bf16[64,1152]{1,0:T(8,128)(2,1)S(1)} %collective-permute-done.28), channel_id=1, source_target_pairs={{0,4},{4,0},{8,12},{12,8},{1,5},{5,1},{9,13},{13,9},{2,6},{6,2},{1... | collective-permute-start | bytes 442376 | tf_op jit(solution)/shard_map/ppermute | solution.py:19
  127.2 15.7 %collective-permute-start.32 = (bf16[64,1152]{1,0:T(8,128)(2,1)S(1)}, bf16[64,1152]{1,0:T(8,128)(2,1)S(1)}, u32[]{:S(2)}, u32[]{:S(2)}) collective-permute-start(bf16[64,1152]{1,0:T(8,128)(2,1)S(1)} %get-tuple-element.59), channel_id=1, source_target_pairs={{0,12},{4,8},{8,4},{12,0},{1,13},{5,9},{9,5},{13,1},{2,14},{6,10},... | collective-permute-start | bytes 442376 | tf_op jit(solution)/shard_map/ppermute | solution.py:19
  130.1 12.7 %collective-permute-start.31 = (bf16[64,1152]{1,0:T(8,128)(2,1)S(1)}, bf16[64,1152]{1,0:T(8,128)(2,1)S(1)}, u32[]{:S(2)}, u32[]{:S(2)}) collective-permute-start(bf16[64,1152]{1,0:T(8,128)(2,1)S(1)} %get-tuple-element.59), channel_id=1, source_target_pairs={{0,8},{4,12},{8,0},{12,4},{1,9},{5,13},{9,1},{13,5},{2,10},{6,14},... | collective-permute-start | bytes 442376 | tf_op jit(solution)/shard_map/ppermute | solution.py:19
  130.1 12.7 %collective-permute-start.30 = (bf16[64,1152]{1,0:T(8,128)(2,1)S(1)}, bf16[64,1152]{1,0:T(8,128)(2,1)S(1)}, u32[]{:S(2)}, u32[]{:S(2)}) collective-permute-start(bf16[64,1152]{1,0:T(8,128)(2,1)S(1)} %get-tuple-element.59), channel_id=1, source_target_pairs={{0,4},{4,0},{8,12},{12,8},{1,5},{5,1},{9,13},{13,9},{2,6},{6,2},{1... | collective-permute-start | bytes 442376 | tf_op jit(solution)/shard_map/ppermute | solution.py:19
  131.7 1.6 collective-permute-start.26
  149.4 8.7 %collective-permute-start.33 = (bf16[256,2048]{1,0:T(8,128)(2,1)S(1)}, bf16[256,2048]{1,0:T(8,128)(2,1)S(1)}, u32[]{:S(2)}, u32[]{:S(2)}) collective-permute-start(bf16[256,2048]{1,0:T(8,128)(2,1)S(1)} %fusion.18.mine_ref), channel_id=1, source_target_pairs={{0,1},{1,0},{2,3},{3,2},{4,5},{5,4},{6,7},{7,6},{8,9},{9,8},{10,11... | collective-permute-start | bytes 3145736 | tf_op jit(solution)/shard_map/ppermute | solution.py:15
  (14 other events, 146.5 us)

commit v5 on v4

--- a/solution.py
+++ b/solution.py
@@ -1,4 +1,5 @@
 import functools
+import math
 
 import jax
 import jax.numpy as jnp
@@ -97,10 +98,17 @@
 def dec_grad_kernel(scale, features_ref, own_ref, next_ref, *rest):
     out_ref = rest[-1]
     features = features_ref[...]
-    own = dot_first(features, own_ref[...])
-    out_ref[:, 0, :] = (scale * own).astype(out_ref.dtype)
-    following = dot_first(features, next_ref[...])
-    out_ref[:, 1, :] = (scale * following).astype(out_ref.dtype)
+    own, following = own_ref[...], next_ref[...]
+    after = scale
+    if math.log2(scale).is_integer():
+        own, following, after = own * scale, following * scale, None
+
+    def product(errors):
+        found = dot_first(features, errors)
+        return (found if after is None else after * found).astype(out_ref.dtype)
+
+    out_ref[:, 0, :] = product(own)
+    out_ref[:, 1, :] = product(following)
 
 
 def dec_grad_call(features, own, following, scale, chunk, chunks, before=None):

time: 164 us -> 165 us (level)
  no operation moved by 1% of the time
where the time goes in v5:
time: 165 us; the launch traced here: 164 us
  starting transfers between devices  50.5 us (31%)
  waiting for transfers between devices  37.9 us (23%)
  Pallas kernels  30.1 us (18%)
  local copies, waits for them, and re-layouts  18.7 us (11%)
  matrix products  17.5 us (11%)
  other arithmetic  8.49 us (5%)
    ppermute x21, starting transfers between devices, swapped(): lax.ppermute(block, axis, [(i, i ^ distance) for i in range(lax.axis_size...  35.2 us
    ppermute x21, waiting for transfers between devices, swapped(): lax.ppermute(block, axis, [(i, i ^ distance) for i in range(lax.axis_size...  28.6 us
    pallas_call x2, Pallas kernels, dec_grad_call(): pl.pallas_call(functools.partial(dec_grad_kernel, scale), grid=(count //...  17.3 us
    optimization_barrier x1, local copies, waits for them, and re-layouts, on_device(): mlp_half, dec_weight = lax.optimization_barrier((mlp_half, dec_weight))  12.3 us
    dot_general x2, matrix products, dot_last(): lax.dot_general(left, right, (((1,), (1,)), ((), ())), preferred_element_...  11.6 us
    ppermute x10, starting transfers between devices, shifted(): lax.ppermute(block, axis, [(i, (i + distance) % count) for i in range(cou...  7.49 us
    pallas_call x2, Pallas kernels, encoder_call(): pl.pallas_call(functools.partial(encoder_kernel, part), in_specs=[pl.Bloc...  5.93 us
    pallas_call x1, Pallas kernels, enc_grad_call(): pl.pallas_call(functools.partial(enc_grad_kernel, scale), grid=(count //...  5.81 us
  transfers between devices with their start and end apart: 34, of which 17 were waited for; matrix products, arithmetic and copies ran while one was open for 16% of the time, Pallas kernels for 13%

profile of v5, /device:TPU:0, one launch (start us, length us, event | category | flops | bytes accessed | tf_op | source)
XLA Modules:
  0.0 164.5 jit_solution(14916813923826520412)
XLA Ops:
  0.6 2.4 %fusion.54 = (bf16[32,1,4608]{2,1,0:T(2,128)(2,1)S(1)}, bf16[32,1,4608]{2,1,0:T(2,128)(2,1)S(1)}) fusion(bf16[32,2,4608]{2,1,0:T(2,128)(2,1)} %param.7), kind=kLoop, calls=%fused_computation.128 | loop fusion | bytes 1179648 | tf_op jit(solution)/shard_map/slice | solution.py:224
  4.8 4.0 %collective-permute-start.2 = (bf16[64,2304]{1,0:T(8,128)(2,1)S(1)}, bf16[64,2304]{1,0:T(8,128)(2,1)S(1)}, u32[]{:S(2)}, u32[]{:S(2)}) collective-permute-start(bf16[64,2304]{1,0:T(8,128)(2,1)S(1)} %pad_maximum_fusion.2), channel_id=1, source_target_pairs={{0,8},{4,12},{8,0},{12,4},{1,9},{5,13},{9,1},{13,5},{2,10},{6,14},... | collective-permute-start | bytes 884744 | tf_op jit(solution)/shard_map/ppermute | solution.py:20
  8.9 1.6 collective-permute-start.1
  13.1 12.3 %copy.28 = bf16[1,2048,2,2304]{3,1,2,0:T(8,128)(2,1)S(1)} copy(bf16[1,2048,2,2304]{3,2,1,0:T(2,128)(2,1)} %param.11) | data formatting | bytes 37748736 | tf_op jit(solution)/shard_map/optimization_barrier | solution.py:229
  26.0 8.8 %collective-permute-done.3 = bf16[64,2304]{1,0:T(8,128)(2,1)S(1)} collective-permute-done((bf16[64,2304]{1,0:T(8,128)(2,1)S(1)}, bf16[64,2304]{1,0:T(8,128)(2,1)S(1)}, u32[]{:S(2)}, u32[]{:S(2)}) %collective-permute-start.3) | collective-permute-done | bytes 294944 | tf_op jit(solution)/shard_map/ppermute | solution.py:20
  35.4 3.0 %shard_map.102 = f32[256,1024]{1,0:T(8,128)S(1)} custom-call(bf16[256,2304]{1,0:T(8,128)(2,1)S(1)} %convolution_convert_fusion.inputs_ref, bf16[2048,2304]{1,0:T(8,128)(2,1)S(1)} %bitcast.38), custom_call_target="tpu_custom_call" | custom-call | tf_op jit(solution)/shard_map/pallas_call | solution.py:72
  38.4 3.0 %shard_map.103 = f32[256,1024]{1,0:T(8,128)S(1)} custom-call(bf16[256,2304]{1,0:T(8,128)(2,1)S(1)} %convolution_convert_fusion.inputs_ref, bf16[2048,2304]{1,0:T(8,128)(2,1)S(1)} %bitcast.39), custom_call_target="tpu_custom_call" | custom-call | tf_op jit(solution)/shard_map/pallas_call | solution.py:72
  42.1 2.1 %collective-permute-done.7 = f32[256,1024]{1,0:T(8,128)S(1)} collective-permute-done((f32[256,1024]{1,0:T(8,128)S(1)}, f32[256,1024]{1,0:T(8,128)S(1)}, u32[]{:S(2)}, u32[]{:S(2)}) %collective-permute-start.7) | collective-permute-done | bytes 1048608 | tf_op jit(solution)/shard_map/ppermute | solution.py:16
  44.9 2.7 %fusion.12 = bf16[256,2304]{1,0:T(8,128)(2,1)S(1)} fusion(bf16[256,2048]{1,0:T(8,128)(2,1)S(1)} %maximum_convert_fusion.features_ref, bf16[2,2048,2304]{2,1,0:T(8,128)(2,1)S(1)} %bitcast.41), kind=kOutput, calls=%fused_computation.14 | convolution fusion | flops 2416508928 | bytes 11665408 | tf_op jit(solution)/shard_map/dot_general | solution.py:253
  47.6 2.7 %fusion.6 = f32[256,2304]{1,0:T(8,128)S(1)} fusion(bf16[256,2048]{1,0:T(8,128)(2,1)S(1)} %maximum_convert_fusion.features_ref, bf16[2,2048,2304]{2,1,0:T(8,128)(2,1)S(1)} %bitcast.42), kind=kOutput, calls=%fused_computation.8 | convolution fusion | flops 2415919104 | bytes 12845056 | tf_op jit(solution)/shard_map/dot_general | solution.py:254
  52.4 4.2 %collective-permute-start.9 = (bf16[256,1152]{1,0:T(8,128)(2,1)}, bf16[256,1152]{1,0:T(8,128)(2,1)}, u32[]{:S(2)}, u32[]{:S(2)}) collective-permute-start(bf16[256,1152]{1,0:T(8,128)(2,1)} %slice.180), channel_id=1, source_target_pairs={{0,2},{1,3},{4,6},{5,7},{8,10},{9,11},{12,14},{13,15},{16,18},{17,... | collective-permute-start | bytes 1769480 | tf_op jit(solution)/shard_map/ppermute | solution.py:285
  59.7 3.6 %collective-permute-start.15 = (bf16[64,1152]{1,0:T(8,128)(2,1)S(1)}, bf16[64,1152]{1,0:T(8,128)(2,1)S(1)}, u32[]{:S(2)}, u32[]{:S(2)}) collective-permute-start(bf16[64,1152]{1,0:T(8,128)(2,1)S(1)} %get-tuple-element.90), channel_id=1, source_target_pairs={{0,12},{4,8},{8,4},{12,0},{1,13},{5,9},{9,5},{13,1},{2,14},{6,10},... | collective-permute-start | bytes 442376 | tf_op jit(solution)/shard_map/ppermute | solution.py:20
  64.6 4.6 %collective-permute-done.9 = bf16[256,1152]{1,0:T(8,128)(2,1)} collective-permute-done((bf16[256,1152]{1,0:T(8,128)(2,1)}, bf16[256,1152]{1,0:T(8,128)(2,1)}, u32[]{:S(2)}, u32[]{:S(2)}) %collective-permute-start.9) | collective-permute-done | bytes 589856 | tf_op jit(solution)/shard_map/ppermute | solution.py:285
  69.2 2.0 %fusion.50 = (bf16[256,1152]{1,0:T(8,128)(2,1)S(1)}, f32[256,1152]{1,0:T(8,128)S(1)}) fusion(bf16[256,1152]{1,0:T(8,128)(2,1)} %collective-permute-done.9, f32[256,2304]{1,0:T(8,128)} %copy-done.1, pred[]{:T(512)S(6)} %lt.27), kind=kLoop, calls=%fused_computation.124 | loop fusion | flops 1179648 | bytes 4718593 | tf_op jit(solution)/shard_map/convert_element_type | solution.py:288
  73.1 1.7 %collective-permute-start.11 = (bf16[64,1152]{1,0:T(8,128)(2,1)S(1)}, bf16[64,1152]{1,0:T(8,128)(2,1)S(1)}, u32[]{:S(2)}, u32[]{:S(2)}) collective-permute-start(bf16[64,1152]{1,0:T(8,128)(2,1)S(1)} %get-tuple-element.94), channel_id=1, source_target_pairs={{0,8},{4,12},{8,0},{12,4},{1,9},{5,13},{9,1},{13,5},{2,10},{6,14},... | collective-permute-start | bytes 442376 | tf_op jit(solution)/shard_map/ppermute | solution.py:20
  75.9 2.5 %collective-permute-start.16 = (f32[64,1152]{1,0:T(8,128)S(1)}, f32[64,1152]{1,0:T(8,128)S(1)}, u32[]{:S(2)}, u32[]{:S(2)}) collective-permute-start(f32[64,1152]{1,0:T(8,128)S(1)} %fusion.36), channel_id=1, source_target_pairs={{0,2},{2,0},{1,3},{3,1},{4,6},{6,4},{5,7},{7,5},{8,10},{10,8},{9,1... | collective-permute-start | bytes 884744 | tf_op jit(solution)/shard_map/ppermute | solution.py:16
  79.0 1.6 %collective-permute-done.12 = bf16[64,1152]{1,0:T(8,128)(2,1)S(1)} collective-permute-done((bf16[64,1152]{1,0:T(8,128)(2,1)S(1)}, bf16[64,1152]{1,0:T(8,128)(2,1)S(1)}, u32[]{:S(2)}, u32[]{:S(2)}) %collective-permute-start.12) | collective-permute-done | bytes 147488 | tf_op jit(solution)/shard_map/ppermute | solution.py:20
  80.6 7.4 %collective-permute-done.11 = bf16[64,1152]{1,0:T(8,128)(2,1)S(1)} collective-permute-done((bf16[64,1152]{1,0:T(8,128)(2,1)S(1)}, bf16[64,1152]{1,0:T(8,128)(2,1)S(1)}, u32[]{:S(2)}, u32[]{:S(2)}) %collective-permute-start.11) | collective-permute-done | bytes 147488 | tf_op jit(solution)/shard_map/ppermute | solution.py:20
  89.6 3.1 %collective-permute-start.22 = (bf16[64,1152]{1,0:T(8,128)(2,1)S(1)}, bf16[64,1152]{1,0:T(8,128)(2,1)S(1)}, u32[]{:S(2)}, u32[]{:S(2)}) collective-permute-start(bf16[64,1152]{1,0:T(8,128)(2,1)S(1)} %get-tuple-element.73), channel_id=1, source_target_pairs={{0,8},{4,12},{8,0},{12,4},{1,9},{5,13},{9,1},{13,5},{2,10},{6,14},... | collective-permute-start | bytes 442376 | tf_op jit(solution)/shard_map/ppermute | solution.py:20
  92.7 2.2 %collective-permute-start.18 = (bf16[64,1152]{1,0:T(8,128)(2,1)S(1)}, bf16[64,1152]{1,0:T(8,128)(2,1)S(1)}, u32[]{:S(2)}, u32[]{:S(2)}) collective-permute-start(bf16[64,1152]{1,0:T(8,128)(2,1)S(1)} %fusion.48), channel_id=1, source_target_pairs={{0,2},{2,0},{1,3},{3,1},{4,6},{6,4},{5,7},{7,5},{8,10},{10,8},{9,1... | collective-permute-start | bytes 442376 | tf_op jit(solution)/shard_map/ppermute | solution.py:16
  95.1 5.6 %collective-permute-done.13 = bf16[64,1152]{1,0:T(8,128)(2,1)S(1)} collective-permute-done((bf16[64,1152]{1,0:T(8,128)(2,1)S(1)}, bf16[64,1152]{1,0:T(8,128)(2,1)S(1)}, u32[]{:S(2)}, u32[]{:S(2)}) %collective-permute-start.13) | collective-permute-done | bytes 147488 | tf_op jit(solution)/shard_map/ppermute | solution.py:20
  100.7 2.2 %collective-permute-start.17 = (bf16[64,1152]{1,0:T(8,128)(2,1)S(1)}, bf16[64,1152]{1,0:T(8,128)(2,1)S(1)}, u32[]{:S(2)}, u32[]{:S(2)}) collective-permute-start(bf16[64,1152]{1,0:T(8,128)(2,1)S(1)} %get-tuple-element.49), channel_id=1, source_target_pairs={{0,4},{4,0},{8,12},{12,8},{1,5},{5,1},{9,13},{13,9},{2,6},{6,2},{1... | collective-permute-start | bytes 442376 | tf_op jit(solution)/shard_map/ppermute | solution.py:20
  104.0 2.3 %collective-permute-start.25 = (bf16[64,1152]{1,0:T(8,128)(2,1)S(1)}, bf16[64,1152]{1,0:T(8,128)(2,1)S(1)}, u32[]{:S(2)}, u32[]{:S(2)}) collective-permute-start(bf16[64,1152]{1,0:T(8,128)(2,1)S(1)} %get-tuple-element.84), channel_id=1, source_target_pairs={{0,2},{1,3},{4,6},{5,7},{8,10},{9,11},{12,14},{13,15},{16,18},{17,... | collective-permute-start | bytes 442376 | tf_op jit(solution)/shard_map/ppermute | solution.py:309
  107.7 1.6 collective-permute-done.17
  110.0 4.9 %collective-permute-start.19 = (bf16[64,1152]{1,0:T(8,128)(2,1)S(1)}, bf16[64,1152]{1,0:T(8,128)(2,1)S(1)}, u32[]{:S(2)}, u32[]{:S(2)}) collective-permute-start(bf16[64,1152]{1,0:T(8,128)(2,1)S(1)} %get-tuple-element.50), channel_id=1, source_target_pairs={{0,4},{4,0},{8,12},{12,8},{1,5},{5,1},{9,13},{13,9},{2,6},{6,2},{1... | collective-permute-start | bytes 442376 | tf_op jit(solution)/shard_map/ppermute | solution.py:20
  115.5 4.2 %collective-permute-start.29 = (bf16[64,1152]{1,0:T(8,128)(2,1)S(1)}, bf16[64,1152]{1,0:T(8,128)(2,1)S(1)}, u32[]{:S(2)}, u32[]{:S(2)}) collective-permute-start(bf16[64,1152]{1,0:T(8,128)(2,1)S(1)} %collective-permute-done.28), channel_id=1, source_target_pairs={{0,4},{4,0},{8,12},{12,8},{1,5},{5,1},{9,13},{13,9},{2,6},{6,2},{1... | collective-permute-start | bytes 442376 | tf_op jit(solution)/shard_map/ppermute | solution.py:20
  121.9 5.2 %fusion = f32[256,2048]{1,0:T(8,128)S(1)} fusion(bf16[2,2048,2304]{2,1,0:T(8,128)(2,1)} %bitcast.43, bf16[256,1152]{1,0:T(8,128)(2,1)S(1)} %broadcast_select_fusion.next_ref, bf16[256,1152]{1,0:T(8,128)(2,1)S(1)} %broadcast_select_fusion.1.next_ref), kind=kOutput, calls=%fused_computation.2 | convolution fusion | flops 2418278400 | bytes 12713984 | tf_op jit(solution)/shard_map/dot_general | solution.py:24
  127.2 3.0 %collective-permute-start.32 = (bf16[64,1152]{1,0:T(8,128)(2,1)S(1)}, bf16[64,1152]{1,0:T(8,128)(2,1)S(1)}, u32[]{:S(2)}, u32[]{:S(2)}) collective-permute-start(bf16[64,1152]{1,0:T(8,128)(2,1)S(1)} %get-tuple-element.59), channel_id=1, source_target_pairs={{0,12},{4,8},{8,4},{12,0},{1,13},{5,9},{9,5},{13,1},{2,14},{6,10},... | collective-permute-start | bytes 442376 | tf_op jit(solution)/shard_map/ppermute | solution.py:20
  134.5 8.6 %shard_map.105.rest_0_ = bf16[2048,2,2304]{2,1,0:T(2,128)(2,1)} custom-call(bf16[256,2048]{1,0:T(8,128)(2,1)S(1)} %maximum_convert_fusion.features_ref, bf16[256,1152]{1,0:T(8,128)(2,1)S(1)} %fusion.31.own_ref, bf16[256,1152]{1,0:T(8,128)(2,1)S(1)} %broadcast_select_fusion.1.next_ref), custom_call_target="tpu_custom_call" | custom-call | flops 2415919104 | bytes 11665408 | tf_op jit(solution)/shard_map/pallas_call | solution.py:129
  143.3 6.4 %fusion.18.mine_ref = bf16[256,2048]{1,0:T(8,128)(2,1)S(1)} fusion(f32[256,2048]{1,0:T(8,128)S(1)} %fusion, bf16[2,2048,2304]{2,1,0:T(8,128)(2,1)} %bitcast.44, bf16[256,1152]{1,0:T(8,128)(2,1)S(1)} %maximum_select_fusion.own_ref, bf16[256,1152]{1,0:T(8,128)(2,1)S(1)} %fusion.31.own_ref), kind=kOutput, calls=%fused_computation.17 | convolution fusion | flops 2419326976 | bytes 13762560 | tf_op jit(solution)/shard_map/dot_general | solution.py:24
  150.0 8.7 %shard_map.107 = bf16[2048,2,2304]{2,1,0:T(2,128)(2,1)} custom-call(bf16[256,2048]{1,0:T(8,128)(2,1)S(1)} %maximum_convert_fusion.features_ref, bf16[256,1152]{1,0:T(8,128)(2,1)S(1)} %maximum_select_fusion.own_ref, bf16[256,1152]{1,0:T(8,128)(2,1)S(1)} %broadcast_select_fusion.next_ref, ...), custom_call_target="tpu_custom_call", output_to_operand_aliasing={{}: (3, {})} | custom-call | flops 2415919104 | bytes 11665408 | tf_op jit(solution)/shard_map/pallas_call | solution.py:129
  158.7 5.8 %shard_map.106 = (bf16[2048,2304]{1,0:T(8,128)(2,1)}, f32[1,2048]{1,0:T(1,128)}) custom-call(bf16[256,2048]{1,0:T(8,128)(2,1)S(1)} %fusion.18.mine_ref, bf16[256,2048]{1,0:T(8,128)(2,1)S(1)} %collective-permute-done.33.other_ref, bf16[256,2048]{1,0:T(8,128)(2,1)S(1)} %compare_convert_fusion.live_ref, bf16[256,2304]{1,0:T(8,128)(2,1)S(1)} %convolution_convert_fusion.inputs_ref), custom_call_target="tpu_custom_call" | custom-call | flops 2415919104 | bytes 13762560 | tf_op jit(solution)/shard_map/pallas_call | solution.py:157
  (133 shorter events, 29.2 us)
Async XLA Ops:
  3.2 1.5 collective-permute-start
  4.8 20.6 %collective-permute-start.2 = (bf16[64,2304]{1,0:T(8,128)(2,1)S(1)}, bf16[64,2304]{1,0:T(8,128)(2,1)S(1)}, u32[]{:S(2)}, u32[]{:S(2)}) collective-permute-start(bf16[64,2304]{1,0:T(8,128)(2,1)S(1)} %pad_maximum_fusion.2), channel_id=1, source_target_pairs={{0,8},{4,12},{8,0},{12,4},{1,9},{5,13},{9,1},{13,5},{2,10},{6,14},... | collective-permute-start | bytes 884744 | tf_op jit(solution)/shard_map/ppermute | solution.py:20
  8.9 17.1 %collective-permute-start.1 = (bf16[64,2304]{1,0:T(8,128)(2,1)S(1)}, bf16[64,2304]{1,0:T(8,128)(2,1)S(1)}, u32[]{:S(2)}, u32[]{:S(2)}) collective-permute-start(bf16[64,2304]{1,0:T(8,128)(2,1)S(1)} %pad_maximum_fusion.2), channel_id=1, source_target_pairs={{0,4},{4,0},{8,12},{12,8},{1,5},{5,1},{9,13},{13,9},{2,6},{6,2},{1... | collective-permute-start | bytes 884744 | tf_op jit(solution)/shard_map/ppermute | solution.py:20
  10.7 1.6 collective-permute-start.5
  25.4 9.3 %collective-permute-start.3 = (bf16[64,2304]{1,0:T(8,128)(2,1)S(1)}, bf16[64,2304]{1,0:T(8,128)(2,1)S(1)}, u32[]{:S(2)}, u32[]{:S(2)}) collective-permute-start(bf16[64,2304]{1,0:T(8,128)(2,1)S(1)} %collective-permute-done.2), channel_id=1, source_target_pairs={{0,4},{4,0},{8,12},{12,8},{1,5},{5,1},{9,13},{13,9},{2,6},{6,2},{1... | collective-permute-start | bytes 884744 | tf_op jit(solution)/shard_map/ppermute | solution.py:20
  38.3 3.6 %collective-permute-start.6 = (f32[256,1024]{1,0:T(8,128)S(1)}, f32[256,1024]{1,0:T(8,128)S(1)}, u32[]{:S(2)}, u32[]{:S(2)}) collective-permute-start(f32[256,1024]{1,0:T(8,128)S(1)} %shard_map.102), channel_id=1, source_target_pairs={{0,1},{1,0},{2,3},{3,2},{4,5},{5,4},{6,7},{7,6},{8,9},{9,8},{10,11... | collective-permute-start | bytes 3145736 | tf_op jit(solution)/shard_map/ppermute | solution.py:16
  41.4 2.8 %collective-permute-start.7 = (f32[256,1024]{1,0:T(8,128)S(1)}, f32[256,1024]{1,0:T(8,128)S(1)}, u32[]{:S(2)}, u32[]{:S(2)}) collective-permute-start(f32[256,1024]{1,0:T(8,128)S(1)} %shard_map.103), channel_id=1, source_target_pairs={{0,1},{1,0},{2,3},{3,2},{4,5},{5,4},{6,7},{7,6},{8,9},{9,8},{10,11... | collective-permute-start | bytes 3145736 | tf_op jit(solution)/shard_map/ppermute | solution.py:16
  52.4 16.8 %collective-permute-start.9 = (bf16[256,1152]{1,0:T(8,128)(2,1)}, bf16[256,1152]{1,0:T(8,128)(2,1)}, u32[]{:S(2)}, u32[]{:S(2)}) collective-permute-start(bf16[256,1152]{1,0:T(8,128)(2,1)} %slice.180), channel_id=1, source_target_pairs={{0,2},{1,3},{4,6},{5,7},{8,10},{9,11},{12,14},{13,15},{16,18},{17,... | collective-permute-start | bytes 1769480 | tf_op jit(solution)/shard_map/ppermute | solution.py:285
  57.4 7.2 %collective-permute-start.8 = (bf16[64,1152]{1,0:T(8,128)(2,1)}, bf16[64,1152]{1,0:T(8,128)(2,1)}, u32[]{:S(2)}, u32[]{:S(2)}) collective-permute-start(bf16[64,1152]{1,0:T(8,128)(2,1)} %get-tuple-element.91), channel_id=1, source_target_pairs={{0,4},{4,0},{8,12},{12,8},{1,5},{5,1},{9,13},{13,9},{2,6},{6,2},{1... | collective-permute-start | bytes 442376 | tf_op jit(solution)/shard_map/ppermute | solution.py:20
  59.3 15.5 %collective-permute-start.14 = (bf16[64,1152]{1,0:T(8,128)(2,1)S(1)}, bf16[64,1152]{1,0:T(8,128)(2,1)S(1)}, u32[]{:S(2)}, u32[]{:S(2)}) collective-permute-start(bf16[64,1152]{1,0:T(8,128)(2,1)S(1)} %copy-done.5), channel_id=1, source_target_pairs={{0,8},{4,12},{8,0},{12,4},{1,9},{5,13},{9,1},{13,5},{2,10},{6,14},... | collective-permute-start | bytes 442376 | tf_op jit(solution)/shard_map/ppermute | solution.py:20
  59.7 15.1 %collective-permute-start.15 = (bf16[64,1152]{1,0:T(8,128)(2,1)S(1)}, bf16[64,1152]{1,0:T(8,128)(2,1)S(1)}, u32[]{:S(2)}, u32[]{:S(2)}) collective-permute-start(bf16[64,1152]{1,0:T(8,128)(2,1)S(1)} %get-tuple-element.90), channel_id=1, source_target_pairs={{0,12},{4,8},{8,4},{12,0},{1,13},{5,9},{9,5},{13,1},{2,14},{6,10},... | collective-permute-start | bytes 442376 | tf_op jit(solution)/shard_map/ppermute | solution.py:20
  71.3 7.7 %collective-permute-start.10 = (bf16[64,1152]{1,0:T(8,128)(2,1)S(1)}, bf16[64,1152]{1,0:T(8,128)(2,1)S(1)}, u32[]{:S(2)}, u32[]{:S(2)}) collective-permute-start(bf16[64,1152]{1,0:T(8,128)(2,1)S(1)} %get-tuple-element.92), channel_id=1, source_target_pairs={{0,4},{4,0},{8,12},{12,8},{1,5},{5,1},{9,13},{13,9},{2,6},{6,2},{1... | collective-permute-start | bytes 442376 | tf_op jit(solution)/shard_map/ppermute | solution.py:20
  71.8 8.8 %collective-permute-start.12 = (bf16[64,1152]{1,0:T(8,128)(2,1)S(1)}, bf16[64,1152]{1,0:T(8,128)(2,1)S(1)}, u32[]{:S(2)}, u32[]{:S(2)}) collective-permute-start(bf16[64,1152]{1,0:T(8,128)(2,1)S(1)} %get-tuple-element.93), channel_id=1, source_target_pairs={{0,12},{4,8},{8,4},{12,0},{1,13},{5,9},{9,5},{13,1},{2,14},{6,10},... | collective-permute-start | bytes 442376 | tf_op jit(solution)/shard_map/ppermute | solution.py:20
  73.1 14.9 %collective-permute-start.11 = (bf16[64,1152]{1,0:T(8,128)(2,1)S(1)}, bf16[64,1152]{1,0:T(8,128)(2,1)S(1)}, u32[]{:S(2)}, u32[]{:S(2)}) collective-permute-start(bf16[64,1152]{1,0:T(8,128)(2,1)S(1)} %get-tuple-element.94), channel_id=1, source_target_pairs={{0,8},{4,12},{8,0},{12,4},{1,9},{5,13},{9,1},{13,5},{2,10},{6,14},... | collective-permute-start | bytes 442376 | tf_op jit(solution)/shard_map/ppermute | solution.py:20
  75.9 19.1 %collective-permute-start.16 = (f32[64,1152]{1,0:T(8,128)S(1)}, f32[64,1152]{1,0:T(8,128)S(1)}, u32[]{:S(2)}, u32[]{:S(2)}) collective-permute-start(f32[64,1152]{1,0:T(8,128)S(1)} %fusion.36), channel_id=1, source_target_pairs={{0,2},{2,0},{1,3},{3,1},{4,6},{6,4},{5,7},{7,5},{8,10},{10,8},{9,1... | collective-permute-start | bytes 884744 | tf_op jit(solution)/shard_map/ppermute | solution.py:16
  88.2 14.7 %collective-permute-start.23 = (bf16[64,1152]{1,0:T(8,128)(2,1)S(1)}, bf16[64,1152]{1,0:T(8,128)(2,1)S(1)}, u32[]{:S(2)}, u32[]{:S(2)}) collective-permute-start(bf16[64,1152]{1,0:T(8,128)(2,1)S(1)} %get-tuple-element.85), channel_id=1, source_target_pairs={{0,12},{4,8},{8,4},{12,0},{1,13},{5,9},{9,5},{13,1},{2,14},{6,10},... | collective-permute-start | bytes 442376 | tf_op jit(solution)/shard_map/ppermute | solution.py:20
  89.6 11.1 %collective-permute-start.13 = (bf16[64,1152]{1,0:T(8,128)(2,1)S(1)}, bf16[64,1152]{1,0:T(8,128)(2,1)S(1)}, u32[]{:S(2)}, u32[]{:S(2)}) collective-permute-start(bf16[64,1152]{1,0:T(8,128)(2,1)S(1)} %get-tuple-element.86), channel_id=1, source_target_pairs={{0,4},{4,0},{8,12},{12,8},{1,5},{5,1},{9,13},{13,9},{2,6},{6,2},{1... | collective-permute-start | bytes 442376 | tf_op jit(solution)/shard_map/ppermute | solution.py:20
  89.6 13.3 %collective-permute-start.22 = (bf16[64,1152]{1,0:T(8,128)(2,1)S(1)}, bf16[64,1152]{1,0:T(8,128)(2,1)S(1)}, u32[]{:S(2)}, u32[]{:S(2)}) collective-permute-start(bf16[64,1152]{1,0:T(8,128)(2,1)S(1)} %get-tuple-element.73), channel_id=1, source_target_pairs={{0,8},{4,12},{8,0},{12,4},{1,9},{5,13},{9,1},{13,5},{2,10},{6,14},... | collective-permute-start | bytes 442376 | tf_op jit(solution)/shard_map/ppermute | solution.py:20
  92.7 15.0 %collective-permute-start.18 = (bf16[64,1152]{1,0:T(8,128)(2,1)S(1)}, bf16[64,1152]{1,0:T(8,128)(2,1)S(1)}, u32[]{:S(2)}, u32[]{:S(2)}) collective-permute-start(bf16[64,1152]{1,0:T(8,128)(2,1)S(1)} %fusion.48), channel_id=1, source_target_pairs={{0,2},{2,0},{1,3},{3,1},{4,6},{6,4},{5,7},{7,5},{8,10},{10,8},{9,1... | collective-permute-start | bytes 442376 | tf_op jit(solution)/shard_map/ppermute | solution.py:16
  100.7 14.4 %collective-permute-start.20 = (bf16[64,1152]{1,0:T(8,128)(2,1)S(1)}, bf16[64,1152]{1,0:T(8,128)(2,1)S(1)}, u32[]{:S(2)}, u32[]{:S(2)}) collective-permute-start(bf16[64,1152]{1,0:T(8,128)(2,1)S(1)} %get-tuple-element.49), channel_id=1, source_target_pairs={{0,8},{4,12},{8,0},{12,4},{1,9},{5,13},{9,1},{13,5},{2,10},{6,14},... | collective-permute-start | bytes 442376 | tf_op jit(solution)/shard_map/ppermute | solution.py:20
  100.7 8.6 %collective-permute-start.17 = (bf16[64,1152]{1,0:T(8,128)(2,1)S(1)}, bf16[64,1152]{1,0:T(8,128)(2,1)S(1)}, u32[]{:S(2)}, u32[]{:S(2)}) collective-permute-start(bf16[64,1152]{1,0:T(8,128)(2,1)S(1)} %get-tuple-element.49), channel_id=1, source_target_pairs={{0,4},{4,0},{8,12},{12,8},{1,5},{5,1},{9,13},{13,9},{2,6},{6,2},{1... | collective-permute-start | bytes 442376 | tf_op jit(solution)/shard_map/ppermute | solution.py:20
  104.0 11.0 %collective-permute-start.25 = (bf16[64,1152]{1,0:T(8,128)(2,1)S(1)}, bf16[64,1152]{1,0:T(8,128)(2,1)S(1)}, u32[]{:S(2)}, u32[]{:S(2)}) collective-permute-start(bf16[64,1152]{1,0:T(8,128)(2,1)S(1)} %get-tuple-element.84), channel_id=1, source_target_pairs={{0,2},{1,3},{4,6},{5,7},{8,10},{9,11},{12,14},{13,15},{16,18},{17,... | collective-permute-start | bytes 442376 | tf_op jit(solution)/shard_map/ppermute | solution.py:309
  106.4 15.5 %collective-permute-start.24 = (bf16[256,1152]{1,0:T(8,128)(2,1)S(1)}, bf16[256,1152]{1,0:T(8,128)(2,1)S(1)}, u32[]{:S(2)}, u32[]{:S(2)}) collective-permute-start(bf16[256,1152]{1,0:T(8,128)(2,1)S(1)} %fusion.28), channel_id=1, source_target_pairs={{2,0},{3,1},{6,4},{7,5},{10,8},{11,9},{14,12},{15,13},{18,16},{19,... | collective-permute-start | bytes 1769480 | tf_op jit(solution)/shard_map/ppermute | solution.py:302
  109.3 6.1 %collective-permute-start.28 = (bf16[64,1152]{1,0:T(8,128)(2,1)S(1)}, bf16[64,1152]{1,0:T(8,128)(2,1)S(1)}, u32[]{:S(2)}, u32[]{:S(2)}) collective-permute-start(bf16[64,1152]{1,0:T(8,128)(2,1)S(1)} %get-tuple-element.50), channel_id=1, source_target_pairs={{0,8},{4,12},{8,0},{12,4},{1,9},{5,13},{9,1},{13,5},{2,10},{6,14},... | collective-permute-start | bytes 442376 | tf_op jit(solution)/shard_map/ppermute | solution.py:20
  110.0 17.1 %collective-permute-start.19 = (bf16[64,1152]{1,0:T(8,128)(2,1)S(1)}, bf16[64,1152]{1,0:T(8,128)(2,1)S(1)}, u32[]{:S(2)}, u32[]{:S(2)}) collective-permute-start(bf16[64,1152]{1,0:T(8,128)(2,1)S(1)} %get-tuple-element.50), channel_id=1, source_target_pairs={{0,4},{4,0},{8,12},{12,8},{1,5},{5,1},{9,13},{13,9},{2,6},{6,2},{1... | collective-permute-start | bytes 442376 | tf_op jit(solution)/shard_map/ppermute | solution.py:20
  115.1 6.0 %collective-permute-start.21 = (bf16[64,1152]{1,0:T(8,128)(2,1)S(1)}, bf16[64,1152]{1,0:T(8,128)(2,1)S(1)}, u32[]{:S(2)}, u32[]{:S(2)}) collective-permute-start(bf16[64,1152]{1,0:T(8,128)(2,1)S(1)} %collective-permute-done.20), channel_id=1, source_target_pairs={{0,4},{4,0},{8,12},{12,8},{1,5},{5,1},{9,13},{13,9},{2,6},{6,2},{1... | collective-permute-start | bytes 442376 | tf_op jit(solution)/shard_map/ppermute | solution.py:20
  115.5 16.3 %collective-permute-start.29 = (bf16[64,1152]{1,0:T(8,128)(2,1)S(1)}, bf16[64,1152]{1,0:T(8,128)(2,1)S(1)}, u32[]{:S(2)}, u32[]{:S(2)}) collective-permute-start(bf16[64,1152]{1,0:T(8,128)(2,1)S(1)} %collective-permute-done.28), channel_id=1, source_target_pairs={{0,4},{4,0},{8,12},{12,8},{1,5},{5,1},{9,13},{13,9},{2,6},{6,2},{1... | collective-permute-start | bytes 442376 | tf_op jit(solution)/shard_map/ppermute | solution.py:20
  127.2 16.0 %collective-permute-start.32 = (bf16[64,1152]{1,0:T(8,128)(2,1)S(1)}, bf16[64,1152]{1,0:T(8,128)(2,1)S(1)}, u32[]{:S(2)}, u32[]{:S(2)}) collective-permute-start(bf16[64,1152]{1,0:T(8,128)(2,1)S(1)} %get-tuple-element.59), channel_id=1, source_target_pairs={{0,12},{4,8},{8,4},{12,0},{1,13},{5,9},{9,5},{13,1},{2,14},{6,10},... | collective-permute-start | bytes 442376 | tf_op jit(solution)/shard_map/ppermute | solution.py:20
  130.1 13.0 %collective-permute-start.31 = (bf16[64,1152]{1,0:T(8,128)(2,1)S(1)}, bf16[64,1152]{1,0:T(8,128)(2,1)S(1)}, u32[]{:S(2)}, u32[]{:S(2)}) collective-permute-start(bf16[64,1152]{1,0:T(8,128)(2,1)S(1)} %get-tuple-element.59), channel_id=1, source_target_pairs={{0,8},{4,12},{8,0},{12,4},{1,9},{5,13},{9,1},{13,5},{2,10},{6,14},... | collective-permute-start | bytes 442376 | tf_op jit(solution)/shard_map/ppermute | solution.py:20
  130.1 13.0 %collective-permute-start.30 = (bf16[64,1152]{1,0:T(8,128)(2,1)S(1)}, bf16[64,1152]{1,0:T(8,128)(2,1)S(1)}, u32[]{:S(2)}, u32[]{:S(2)}) collective-permute-start(bf16[64,1152]{1,0:T(8,128)(2,1)S(1)} %get-tuple-element.59), channel_id=1, source_target_pairs={{0,4},{4,0},{8,12},{12,8},{1,5},{5,1},{9,13},{13,9},{2,6},{6,2},{1... | collective-permute-start | bytes 442376 | tf_op jit(solution)/shard_map/ppermute | solution.py:20
  131.7 1.6 collective-permute-start.26
  149.7 9.0 %collective-permute-start.33 = (bf16[256,2048]{1,0:T(8,128)(2,1)S(1)}, bf16[256,2048]{1,0:T(8,128)(2,1)S(1)}, u32[]{:S(2)}, u32[]{:S(2)}) collective-permute-start(bf16[256,2048]{1,0:T(8,128)(2,1)S(1)} %fusion.18.mine_ref), channel_id=1, source_target_pairs={{0,1},{1,0},{2,3},{3,2},{4,5},{5,4},{6,7},{7,6},{8,9},{9,8},{10,11... | collective-permute-start | bytes 3145736 | tf_op jit(solution)/shard_map/ppermute | solution.py:16
  (14 other events, 146.5 us)
